TPU v7x, 32 devices: a whole 2x2x4 slice. The times are simulated.
32 devices in a mesh: seq: 4 (over x, core), head: 8 (over z, y).
Axes of the slice: x: 2, y: 2, z: 4, core: 2. Of those that a mesh axis runs over, the one named last changes fastest.
Arguments:
- x_inner: bfloat16 [6144, 16384], P('seq', 'head'), may hold values from -400 to 400
- z_gate: bfloat16 [6144, 16384], P('seq', 'head'), may hold values from -6 to 6
- bc_raw: bfloat16 [6144, 512], P(('seq', 'head')), may hold values from -6 to 6
- conv_weight: float32 [4, 512], replicated, may hold values from -3 to 3
- conv_bias: float32 [512], replicated, may hold values from -3 to 3
- dt_raw: float32 [6144, 128], P('seq', 'head'), may hold values from -6 to 6144
- a_log: float32 [128], P('head'), may hold values from -20 to 1
- d_skip: float32 [128], P('head'), may hold values from 0.5 to 1.5
- norm_gain: float32 [16384], P('head'), may hold values from 0.5 to 1.5
Outputs:
- mixer_out: bfloat16 [6144, 16384], P('seq', 'head')
All inputs are finite; a program needn't handle non-finite values.
Results may differ from a plain program's by a relative error of at most 0.0034.
Values may be sent and summed in bfloat16 or wider, within the bound.
No kernel may reach another device: no remote copies, remote signals or barrier semaphores. Data moves between devices by JAX's collectives and lax.ppermute only.
A program may use at most 128 MiB of HBM per device.

v0:
```python
import jax
import jax.numpy as jnp
from jax import lax
from jax.sharding import PartitionSpec as P

HEAD_DIM = 128
STATE = 256
BLOCK = 256
INNER = 16384


def shifted(shard, axis, by):
    length = lax.axis_size(axis)
    pairs = [(i, i + by) for i in range(length) if 0 <= i + by < length]
    return lax.ppermute(shard, axis, pairs)


def prefix(part, axis, combine, identity):
    place = lax.axis_index(axis)
    gathered = jax.tree.map(lambda a: lax.all_gather(a, axis), part)
    state = jax.tree.map(lambda a, e: jnp.zeros_like(a) + jnp.asarray(e, a.dtype), part, identity)

    def one(hop, state):
        return combine(
            state, jax.tree.map(lambda a: lax.dynamic_index_in_dim(a, hop, 0, False), gathered)
        )

    return lax.fori_loop(0, place, one, state)


def convolve_rows(padded, conv_weight, conv_bias):
    tap_count = conv_weight.shape[0]
    row_count = padded.shape[0] - tap_count + 1
    padded_float = padded.astype(jnp.float32)
    accumulated = jnp.broadcast_to(conv_bias[None, :], (row_count, padded.shape[1]))
    for offset in range(tap_count):
        accumulated = (
            accumulated + conv_weight[offset][None, :] * padded_float[offset : offset + row_count]
        )
    return jax.nn.silu(accumulated).astype(jnp.bfloat16)


def on_device(x_inner, z_gate, bc_raw, conv_weight, conv_bias, dt_raw, a_log, d_skip, norm_gain):
    highest = lax.Precision.HIGHEST
    rim_count = conv_weight.shape[0] - 1
    rim_rows = shifted(bc_raw[-rim_count:], ("seq", "head"), 1)
    own_act = convolve_rows(jnp.concatenate([rim_rows, bc_raw], axis=0), conv_weight, conv_bias)
    bc_act = lax.all_gather(own_act, "head", axis=0, tiled=True)
    length = x_inner.shape[0]
    head_count = a_log.shape[0]
    block_count = length // BLOCK
    step_size = jax.nn.softplus(dt_raw)
    log_step = -jnp.exp(a_log)[None, :] * step_size
    cum_log = jnp.cumsum(log_step.reshape(block_count, BLOCK, head_count), axis=1)
    size_blocks = step_size.reshape(block_count, BLOCK, head_count)
    b_blocks = bc_act[:, :STATE].reshape(block_count, BLOCK, STATE)
    c_blocks = bc_act[:, STATE:].reshape(block_count, BLOCK, STATE)
    x_float = x_inner.astype(jnp.float32).reshape(block_count, BLOCK, head_count, HEAD_DIM)
    gram_blocks = jnp.einsum("cin,cjn->cij", c_blocks, b_blocks, preferred_element_type=jnp.float32)
    lower_mask = jnp.tril(jnp.ones((BLOCK, BLOCK), dtype=bool))
    by_head = jnp.transpose(cum_log, (0, 2, 1))
    spread = by_head[:, :, :, None] - by_head[:, :, None, :]
    decay_blocks = jnp.where(lower_mask, jnp.exp(jnp.where(lower_mask, spread, 0.0)), 0.0)
    weights = (
        gram_blocks[:, None] * decay_blocks * jnp.transpose(size_blocks, (0, 2, 1))[:, :, None, :]
    )
    inner_part = jnp.einsum("chij,cjhp->cihp", weights, x_float, precision=highest)
    tail_weight = jnp.exp(cum_log[:, -1:, :] - cum_log) * size_blocks
    block_states = jnp.einsum(
        "cjhp,cjn->chpn",
        x_float * tail_weight[..., None],
        b_blocks.astype(jnp.float32),
        precision=highest,
    )
    block_decay = jnp.exp(cum_log[:, -1, :])
    zero_state = jnp.zeros((head_count, HEAD_DIM, STATE), jnp.float32)
    starts = []
    current = zero_state
    for block_index in range(block_count):
        starts.append(current)
        current = block_decay[block_index][:, None, None] * current + block_states[block_index]
    zero_starts = jnp.stack(starts)
    log_total = jnp.sum(cum_log[:, -1, :], axis=0)

    def combine(earlier, later):
        return (earlier[0] + later[0], jnp.exp(later[0])[:, None, None] * earlier[1] + later[1])

    identity = (jnp.zeros_like(log_total), zero_state)
    chained = prefix((log_total, current), "seq", combine, identity)
    incoming = chained[1]
    c_float = c_blocks.astype(jnp.float32)
    carried_part = jnp.exp(cum_log)[..., None] * jnp.einsum(
        "cin,chpn->cihp", c_float, zero_starts, precision=highest
    )
    prior_log = jnp.cumsum(cum_log[:, -1, :], axis=0) - cum_log[:, -1, :]
    entry_part = jnp.exp(cum_log + prior_log[:, None, :])[..., None] * jnp.einsum(
        "cin,hpn->cihp", c_float, incoming, precision=highest
    )
    carried_part = carried_part + entry_part
    ssm_out = inner_part + carried_part + d_skip[None, None, :, None] * x_float
    gated_out = ssm_out.reshape(length, head_count * HEAD_DIM) * jax.nn.silu(
        z_gate.astype(jnp.float32)
    )
    square_sum = lax.psum(jnp.sum(gated_out * gated_out, axis=1), "head")
    inverse_rms = lax.rsqrt(square_sum / INNER + 1e-05)
    return (gated_out * inverse_rms[:, None] * norm_gain[None, :]).astype(jnp.bfloat16)


def solution(mesh):
    placed = (
        P("seq", "head"),
        P("seq", "head"),
        P(("seq", "head"), None),
        P(),
        P(),
        P("seq", "head"),
        P("head"),
        P("head"),
        P("head"),
    )
    return jax.shard_map(
        on_device, mesh=mesh, in_specs=placed, out_specs=P("seq", "head"), check_vma=False
    )
```

profile of v0, /device:TPU:0, one launch (start us, length us, event | category | flops | bytes accessed | tf_op | source)
XLA Modules:
  0.0 240.7 jit_solution(1866487842041978660)
XLA Ops:
  6.5 0.7 slice.83
  7.2 4.9 %collective-permute-start = (bf16[3,512]{1,0:T(4,128)(2,1)S(1)}, bf16[3,512]{1,0:T(4,128)(2,1)S(1)}, u32[]{:S(2)}, u32[]{:S(2)}) collective-permute-start(bf16[3,512]{1,0:T(4,128)(2,1)S(1)} %slice.83), channel_id=1, source_target_pairs={{0,1},{1,2},{2,3},{3,4},{4,5},{5,6},{6,7},{7,8},{8,9},{9,10},{10,1... | collective-permute-start | bytes 9224 | tf_op jit(solution)/shard_map/ppermute | solution.py:15
  12.1 0.9 fusion.35
  13.4 1.0 maximum_convert_fusion
  14.4 1.6 multiply_convert_fusion.1
  16.8 1.0 broadcast_multiply_fusion
  17.9 3.4 %reduce-window.6 = f32[6,16,2,128]{3,1,2,0:T(8,128)S(1)} reduce-window(f32[6,16,2,128]{3,1,2,0:T(8,128)S(1)} %copy.36, f32[]{:T(128)} %constant.43.clone.1), window={size=1x1x1x128 pad=0_0x0_0x0_0x127_0}, to_apply=%region_0.1 | reduce-window | flops 3121152 | bytes 196612 | tf_op jit(solution)/shard_map/reduce-window
  21.5 7.8 %copy.51 = bf16[192,8,16,128]{3,2,1,0:T(8,128)(2,1)} copy(bf16[192,8,16,128]{3,1,2,0:T(8,128)(2,1)} %bitcast.103) | data formatting | bytes 12582912
  29.7 1.5 broadcast_dynamic-update-slice_fusion
  31.6 30.9 %all-gather.4.cloned.1.call-done = bf16[1536,512]{1,0:T(8,128)(2,1)} async-done(((bf16[192,512]{1,0:T(8,128)(2,1)}), bf16[1536,512]{1,0:T(8,128)(2,1)}) %all-gather.4.cloned.1.call-update) | async-done | bytes 1572880 | tf_op jit(solution)/shard_map/all_gather | solution.py:48
  62.4 1.6 fusion.34
  64.0 16.1 %fusion.7 = f32[6,16,128,256]{3,2,1,0:T(8,128)S(1)} fusion(bf16[6,256,256,1]{2,1,3,0:T(8,128)(2,1)S(1)} %bitcast.101, f32[6,256,16]{1,2,0:T(8,128)S(1)} %get-tuple-element.72, bf16[6,256,16,128]{3,2,1,0:T(8,128)(2,1)} %bitcast.91), kind=kOutput, calls=%fused_computation.13 | convolution fusion | flops 9669967872 | bytes 19759104 | tf_op jit(solution)/shard_map/cjhp,cjn->chpn/dot_general | solution.py:69
  81.6 0.9 constant_dynamic-update-slice_fusion
  82.5 2.1 fusion.30
  84.5 4.6 %copy-done = f32[6,16,128,256]{3,2,1,0:T(8,128)} copy-done((f32[6,16,128,256]{3,2,1,0:T(8,128)}, f32[6,16,128,256]{3,2,1,0:T(8,128)S(1)}, u32[]{:S(2)}) %copy-start) | copy-done | bytes 12582936
  90.8 6.1 %all-reduce = f32[64]{0:T(128)S(1)} all-reduce(f32[64]{0:T(128)S(1)} %dynamic-update-slice), channel_id=2, replica_groups=mesh['seq'=4,'head'=8] {'seq'}, use_global_device_ids=true, to_apply=%add | all-reduce | flops 64 | bytes 512
  97.4 21.9 %fusion = f32[6,16,256,128]{3,2,1,0:T(8,128)} fusion(f32[6,16,256]{2,1,0:T(8,128)S(1)} %copy.38, f32[6,16,256]{2,1,0:T(8,128)S(1)} %get-tuple-element.74, f32[6,256,256]{2,1,0:T(8,128)S(1)} %fusion.37, pred[256,256]{1,0:T(8,128)(4,1)S(1)} %iota_compare_fusion, bf16[6,256,16,128]{3,2,1,0:T(8,128)(2,1)} %bitcast.92), kind=kOutput, calls=%fused_computation.2 | convolution fusion | flops 9695133696 | bytes 20709376 | tf_op jit(solution)/shard_map/chij,cjhp->cihp/dot_general | solution.py:67
  119.3 27.1 %all-gather.6.cloned.1.call-done = f32[4,16,128,256]{3,2,1,0:T(8,128)} async-done(((f32[1,16,128,256]{3,2,1,0:T(8,128)}), f32[4,16,128,256]{3,2,1,0:T(8,128)}) %all-gather.6.cloned.1.call-update) | async-done | bytes 8388624 | tf_op jit(solution)/shard_map/all_gather | solution.py:20
  146.6 5.5 %fusion.22 = f32[6,256,16,128]{3,1,2,0:T(8,128)S(1)} fusion(bf16[6,256,256,1]{2,1,3,0:T(8,128)(2,1)S(1)} %bitcast.97, f32[16,128,256]{2,1,0:T(8,128)S(1)} %get-tuple-element.49), kind=kOutput, calls=%fused_computation.37 | convolution fusion | flops 9663676416 | bytes 15466496 | tf_op jit(solution)/shard_map/cin,hpn->cihp/dot_general | solution.py:96
  152.2 20.2 %fusion.8 = f32[6,256,16,128]{3,1,2,0:T(8,128)} fusion(f32[6,16,256,128]{3,2,1,0:T(8,128)} %fusion, f32[6,256,16,128]{3,1,2,0:T(8,128)S(1)} %fusion.22, f32[16]{0:T(128)S(1)} %copy-done.1, f32[6,256,16]{1,2,0:T(8,128)S(1)} %get-tuple-element.71, f32[6,256,16]{1,2,0:T(8,128)S(1)} %get-tuple-element.70, bf16[6,256,16,128]{3,2,1,0:T(8,128)(2,1)S(1)} %bitcast.95, ...), kind=kOutput, calls=%fused_computation.14 | convolution fusion | flops 9685696512 | bytes 57606208 | tf_op jit(solution)/shard_map/cin,chpn->cihp/dot_general | solution.py:92
  172.4 16.3 %copy.43 = f32[6,256,16,128]{3,2,1,0:T(8,128)} copy(f32[6,256,16,128]{3,1,2,0:T(8,128)} %fusion.8) | data formatting | bytes 25165824 | tf_op jit(solution)/shard_map/add | solution.py:100
  188.6 10.1 %multiply_reduce_fusion = f32[1536]{0:T(1024)S(1)} fusion(bf16[1536,2048]{1,0:T(8,128)(2,1)} %param.12, f32[192,8,16,128]{3,2,1,0:T(8,128)} %bitcast.89), kind=kLoop, calls=%fused_computation.21 | loop fusion | flops 25164288 | bytes 18880512 | tf_op jit(solution)/shard_map/reduce_sum | solution.py:104
  198.8 21.6 %psum.7 = f32[1536]{0:T(1024)S(1)} all-reduce(f32[1536]{0:T(1024)S(1)} %multiply_reduce_fusion), channel_id=1, replica_groups=mesh['seq'=4,'head'=8] {'head'}, use_global_device_ids=true, to_apply=%region_7.8 | all-reduce | flops 1536 | bytes 12288 | tf_op jit(solution)/shard_map/psum | solution.py:104
  220.4 13.4 %multiply_convert_fusion = bf16[1536,2048]{1,0:T(8,128)(2,1)} fusion(f32[2048]{0:T(1024)S(1)} %copy-done.2, f32[1536]{0:T(1024)S(1)} %add_rsqrt_fusion, bf16[1536,2048]{1,0:T(8,128)(2,1)} %param.12, f32[192,8,16,128]{3,2,1,0:T(8,128)} %bitcast.90), kind=kLoop, calls=%fused_computation.20 | loop fusion | flops 28311552 | bytes 25180160 | tf_op jit(solution)/shard_map/convert_element_type | solution.py:106
  (51 shorter events, 5.2 us)
Async XLA Ops:
  6.5 55.9 %all-gather.4.cloned.1.call-start = ((), (), s32[]{:S(2)}) async-start(), calls=%async_computation | async-start | bytes 1769472 | tf_op jit(solution)/shard_map/all_gather | solution.py:48
  7.2 6.2 %collective-permute-start = (bf16[3,512]{1,0:T(4,128)(2,1)S(1)}, bf16[3,512]{1,0:T(4,128)(2,1)S(1)}, u32[]{:S(2)}, u32[]{:S(2)}) collective-permute-start(bf16[3,512]{1,0:T(4,128)(2,1)S(1)} %slice.83), channel_id=1, source_target_pairs={{0,1},{1,2},{2,3},{3,4},{4,5},{5,6},{6,7},{7,8},{8,9},{9,10},{10,1... | collective-permute-start | bytes 9224 | tf_op jit(solution)/shard_map/ppermute | solution.py:15
  16.1 130.3 %all-gather.6.cloned.1.call-start = ((), (), s32[]{:S(2)}) async-start(), calls=%async_computation.1 | async-start | bytes 10485760 | tf_op jit(solution)/shard_map/all_gather | solution.py:20
  62.4 17.7 %slice-start.2 = ((s8[12582912]{0:T(1024)(128)(4,1)}), s8[4194304]{0:T(1024)(128)(4,1)S(1)}, s32[]{:S(2)}) async-start(s8[12582912]{0:T(1024)(128)(4,1)} %bitcast.99), calls=%async_computation.4 | async-start | bytes 8388608
  64.0 16.1 %slice-start.3 = ((s8[12582912]{0:T(1024)(128)(4,1)}), s8[4194304]{0:T(1024)(128)(4,1)S(1)}, s32[]{:S(2)}) async-start(s8[12582912]{0:T(1024)(128)(4,1)} %bitcast.99), calls=%async_computation.5 | async-start | bytes 8388608
  64.0 16.1 %slice-start.4 = ((s8[12582912]{0:T(1024)(128)(4,1)}), s8[4194304]{0:T(1024)(128)(4,1)S(1)}, s32[]{:S(2)}) async-start(s8[12582912]{0:T(1024)(128)(4,1)} %bitcast.99), calls=%async_computation.6 | async-start | bytes 8388608
  81.5 7.6 %copy-start.3 = (u32[32]{0:T(128)S(1)}, u32[32]{0:T(128)}, u32[]{:S(2)}) copy-start(u32[32]{0:T(128)} %constant.50) | copy-start | bytes 388
  84.5 4.6 %copy-start = (f32[6,16,128,256]{3,2,1,0:T(8,128)}, f32[6,16,128,256]{3,2,1,0:T(8,128)S(1)}, u32[]{:S(2)}) copy-start(f32[6,16,128,256]{3,2,1,0:T(8,128)S(1)} %get-tuple-element.66) | copy-start | bytes 37748740
  146.6 5.6 %slice-start = ((s8[6291456]{0:T(1024)(128)(4,1)}), s8[4194304]{0:T(1024)(128)(4,1)S(1)}, s32[]{:S(2)}) async-start(s8[6291456]{0:T(1024)(128)(4,1)} %bitcast.93), calls=%async_computation.2 | async-start | bytes 8388608
  146.6 5.6 %copy-start.1 = (f32[16]{0:T(128)S(1)}, f32[16]{0:T(128)}, u32[]{:S(2)}) copy-start(f32[16]{0:T(128)} %param.18) | copy-start | bytes 196
  146.6 5.6 %slice-start.1 = ((s8[6291456]{0:T(1024)(128)(4,1)}), s8[2097152]{0:T(1024)(128)(4,1)S(1)}, s32[]{:S(2)}) async-start(s8[6291456]{0:T(1024)(128)(4,1)} %bitcast.93), calls=%async_computation.3 | async-start | bytes 4194304
  188.6 31.8 %copy-start.2 = (f32[2048]{0:T(1024)S(1)}, f32[2048]{0:T(1024)}, u32[]{:S(2)}) copy-start(f32[2048]{0:T(1024)} %param.19) | copy-start | bytes 24580
Sparse Core Ops, SparseCore 0:
  16.2 46.1 all-gather.3
  89.2 57.0 all-gather.5
where the time goes:
time: 243 us; the launch traced here: 241 us
  matrix products  64 us (26%)
  waiting for transfers between devices  58.4 us (24%)
  other arithmetic  36.2 us (15%)
  local copies, waits for them, and re-layouts  35 us (14%)
  blocking collectives  27.7 us (11%)
  between operations  14.4 us (6%)
  starting transfers between devices  4.9 us (2%)
    all_gather x1, waiting for transfers between devices, on_device(): bc_act = lax.all_gather(own_act, 'head', axis=0, tiled=True)  30.9 us
    all_gather x1, waiting for transfers between devices, prefix(): gathered = jax.tree.map(lambda a: lax.all_gather(a, axis), part)  27.1 us
    dot_general x1, matrix products, on_device(): jnp.einsum('chij,cjhp->cihp', weights, x_float, precision=highest)  21.9 us
    psum x1, blocking collectives, on_device(): square_sum = lax.psum(jnp.sum(gated_out * gated_out, axis=1), 'head')  21.6 us
    dot_general x1, matrix products, on_device(): jnp.einsum('cin,chpn->cihp', c_float, zero_starts, precision=highest)  20.2 us
    add x1, local copies, waits for them, and re-layouts, on_device(): ssm_out = inner_part + carried_part + d_skip[None, None, :, None] * x_float  16.3 us
    dot_general x1, matrix products, on_device(): jnp.einsum('cjhp,cjn->chpn', x_float * tail_weight[..., None], b_blocks.a...  16.1 us
    unnamed x23, local copies, waits for them, and re-layouts  14.9 us
  transfers between devices with their start and end apart: 3, of which 3 were waited for; matrix products, arithmetic and copies ran while one was open for 16% of the time, Pallas kernels for 0%

commit v1 on v0

v1 whole, which is shorter than its diff:
```python
import functools
import math

import jax
import jax.numpy as jnp
from jax import lax
from jax.experimental import pallas as pl
from jax.experimental.pallas import tpu as pltpu
from jax.sharding import PartitionSpec as P

HEAD_DIM = 128
STATE = 256
BLOCK = 256
INNER = 16384
RIM = 16
SLOT = 16
LOG2E = math.log2(math.e)
F32 = jnp.float32
BF16 = jnp.bfloat16
HIGHEST = lax.Precision.HIGHEST
VMEM_LIMIT = 48 * 1024 * 1024


def params():
    return pltpu.CompilerParams(vmem_limit_bytes=VMEM_LIMIT)


def whole(memory_space=pltpu.VMEM):
    return pl.BlockSpec(memory_space=memory_space)


def cost(flops, nbytes, trans=0):
    return pl.CostEstimate(flops=int(flops), bytes_accessed=int(nbytes), transcendentals=int(trans))


def silu(v):
    half = 0.5 * v
    return half + half * jnp.tanh(half)


def split(v):
    high = v.astype(BF16).astype(F32)
    return high, v - high


def conv_slab(slab, weight, bias):
    taps = weight.shape[0]
    total = jnp.broadcast_to(bias, slab.shape)
    for k in range(taps):
        shift = taps - 1 - k
        moved = pltpu.roll(slab, shift, 0) if shift else slab
        total = total + weight[k : k + 1, :] * moved
    total = total[RIM:]
    return (total * jax.nn.sigmoid(total)).astype(BF16)


def rates_kernel(dt_ref, a_ref, q_ref, b_ref, ends_ref):
    block_count = dt_ref.shape[1] // BLOCK
    rate = -jnp.exp(a_ref[...])
    upper = (
        lax.broadcasted_iota(jnp.int32, (BLOCK, BLOCK), 0)
        <= lax.broadcasted_iota(jnp.int32, (BLOCK, BLOCK), 1)
    ).astype(F32)
    prior = jnp.zeros((SLOT, 1), F32)
    lane = lax.broadcasted_iota(jnp.int32, (SLOT, 128), 1)
    ends = jnp.zeros((SLOT, 128), F32)
    for c in range(block_count):
        columns = slice(c * BLOCK, (c + 1) * BLOCK)
        dt = dt_ref[:, columns]
        step = jnp.maximum(dt, 0.0) + jnp.log1p(jnp.exp(-jnp.abs(dt)))
        cum = jnp.dot(rate * step, upper, precision=HIGHEST, preferred_element_type=F32)
        last = cum[:, BLOCK - 1 : BLOCK]
        scaled = cum * LOG2E
        b_ref[:, columns] = scaled - jnp.log(step) * LOG2E
        parts = [scaled]
        parts.extend(split(jnp.exp(last - cum) * step))
        parts.extend(split(jnp.exp(cum)))
        parts.extend(split(jnp.exp(cum + prior)))
        parts.append(jnp.zeros_like(cum))
        q_ref[columns, :] = jnp.concatenate(parts, axis=0).T
        ends = jnp.where(lane == c, last, ends)
        prior = prior + last
    ends_ref[...] = ends


def rates(dt, a_log):
    length = dt.shape[1]
    return pl.pallas_call(
        rates_kernel,
        out_shape=[
            jax.ShapeDtypeStruct((length, 128), F32),
            jax.ShapeDtypeStruct((SLOT, length), F32),
            jax.ShapeDtypeStruct((SLOT, 128), F32),
        ],
        in_specs=[whole()] * 2,
        out_specs=[whole()] * 3,
        compiler_params=params(),
        cost_estimate=cost(12 * 2 * SLOT * BLOCK * length, 1 << 20),
    )(dt, a_log)


def expander(ref, slot):
    row = lax.broadcasted_iota(jnp.int32, ref.shape, 0)
    head = lax.broadcasted_iota(jnp.int32, ref.shape, 1) // HEAD_DIM
    ref[...] = ((row == slot * SLOT + head) | (row == (slot + 1) * SLOT + head)).astype(BF16)


def act_kernel(own_rows, zone_count, me_ref, own_ref, *refs):
    zones = refs[: zone_count - 1]
    side_ref, others_ref, rim_ref, weight_ref, bias_ref, act_ref, first_ref, last_ref, raw = refs[
        zone_count - 1 :
    ]
    me = me_ref[0]
    size = 2 * zone_count
    per = own_ref.shape[0]

    def place(owner, ref, start):
        at = pl.multiple_of(RIM + owner * own_rows, 16)
        raw[pl.ds(at, own_rows), :] = ref[start : start + own_rows, :]

        @pl.when(owner == size - 1)
        def _():
            last_ref[0:RIM, :] = ref[start + own_rows - RIM : start + own_rows, :]
            if per > own_rows:
                last_ref[RIM : 2 * RIM, :] = ref[start + own_rows : start + own_rows + RIM, :]

    raw[0:RIM, :] = rim_ref[...]
    place(me, own_ref, 0)
    partner = me + 1 - 2 * lax.rem(me, 2)
    place(partner, side_ref, 0)
    for k in range(1, zone_count):
        place(lax.rem(me - 2 * k + size, size), zones[k - 1], 0)
        place(lax.rem(partner - 2 * k + size, size), others_ref, (k - 1) * per)
    first_ref[...] = raw[RIM : 2 * RIM, :]
    weight = weight_ref[...]
    bias = bias_ref[...]
    for c in range(act_ref.shape[0] // BLOCK):
        slab = raw[c * BLOCK : c * BLOCK + RIM + BLOCK, :].astype(F32)
        act_ref[c * BLOCK : (c + 1) * BLOCK, :] = conv_slab(slab, weight, bias)


def activate(me, own, zones, side, others, rim, weight, bias, own_rows):
    zone_count = len(zones) + 1
    length = 2 * zone_count * own_rows
    columns = own.shape[1]
    return pl.pallas_call(
        functools.partial(act_kernel, own_rows, zone_count),
        out_shape=[
            jax.ShapeDtypeStruct((length, columns), BF16),
            jax.ShapeDtypeStruct((RIM, columns), BF16),
            jax.ShapeDtypeStruct((2 * RIM, columns), BF16),
        ],
        in_specs=[whole(pltpu.SMEM)] + [whole()] * (zone_count + 5),
        out_specs=[whole()] * 3,
        scratch_shapes=[pltpu.VMEM((RIM + length, columns), BF16)],
        compiler_params=params(),
        cost_estimate=cost(20 * length * columns, 4 * length * columns, length * columns),
    )(me, own, *zones, side, others, rim, weight, bias)


def block_state(b_block, x_ref, q_block, expand_ref, columns):
    weight = jnp.dot(q_block, expand_ref[:, columns], preferred_element_type=F32)
    scaled = (x_ref[:, columns].astype(F32) * weight).astype(BF16)
    return lax.dot_general(
        b_block, scaled, (((0,), (0,)), ((), ())), preferred_element_type=F32
    )


def tiles(width):
    step = min(512, width)
    return [slice(i, i + step) for i in range(0, width, step)]


def later_states_kernel(b_ref, x_ref, q_ref, dec_ref, starts_ref, total_ref, expand_ref):
    step = pl.program_id(0)

    @pl.when(step == 0)
    def _():
        expander(expand_ref, 1)
        total_ref[...] = jnp.zeros_like(total_ref)

    b_block = b_ref[...]
    q_block = q_ref[...].astype(BF16)
    for columns in tiles(x_ref.shape[1]):
        before = total_ref[:, columns]
        starts_ref[0, :, columns] = before.astype(BF16)
        decay = dec_ref[pl.ds(step + 1, 1), columns]
        total_ref[:, columns] = decay * before + block_state(
            b_block, x_ref, q_block, expand_ref, columns
        )


def later_states(b_act, x, q, dec):
    length, width = x.shape
    count = length // BLOCK - 1
    return pl.pallas_call(
        later_states_kernel,
        grid=(count,),
        out_shape=[
            jax.ShapeDtypeStruct((count, STATE, width), BF16),
            jax.ShapeDtypeStruct((STATE, width), F32),
        ],
        in_specs=[
            pl.BlockSpec((BLOCK, STATE), lambda c: (c + 1, 0)),
            pl.BlockSpec((BLOCK, width), lambda c: (c + 1, 0)),
            pl.BlockSpec((BLOCK, 128), lambda c: (c + 1, 0)),
            pl.BlockSpec(dec.shape, lambda c: (0, 0)),
        ],
        out_specs=[
            pl.BlockSpec((1, STATE, width), lambda c: (c, 0, 0)),
            pl.BlockSpec((STATE, width), lambda c: (0, 0)),
        ],
        scratch_shapes=[pltpu.VMEM((128, width), BF16)],
        compiler_params=params(),
        cost_estimate=cost(4 * length * STATE * width, 4 * length * width),
    )(b_act, x, q, dec)


def first_state_kernel(
    b_ref, first_ref, rim_ref, weight_ref, bias_ref, x_ref, q_ref, dec_ref, later_ref,
    b_out, state_ref, total_ref, expand_ref,
):
    expander(expand_ref, 1)
    slab = jnp.concatenate([rim_ref[...], first_ref[...]], axis=0).astype(F32)
    fixed = conv_slab(slab, weight_ref[...], bias_ref[...])
    b_block = jnp.concatenate([fixed, b_ref[RIM:, :]], axis=0)
    b_out[...] = b_block
    q_block = q_ref[...].astype(BF16)
    row = dec_ref.shape[0] - 2
    for columns in tiles(x_ref.shape[1]):
        state = block_state(b_block, x_ref, q_block, expand_ref, columns)
        state_ref[:, columns] = state
        total = later_ref[:, columns] + dec_ref[row : row + 1, columns] * state
        total_ref[:, columns] = total.astype(BF16)


def first_state(b_act, first, rim, weight, bias, x, q, dec, later):
    length, width = x.shape
    full = lambda a: pl.BlockSpec(a.shape, lambda c: (0,) * a.ndim)
    return pl.pallas_call(
        first_state_kernel,
        grid=(1,),
        out_shape=[
            jax.ShapeDtypeStruct(b_act.shape, BF16),
            jax.ShapeDtypeStruct((STATE, width), F32),
            jax.ShapeDtypeStruct((STATE, width), BF16),
        ],
        in_specs=[
            pl.BlockSpec((BLOCK, STATE), lambda c: (0, 0)),
            full(first), full(rim), full(weight), full(bias),
            pl.BlockSpec((BLOCK, width), lambda c: (0, 0)),
            pl.BlockSpec((BLOCK, 128), lambda c: (0, 0)),
            full(dec), full(later),
        ],
        out_specs=[
            pl.BlockSpec((BLOCK, STATE), lambda c: (0, 0)),
            pl.BlockSpec((STATE, width), lambda c: (0, 0)),
            pl.BlockSpec((STATE, width), lambda c: (0, 0)),
        ],
        scratch_shapes=[pltpu.VMEM((128, width), BF16)],
        input_output_aliases={0: 0},
        compiler_params=params(),
        cost_estimate=cost(4 * BLOCK * STATE * width, 12 * BLOCK * width),
    )(b_act, first, rim, weight, bias, x, q, dec, later)


def inner_kernel(
    c_ref, b_ref, x_ref, q_ref, brow_ref, starts_ref, state_ref, dec_ref, skip_ref,
    out_ref, expand_ref,
):
    step = pl.program_id(0)
    block_count = pl.num_programs(0)
    half = BLOCK // 2

    @pl.when(step == 0)
    def _():
        expander(expand_ref, 3)

    c_block = c_ref[...]
    gram = lax.dot_general(
        c_block, b_ref[...], (((1,), (1,)), ((), ())), preferred_element_type=F32
    )
    lower = lax.broadcasted_iota(jnp.int32, (half, half), 0) >= lax.broadcasted_iota(
        jnp.int32, (half, half), 1
    )
    gram_00 = jnp.where(lower, gram[:half, :half], 0.0)
    gram_10 = gram[half:, :half]
    gram_11 = jnp.where(lower, gram[half:, half:], 0.0)
    q_block = q_ref[...]
    q_short = q_block.astype(BF16)
    head_count = x_ref.shape[1] // HEAD_DIM
    for h in range(head_count):
        columns = slice(h * HEAD_DIM, (h + 1) * HEAD_DIM)
        rise = jnp.broadcast_to(q_block[:, h : h + 1], (BLOCK, half))
        fall = brow_ref[h : h + 1, :]
        w_00 = gram_00 * jnp.exp2(jnp.minimum(rise[:half] - fall[:, :half], 120.0))
        w_10 = gram_10 * jnp.exp2(rise[half:] - fall[:, :half])
        w_11 = gram_11 * jnp.exp2(jnp.minimum(rise[half:] - fall[:, half:], 120.0))
        x_head = x_ref[:, columns]
        top = jnp.dot(w_00.astype(BF16), x_head[:half], preferred_element_type=F32)
        low = jnp.concatenate([w_10.astype(BF16), w_11.astype(BF16)], axis=1)
        bottom = jnp.dot(low, x_head, preferred_element_type=F32)
        out_ref[:, columns] = jnp.concatenate([top, bottom], axis=0) + skip_ref[
            :, columns
        ] * x_head.astype(F32)

    @pl.when(step > 0)
    def _():
        for columns in tiles(x_ref.shape[1]):
            decay = dec_ref[pl.ds(block_count + step, 1), columns]
            start = starts_ref[0, :, columns].astype(F32) + decay * state_ref[:, columns]
            grown = jnp.dot(q_short, expand_ref[:, columns], preferred_element_type=F32)
            carried = jnp.dot(c_block, start.astype(BF16), preferred_element_type=F32)
            out_ref[:, columns] += grown * carried


def inner(c_act, b_act, x, q, brow, starts, state, dec, skip):
    length, width = x.shape
    count = length // BLOCK
    full = lambda a: pl.BlockSpec(a.shape, lambda c: (0,) * a.ndim)
    return pl.pallas_call(
        inner_kernel,
        grid=(count,),
        out_shape=jax.ShapeDtypeStruct((length, width), F32),
        in_specs=[
            pl.BlockSpec((BLOCK, STATE), lambda c: (c, 0)),
            pl.BlockSpec((BLOCK, STATE), lambda c: (c, 0)),
            pl.BlockSpec((BLOCK, width), lambda c: (c, 0)),
            pl.BlockSpec((BLOCK, 128), lambda c: (c, 0)),
            pl.BlockSpec((SLOT, BLOCK), lambda c: (0, c)),
            pl.BlockSpec((1, STATE, width), lambda c: (jnp.maximum(c - 1, 0), 0, 0)),
            full(state), full(dec), full(skip),
        ],
        out_specs=pl.BlockSpec((BLOCK, width), lambda c: (c, 0)),
        scratch_shapes=[pltpu.VMEM((128, width), BF16)],
        compiler_params=params(),
        cost_estimate=cost(8 * length * STATE * width, 8 * length * width, length * width * 2),
    )(c_act, b_act, x, q, brow, starts, state, dec, skip)


def gate_kernel(c_ref, y_ref, z_ref, q_ref, in_ref, out_ref, sum_ref, expand_ref):
    @pl.when(pl.program_id(0) == 0)
    def _():
        expander(expand_ref, 5)

    c_block = c_ref[...]
    q_short = q_ref[...].astype(BF16)
    squares = jnp.zeros((BLOCK, 128), F32)
    for columns in tiles(y_ref.shape[1]):
        grown = jnp.dot(q_short, expand_ref[:, columns], preferred_element_type=F32)
        carried = jnp.dot(c_block, in_ref[:, columns], preferred_element_type=F32)
        gated = (y_ref[:, columns] + grown * carried) * silu(z_ref[:, columns].astype(F32))
        out_ref[:, columns] = gated
        square = gated * gated
        for i in range(0, square.shape[1], 128):
            squares = squares + square[:, i : i + 128]
    sum_ref[...] = lax.dot_general(
        jnp.ones((8, 128), F32), squares, (((1,), (1,)), ((), ())),
        precision=HIGHEST, preferred_element_type=F32,
    )[0:1]


def gate(c_act, y, z, q, incoming):
    length, width = y.shape
    count = length // BLOCK
    return pl.pallas_call(
        gate_kernel,
        grid=(count,),
        out_shape=[
            jax.ShapeDtypeStruct((length, width), F32),
            jax.ShapeDtypeStruct((1, length), F32),
        ],
        in_specs=[
            pl.BlockSpec((BLOCK, STATE), lambda c: (c, 0)),
            pl.BlockSpec((BLOCK, width), lambda c: (c, 0)),
            pl.BlockSpec((BLOCK, width), lambda c: (c, 0)),
            pl.BlockSpec((BLOCK, 128), lambda c: (c, 0)),
            pl.BlockSpec((STATE, width), lambda c: (0, 0)),
        ],
        out_specs=[
            pl.BlockSpec((BLOCK, width), lambda c: (c, 0)),
            pl.BlockSpec((1, BLOCK), lambda c: (0, c)),
        ],
        scratch_shapes=[pltpu.VMEM((128, width), BF16)],
        input_output_aliases={1: 0},
        compiler_params=params(),
        cost_estimate=cost(4 * length * STATE * width, 10 * length * width, length * width),
    )(c_act, y, z, q, incoming)


def norm_kernel(g_ref, one_ref, two_ref, gain_ref, out_ref):
    square_sum = one_ref[...] + two_ref[...]
    inverse = lax.rsqrt(square_sum / INNER + 1e-05)
    scale = jnp.broadcast_to(inverse, (128, BLOCK)).T
    for i in range(0, g_ref.shape[1], 128):
        columns = slice(i, i + 128)
        out_ref[:, columns] = (g_ref[:, columns] * scale * gain_ref[:, columns]).astype(BF16)


def norm(gated, one, two, gain):
    length, width = gated.shape
    return pl.pallas_call(
        norm_kernel,
        grid=(length // BLOCK,),
        out_shape=jax.ShapeDtypeStruct((length, width), BF16),
        in_specs=[
            pl.BlockSpec((BLOCK, width), lambda c: (c, 0)),
            pl.BlockSpec((1, BLOCK), lambda c: (0, c)),
            pl.BlockSpec((1, BLOCK), lambda c: (0, c)),
            pl.BlockSpec((1, width), lambda c: (0, 0)),
        ],
        out_specs=pl.BlockSpec((BLOCK, width), lambda c: (c, 0)),
        compiler_params=params(),
        cost_estimate=cost(4 * length * width, 6 * length * width),
    )(gated, one, two, gain)


def zone_shift(a, k):
    size = lax.axis_size("head")
    return lax.ppermute(a, "head", [(i, (i + 2 * k) % size) for i in range(size)])


def side_swap(a):
    size = lax.axis_size("head")
    return lax.ppermute(a, "head", [(i, i ^ 1) for i in range(size)])


def gather(own):
    zone_count = lax.axis_size("head") // 2
    zones = [zone_shift(own, k) for k in range(1, zone_count)]
    side = side_swap(own)
    others = side_swap(jnp.concatenate(zones, axis=0))
    return own, zones, side, others


def spread_heads(rows):
    return jnp.repeat(rows, HEAD_DIM, axis=1)


def chained_state(total, log_total):
    size = lax.axis_size("seq")
    place = lax.axis_index("seq")
    if size == 4:
        swap = [(0, 1), (1, 0), (2, 3), (3, 2)]
        odd = lax.rem(place, 2) == 1
        half = total.shape[1] // 2
        partner_log = lax.ppermute(log_total, "seq", swap)
        own_decay = spread_heads(jnp.exp(log_total)[None, :])
        partner_decay = spread_heads(jnp.exp(partner_log)[None, :])
        early, late = total[:, :half], total[:, half:]
        kept = jnp.where(odd, early, late)
        got = lax.ppermute(jnp.where(odd, late, early), "seq", swap)
        kept_partner_decay = jnp.where(odd, partner_decay[:, :half], partner_decay[:, half:])
        kept_own_decay = jnp.where(odd, own_decay[:, :half], own_decay[:, half:])
        kept_f, got_f = kept.astype(F32), got.astype(F32)
        both = jnp.where(
            odd, kept_own_decay * got_f + kept_f, kept_partner_decay * kept_f + got_f
        )
        crossed = lax.ppermute(both.astype(BF16), "seq", [(0, 2), (1, 3)])
        crossed_f = crossed.astype(F32)
        after_even = (
            jnp.where(odd, kept_partner_decay, kept_own_decay) * crossed_f
            + jnp.where(odd, got_f, kept_f)
        ).astype(BF16)
        last = lax.ppermute(jnp.where(odd, crossed, after_even), "seq", swap)
        return jnp.concatenate(
            [jnp.where(odd, after_even, last), jnp.where(odd, last, crossed)], axis=1
        )
    totals = lax.all_gather(total, "seq")
    logs = lax.all_gather(log_total, "seq")

    def one(hop, state):
        decay = spread_heads(jnp.exp(lax.dynamic_index_in_dim(logs, hop, 0, True)))
        return decay * state + lax.dynamic_index_in_dim(totals, hop, 0, False).astype(F32)

    return lax.fori_loop(0, place, one, jnp.zeros(total.shape, F32)).astype(BF16)


def on_device(x_inner, z_gate, bc_raw, conv_weight, conv_bias, dt_raw, a_log, d_skip, norm_gain):
    length = x_inner.shape[0]
    head_count = a_log.shape[0]
    block_count = length // BLOCK
    own_rows = bc_raw.shape[0]
    seq_size = lax.axis_size("seq")
    me = lax.axis_index("head").astype(jnp.int32).reshape(1)
    weight_b, weight_c = conv_weight[:, :STATE], conv_weight[:, STATE:]
    bias_b, bias_c = conv_bias[None, :STATE], conv_bias[None, STATE:]
    no_rim = jnp.zeros((RIM, STATE), BF16)

    own_c = bc_raw[:, STATE:]
    own_b = jnp.concatenate([bc_raw[:, :STATE], own_c[-RIM:]], axis=0)
    parts_b = gather(own_b)
    parts_c = gather(own_c)

    pad = ((0, SLOT - head_count), (0, 0))
    q, brow, ends = rates(jnp.pad(dt_raw.T, pad), jnp.pad(a_log[:, None], pad))
    end = ends[:head_count, :block_count].T
    log_total = jnp.sum(end, axis=0)
    from_one = jnp.cumsum(end[1:], axis=0)
    nothing = jnp.zeros((2, head_count), F32)
    logs = jnp.concatenate([end, nothing, from_one, log_total[None]], axis=0)
    dec = spread_heads(jnp.exp(logs))
    skip = spread_heads(d_skip[None, :])

    b_act, first_b, last_rows = activate(me, *parts_b, no_rim, weight_b, bias_b, own_rows)
    rims = lax.ppermute(last_rows, "seq", [(i, i + 1) for i in range(seq_size - 1)])
    starts, later = later_states(b_act, x_inner, q, dec)
    b_act, state_0, total = first_state(
        b_act, first_b, rims[:RIM], weight_b, bias_b, x_inner, q, dec, later
    )
    incoming = chained_state(total, log_total)
    c_act, _, _ = activate(me, *parts_c, rims[RIM:], weight_c, bias_c, own_rows)
    local = inner(c_act, b_act, x_inner, q, brow, starts, state_0, dec, skip)
    gated, squares = gate(c_act, local, z_gate, q, incoming)
    for k in range(1, lax.axis_size("head") // 2):
        squares = squares if k > 1 else [squares]
        squares.append(zone_shift(squares[0], k))
    column = sum(squares[1:], squares[0])
    return norm(gated, column, side_swap(column), norm_gain[None, :])


def solution(mesh):
    placed = (
        P("seq", "head"),
        P("seq", "head"),
        P(("seq", "head"), None),
        P(),
        P(),
        P("seq", "head"),
        P("head"),
        P("head"),
        P("head"),
    )
    return jax.shard_map(
        on_device, mesh=mesh, in_specs=placed, out_specs=P("seq", "head"), check_vma=False
    )
```

time: 243 us -> 122 us (0.50)
  matrix products: 64 us -> 0 us
  Pallas kernels: 0 us -> 52.9 us
  other arithmetic: 36.2 us -> 1.48 us
  local copies, waits for them, and re-layouts: 35 us -> 6.78 us
  blocking collectives: 27.7 us -> 0 us
  waiting for transfers between devices: 58.4 us -> 34.7 us
  starting transfers between devices: 4.9 us -> 24.8 us
  between operations: 14.4 us -> 0.2 us
    dot_general x5 -> x0, matrix products: 64 us -> none  [the longest x1 21.9 us: on_device(): jnp.einsum('chij,cjhp->cihp', weights, x_float, precision=highest)]
    all_gather x2 -> x0, waiting for transfers between devices: 57.9 us -> none  [the longest x1 30.9 us: on_device(): bc_act = lax.all_gather(own_act, 'head', axis=0, tiled=True)]
    pallas_call x0 -> x8, Pallas kernels: none -> 52.9 us  [the longest x1 14.4 us: inner(): pl.pallas_call(inner_kernel, grid=(count,), out_shape=jax.ShapeDtypeStruc...]
    ppermute x1 -> x19, waiting for transfers between devices: 0.45 us -> 34.7 us  [the longest x5 18.6 us: side_swap(): return lax.ppermute(a, 'head', [(i, i ^ 1) for i in range(size)])]
    psum x1 -> x0, blocking collectives: 21.6 us -> none  [on_device(): square_sum = lax.psum(jnp.sum(gated_out * gated_out, axis=1), 'head')]
    ppermute x1 -> x19, starting transfers between devices: 4.86 us -> 24.8 us  [the longest x9 12.6 us: zone_shift(): lax.ppermute(a, 'head', [(i, (i + 2 * k) % size) for i in range(size)])]
    add x1 -> x0, local copies, waits for them, and re-layouts: 16.3 us -> none  [on_device(): ssm_out = inner_part + carried_part + d_skip[None, None, :, None] * x_float]
    convert_element_type x3 -> x1, other arithmetic: 16 us -> 0.35 us  [chained_state(): crossed = lax.ppermute(both.astype(BF16), 'seq', [(0, 2), (1, 3)])]
  transfers between devices with their start and end apart: 3 -> 19, of which waited for: 3 -> 10; matrix products, arithmetic and copies ran while one was open for 16% -> 3% of each run, Pallas kernels for 0% -> 21%
where the time goes in v1:
time: 122 us; the launch traced here: 121 us
  Pallas kernels  52.9 us (43%)
  waiting for transfers between devices  34.7 us (28%)
  starting transfers between devices  24.8 us (20%)
  local copies, waits for them, and re-layouts  6.78 us (6%)
  other arithmetic  1.48 us (1%)
    ppermute x5, waiting for transfers between devices, side_swap(): return lax.ppermute(a, 'head', [(i, i ^ 1) for i in range(size)])  18.6 us
    ppermute x9, waiting for transfers between devices, zone_shift(): lax.ppermute(a, 'head', [(i, (i + 2 * k) % size) for i in range(size)])  14.6 us
    pallas_call x1, Pallas kernels, inner(): pl.pallas_call(inner_kernel, grid=(count,), out_shape=jax.ShapeDtypeStruc...  14.4 us
    pallas_call x1, Pallas kernels, gate(): pl.pallas_call(gate_kernel, grid=(count,), out_shape=[jax.ShapeDtypeStruc...  14.3 us
    ppermute x9, starting transfers between devices, zone_shift(): lax.ppermute(a, 'head', [(i, (i + 2 * k) % size) for i in range(size)])  12.6 us
    pallas_call x1, Pallas kernels, later_states(): pl.pallas_call(later_states_kernel, grid=(count,), out_shape=[jax.ShapeDt...  9.09 us
    pallas_call x1, Pallas kernels, norm(): pl.pallas_call(norm_kernel, grid=(length // BLOCK,), out_shape=jax.ShapeD...  8.97 us
    ppermute x5, starting transfers between devices, side_swap(): return lax.ppermute(a, 'head', [(i, i ^ 1) for i in range(size)])  6.27 us
  transfers between devices with their start and end apart: 19, of which 10 were waited for; matrix products, arithmetic and copies ran while one was open for 3% of the time, Pallas kernels for 21%

profile of v1, /device:TPU:0, one launch (start us, length us, event | category | flops | bytes accessed | tf_op | source)
XLA Modules:
  0.0 120.8 jit_solution(17111007916572081118)
XLA Ops:
  1.7 3.0 %collective-permute-start.8 = (bf16[208,256]{1,0:T(8,128)(2,1)S(1)}, bf16[208,256]{1,0:T(8,128)(2,1)S(1)}, u32[]{:S(2)}, u32[]{:S(2)}) collective-permute-start(bf16[208,256]{1,0:T(8,128)(2,1)S(1)} %pad_maximum_fusion.3.own_ref), channel_id=1, source_target_pairs={{0,1},{1,0},{2,3},{3,2},{4,5},{5,4},{6,7},{7,6},{8,9},{9,8},{10,11... | collective-permute-start | bytes 319496 | tf_op jit(solution)/shard_map/ppermute | solution.py:425
  4.7 3.6 %collective-permute-start.7 = (bf16[208,256]{1,0:T(8,128)(2,1)S(1)}, bf16[208,256]{1,0:T(8,128)(2,1)S(1)}, u32[]{:S(2)}, u32[]{:S(2)}) collective-permute-start(bf16[208,256]{1,0:T(8,128)(2,1)S(1)} %pad_maximum_fusion.3.own_ref), channel_id=1, source_target_pairs={{0,6},{1,7},{2,0},{3,1},{4,2},{5,3},{6,4},{7,5},{8,14},{9,15},{10,... | collective-permute-start | bytes 319496 | tf_op jit(solution)/shard_map/ppermute | solution.py:420
  13.2 4.1 %collective-permute-done.6.refs_1_ = bf16[208,256]{1,0:T(8,128)(2,1)S(1)} collective-permute-done((bf16[208,256]{1,0:T(8,128)(2,1)S(1)}, bf16[208,256]{1,0:T(8,128)(2,1)S(1)}, u32[]{:S(2)}, u32[]{:S(2)}) %collective-permute-start.6) | collective-permute-done | bytes 106528 | tf_op jit(solution)/shard_map/ppermute | solution.py:420
  19.0 7.1 %collective-permute-done.9.refs_4_ = bf16[624,256]{1,0:T(8,128)(2,1)S(1)} collective-permute-done((bf16[624,256]{1,0:T(8,128)(2,1)S(1)}, bf16[624,256]{1,0:T(8,128)(2,1)S(1)}, u32[]{:S(2)}, u32[]{:S(2)}) %collective-permute-start.9) | collective-permute-done | bytes 319520 | tf_op jit(solution)/shard_map/ppermute | solution.py:425
  27.2 1.3 %collective-permute-start.10 = (bf16[32,256]{1,0:T(8,128)(2,1)S(1)}, bf16[32,256]{1,0:T(8,128)(2,1)S(1)}, u32[]{:S(2)}, u32[]{:S(2)}) collective-permute-start(bf16[32,256]{1,0:T(8,128)(2,1)S(1)} %get-tuple-element.19), channel_id=1, source_target_pairs={{0,8},{8,16},{16,24},{1,9},{9,17},{17,25},{2,10},{10,18},{18,26},{... | collective-permute-start | bytes 49160 | tf_op jit(solution)/shard_map/ppermute | solution.py:506
  28.5 9.1 %shard_map.94 = (bf16[5,256,2048]{2,1,0:T(8,128)(2,1)}, f32[256,2048]{1,0:T(8,128)S(1)}) custom-call(bf16[1536,256]{1,0:T(8,128)(2,1)S(1)} %get-tuple-element.21.b_ref, bf16[1536,2048]{1,0:T(8,128)(2,1)} %x_ref.5, f32[1536,128]{1,0:T(8,128)S(1)} %get-tuple-element.23.q_ref, f32[14,2048]{1,0:T(8,128)S(1)} %bitcast.18), custom_call_target="tpu_custom_call" | custom-call | flops 3221225472 | bytes 12582912 | tf_op jit(solution)/shard_map/pallas_call | solution.py:196
  37.6 1.3 %copy-done = f32[256,2048]{1,0:T(8,128)} copy-done((f32[256,2048]{1,0:T(8,128)}, f32[256,2048]{1,0:T(8,128)S(1)}, u32[]{:S(2)}) %copy-start) | copy-done | bytes 2097176
  38.9 3.1 %shard_map.95 = (bf16[1536,256]{1,0:T(8,128)(2,1)S(1)}, f32[256,2048]{1,0:T(8,128)S(1)}, bf16[256,2048]{1,0:T(8,128)(2,1)S(1)}) custom-call(bf16[1536,256]{1,0:T(8,128)(2,1)S(1)} %get-tuple-element.21.b_ref, bf16[16,256]{1,0:T(8,128)(2,1)S(1)} %get-tuple-element.22.first_ref, ...), custom_call_target="tpu_custom_call", output_to_operand_aliasing={{0}: (0, {})} | custom-call | flops 536870912 | bytes 6291456 | tf_op jit(solution)/shard_map/pallas_call | solution.py:240
  42.1 2.3 %collective-permute-start.12 = (bf16[256,1024]{1,0:T(8,128)(2,1)S(1)}, bf16[256,1024]{1,0:T(8,128)(2,1)S(1)}, u32[]{:S(2)}, u32[]{:S(2)}) collective-permute-start(bf16[256,1024]{1,0:T(8,128)(2,1)S(1)} %broadcast_select_fusion.4), channel_id=1, source_target_pairs={{0,8},{8,0},{16,24},{24,16},{1,9},{9,1},{17,25},{25,17},{2,10},{10... | collective-permute-start | bytes 1572872 | tf_op jit(solution)/shard_map/ppermute | solution.py:452
  44.5 1.5 %collective-permute-done.11 = f32[16]{0:T(128)S(1)} collective-permute-done((f32[16]{0:T(128)S(1)}, f32[16]{0:T(128)S(1)}, u32[]{:S(2)}, u32[]{:S(2)}) %collective-permute-start.11) | collective-permute-done | bytes 96 | tf_op jit(solution)/shard_map/ppermute | solution.py:447
  46.5 2.2 %collective-permute-start.13 = (bf16[256,1024]{1,0:T(8,128)(2,1)S(1)}, bf16[256,1024]{1,0:T(8,128)(2,1)S(1)}, u32[]{:S(2)}, u32[]{:S(2)}) collective-permute-start(bf16[256,1024]{1,0:T(8,128)(2,1)S(1)} %fusion.1), channel_id=1, source_target_pairs={{0,16},{8,24},{1,17},{9,25},{2,18},{10,26},{3,19},{11,27},{4,20},{... | collective-permute-start | bytes 1572872 | tf_op jit(solution)/shard_map/ppermute | solution.py:459
  49.2 2.0 %collective-permute-start.1 = (bf16[192,256]{1,0:T(8,128)(2,1)S(1)}, bf16[192,256]{1,0:T(8,128)(2,1)S(1)}, u32[]{:S(2)}, u32[]{:S(2)}) collective-permute-start(bf16[192,256]{1,0:T(8,128)(2,1)S(1)} %get-tuple-element.41.own_ref), channel_id=1, source_target_pairs={{0,4},{1,5},{2,6},{3,7},{4,0},{5,1},{6,2},{7,3},{8,12},{9,13},{10,... | collective-permute-start | bytes 294920 | tf_op jit(solution)/shard_map/ppermute | solution.py:420
  51.2 1.9 %collective-permute-start = (bf16[192,256]{1,0:T(8,128)(2,1)S(1)}, bf16[192,256]{1,0:T(8,128)(2,1)S(1)}, u32[]{:S(2)}, u32[]{:S(2)}) collective-permute-start(bf16[192,256]{1,0:T(8,128)(2,1)S(1)} %get-tuple-element.41.own_ref), channel_id=1, source_target_pairs={{0,2},{1,3},{2,4},{3,5},{4,6},{5,7},{6,0},{7,1},{8,10},{9,11},{10,... | collective-permute-start | bytes 294920 | tf_op jit(solution)/shard_map/ppermute | solution.py:420
  53.6 6.7 %collective-permute-done.1.refs_1_ = bf16[192,256]{1,0:T(8,128)(2,1)S(1)} collective-permute-done((bf16[192,256]{1,0:T(8,128)(2,1)S(1)}, bf16[192,256]{1,0:T(8,128)(2,1)S(1)}, u32[]{:S(2)}, u32[]{:S(2)}) %collective-permute-start.1) | collective-permute-done | bytes 98336 | tf_op jit(solution)/shard_map/ppermute | solution.py:420
  60.9 1.5 %collective-permute-start.3 = (bf16[192,256]{1,0:T(8,128)(2,1)S(1)}, bf16[192,256]{1,0:T(8,128)(2,1)S(1)}, u32[]{:S(2)}, u32[]{:S(2)}) collective-permute-start(bf16[192,256]{1,0:T(8,128)(2,1)S(1)} %get-tuple-element.41.own_ref), channel_id=1, source_target_pairs={{0,1},{1,0},{2,3},{3,2},{4,5},{5,4},{6,7},{7,6},{8,9},{9,8},{10,11... | collective-permute-start | bytes 294920 | tf_op jit(solution)/shard_map/ppermute | solution.py:425
  62.4 8.3 %collective-permute-done.3.refs_3_ = bf16[192,256]{1,0:T(8,128)(2,1)S(1)} collective-permute-done((bf16[192,256]{1,0:T(8,128)(2,1)S(1)}, bf16[192,256]{1,0:T(8,128)(2,1)S(1)}, u32[]{:S(2)}, u32[]{:S(2)}) %collective-permute-start.3) | collective-permute-done | bytes 98336 | tf_op jit(solution)/shard_map/ppermute | solution.py:425
  72.4 14.4 %shard_map.96.y_ref = f32[1536,2048]{1,0:T(8,128)} custom-call(bf16[1536,256]{1,0:T(8,128)(2,1)S(1)} %get-tuple-element.20.c_ref, bf16[1536,256]{1,0:T(8,128)(2,1)S(1)} %get-tuple-element.26.b_ref, bf16[1536,2048]{1,0:T(8,128)(2,1)} %x_ref.5, f32[1536,128]{1,0:T(8,128)S(1)} %get-tuple-element.23.q_ref, f32[16,1536]{1,0:T(8,128)S(1)} %get-tuple-element.27.brow_ref, ...), custom_call_target="tpu_custom_call" | custom-call | flops 6442450944 | bytes 25165824 | tf_op jit(solution)/shard_map/pallas_call | solution.py:321
  87.0 14.3 %shard_map.97 = (f32[1536,2048]{1,0:T(8,128)}, f32[1,1536]{1,0:T(1,128)S(1)}) custom-call(bf16[1536,256]{1,0:T(8,128)(2,1)S(1)} %get-tuple-element.20.c_ref, f32[1536,2048]{1,0:T(8,128)} %shard_map.96.y_ref, bf16[1536,2048]{1,0:T(8,128)(2,1)} %z_ref.1, f32[1536,128]{1,0:T(8,128)S(1)} %get-tuple-element.23.q_ref, ...), custom_call_target="tpu_custom_call", output_to_operand_aliasing={{0}: (1, {})} | custom-call | flops 3221225472 | bytes 31457280 | tf_op jit(solution)/shard_map/pallas_call | solution.py:366
  101.5 1.2 collective-permute-start.16
  102.7 2.0 %collective-permute-start.15 = (f32[1,1536]{1,0:T(1,128)S(1)}, f32[1,1536]{1,0:T(1,128)S(1)}, u32[]{:S(2)}, u32[]{:S(2)}) collective-permute-start(f32[1,1536]{1,0:T(1,128)S(1)} %get-tuple-element.32), channel_id=1, source_target_pairs={{0,2},{1,3},{2,4},{3,5},{4,6},{5,7},{6,0},{7,1},{8,10},{9,11},{10,... | collective-permute-start | bytes 18440 | tf_op jit(solution)/shard_map/ppermute | solution.py:420
  104.9 1.2 collective-permute-done.16
  106.1 2.1 %collective-permute-done.15 = f32[1,1536]{1,0:T(1,128)S(1)} collective-permute-done((f32[1,1536]{1,0:T(1,128)S(1)}, f32[1,1536]{1,0:T(1,128)S(1)}, u32[]{:S(2)}, u32[]{:S(2)}) %collective-permute-start.15) | collective-permute-done | bytes 6176 | tf_op jit(solution)/shard_map/ppermute | solution.py:420
  108.8 3.1 %collective-permute-done.18.two_ref = f32[1,1536]{1,0:T(1,128)S(1)} collective-permute-done((f32[1,1536]{1,0:T(1,128)S(1)}, f32[1,1536]{1,0:T(1,128)S(1)}, u32[]{:S(2)}, u32[]{:S(2)}) %collective-permute-start.18) | collective-permute-done | bytes 6176 | tf_op jit(solution)/shard_map/ppermute | solution.py:425
  111.9 9.0 %shard_map.98 = bf16[1536,2048]{1,0:T(8,128)(2,1)} custom-call(f32[1536,2048]{1,0:T(8,128)} %get-tuple-element.31.g_ref, f32[1,1536]{1,0:T(1,128)S(1)} %add_add_fusion.one_ref, f32[1,1536]{1,0:T(1,128)S(1)} %collective-permute-done.18.two_ref, f32[1,2048]{1,0:T(1,128)S(1)} %bitcast.24), custom_call_target="tpu_custom_call" | custom-call | flops 12582912 | bytes 18874368 | tf_op jit(solution)/shard_map/pallas_call | solution.py:402
  (63 shorter events, 14.2 us)
Async XLA Ops:
  1.7 17.3 %collective-permute-start.8 = (bf16[208,256]{1,0:T(8,128)(2,1)S(1)}, bf16[208,256]{1,0:T(8,128)(2,1)S(1)}, u32[]{:S(2)}, u32[]{:S(2)}) collective-permute-start(bf16[208,256]{1,0:T(8,128)(2,1)S(1)} %pad_maximum_fusion.3.own_ref), channel_id=1, source_target_pairs={{0,1},{1,0},{2,3},{3,2},{4,5},{5,4},{6,7},{7,6},{8,9},{9,8},{10,11... | collective-permute-start | bytes 319496 | tf_op jit(solution)/shard_map/ppermute | solution.py:425
  4.7 8.5 %collective-permute-start.7 = (bf16[208,256]{1,0:T(8,128)(2,1)S(1)}, bf16[208,256]{1,0:T(8,128)(2,1)S(1)}, u32[]{:S(2)}, u32[]{:S(2)}) collective-permute-start(bf16[208,256]{1,0:T(8,128)(2,1)S(1)} %pad_maximum_fusion.3.own_ref), channel_id=1, source_target_pairs={{0,6},{1,7},{2,0},{3,1},{4,2},{5,3},{6,4},{7,5},{8,14},{9,15},{10,... | collective-permute-start | bytes 319496 | tf_op jit(solution)/shard_map/ppermute | solution.py:420
  8.3 9.0 %collective-permute-start.6 = (bf16[208,256]{1,0:T(8,128)(2,1)S(1)}, bf16[208,256]{1,0:T(8,128)(2,1)S(1)}, u32[]{:S(2)}, u32[]{:S(2)}) collective-permute-start(bf16[208,256]{1,0:T(8,128)(2,1)S(1)} %pad_maximum_fusion.3.own_ref), channel_id=1, source_target_pairs={{0,4},{1,5},{2,6},{3,7},{4,0},{5,1},{6,2},{7,3},{8,12},{9,13},{10,... | collective-permute-start | bytes 319496 | tf_op jit(solution)/shard_map/ppermute | solution.py:420
  8.3 9.0 %collective-permute-start.5 = (bf16[208,256]{1,0:T(8,128)(2,1)S(1)}, bf16[208,256]{1,0:T(8,128)(2,1)S(1)}, u32[]{:S(2)}, u32[]{:S(2)}) collective-permute-start(bf16[208,256]{1,0:T(8,128)(2,1)S(1)} %pad_maximum_fusion.3.own_ref), channel_id=1, source_target_pairs={{0,2},{1,3},{2,4},{3,5},{4,6},{5,7},{6,0},{7,1},{8,10},{9,11},{10,... | collective-permute-start | bytes 319496 | tf_op jit(solution)/shard_map/ppermute | solution.py:420
  10.1 0.9 copy-start.2
  17.3 8.8 %collective-permute-start.9 = (bf16[624,256]{1,0:T(8,128)(2,1)S(1)}, bf16[624,256]{1,0:T(8,128)(2,1)S(1)}, u32[]{:S(2)}, u32[]{:S(2)}) collective-permute-start(bf16[624,256]{1,0:T(8,128)(2,1)S(1)} %pad_maximum_fusion.1), channel_id=1, source_target_pairs={{0,1},{1,0},{2,3},{3,2},{4,5},{5,4},{6,7},{7,6},{8,9},{9,8},{10,11... | collective-permute-start | bytes 958472 | tf_op jit(solution)/shard_map/ppermute | solution.py:425
  27.2 11.7 %collective-permute-start.10 = (bf16[32,256]{1,0:T(8,128)(2,1)S(1)}, bf16[32,256]{1,0:T(8,128)(2,1)S(1)}, u32[]{:S(2)}, u32[]{:S(2)}) collective-permute-start(bf16[32,256]{1,0:T(8,128)(2,1)S(1)} %get-tuple-element.19), channel_id=1, source_target_pairs={{0,8},{8,16},{16,24},{1,9},{9,17},{17,25},{2,10},{10,18},{18,26},{... | collective-permute-start | bytes 49160 | tf_op jit(solution)/shard_map/ppermute | solution.py:506
  37.6 1.3 %copy-start = (f32[256,2048]{1,0:T(8,128)}, f32[256,2048]{1,0:T(8,128)S(1)}, u32[]{:S(2)}) copy-start(f32[256,2048]{1,0:T(8,128)S(1)} %get-tuple-element.25.later_ref) | copy-start | bytes 6291460
  42.0 30.3 %copy-start.3 = (f32[16]{0:T(128)S(1)}, f32[16]{0:T(128)}, u32[]{:S(2)}) copy-start(f32[16]{0:T(128)} %param.16) | copy-start | bytes 196
  42.1 4.0 %collective-permute-start.12 = (bf16[256,1024]{1,0:T(8,128)(2,1)S(1)}, bf16[256,1024]{1,0:T(8,128)(2,1)S(1)}, u32[]{:S(2)}, u32[]{:S(2)}) collective-permute-start(bf16[256,1024]{1,0:T(8,128)(2,1)S(1)} %broadcast_select_fusion.4), channel_id=1, source_target_pairs={{0,8},{8,0},{16,24},{24,16},{1,9},{9,1},{17,25},{25,17},{2,10},{10... | collective-permute-start | bytes 1572872 | tf_op jit(solution)/shard_map/ppermute | solution.py:452
  44.4 1.5 %collective-permute-start.11 = (f32[16]{0:T(128)S(1)}, f32[16]{0:T(128)S(1)}, u32[]{:S(2)}, u32[]{:S(2)}) collective-permute-start(f32[16]{0:T(128)S(1)} %get-tuple-element.45), channel_id=1, source_target_pairs={{0,8},{8,0},{16,24},{24,16},{1,9},{9,1},{17,25},{25,17},{2,10},{10... | collective-permute-start | bytes 200 | tf_op jit(solution)/shard_map/ppermute | solution.py:447
  46.5 25.3 %collective-permute-start.13 = (bf16[256,1024]{1,0:T(8,128)(2,1)S(1)}, bf16[256,1024]{1,0:T(8,128)(2,1)S(1)}, u32[]{:S(2)}, u32[]{:S(2)}) collective-permute-start(bf16[256,1024]{1,0:T(8,128)(2,1)S(1)} %fusion.1), channel_id=1, source_target_pairs={{0,16},{8,24},{1,17},{9,25},{2,18},{10,26},{3,19},{11,27},{4,20},{... | collective-permute-start | bytes 1572872 | tf_op jit(solution)/shard_map/ppermute | solution.py:459
  48.7 4.9 %collective-permute-start.2 = (bf16[192,256]{1,0:T(8,128)(2,1)S(1)}, bf16[192,256]{1,0:T(8,128)(2,1)S(1)}, u32[]{:S(2)}, u32[]{:S(2)}) collective-permute-start(bf16[192,256]{1,0:T(8,128)(2,1)S(1)} %get-tuple-element.41.own_ref), channel_id=1, source_target_pairs={{0,6},{1,7},{2,0},{3,1},{4,2},{5,3},{6,4},{7,5},{8,14},{9,15},{10,... | collective-permute-start | bytes 294920 | tf_op jit(solution)/shard_map/ppermute | solution.py:420
  49.2 11.1 %collective-permute-start.1 = (bf16[192,256]{1,0:T(8,128)(2,1)S(1)}, bf16[192,256]{1,0:T(8,128)(2,1)S(1)}, u32[]{:S(2)}, u32[]{:S(2)}) collective-permute-start(bf16[192,256]{1,0:T(8,128)(2,1)S(1)} %get-tuple-element.41.own_ref), channel_id=1, source_target_pairs={{0,4},{1,5},{2,6},{3,7},{4,0},{5,1},{6,2},{7,3},{8,12},{9,13},{10,... | collective-permute-start | bytes 294920 | tf_op jit(solution)/shard_map/ppermute | solution.py:420
  51.2 9.1 %collective-permute-start = (bf16[192,256]{1,0:T(8,128)(2,1)S(1)}, bf16[192,256]{1,0:T(8,128)(2,1)S(1)}, u32[]{:S(2)}, u32[]{:S(2)}) collective-permute-start(bf16[192,256]{1,0:T(8,128)(2,1)S(1)} %get-tuple-element.41.own_ref), channel_id=1, source_target_pairs={{0,2},{1,3},{2,4},{3,5},{4,6},{5,7},{6,0},{7,1},{8,10},{9,11},{10,... | collective-permute-start | bytes 294920 | tf_op jit(solution)/shard_map/ppermute | solution.py:420
  60.3 10.4 %collective-permute-start.4 = (bf16[576,256]{1,0:T(8,128)(2,1)S(1)}, bf16[576,256]{1,0:T(8,128)(2,1)S(1)}, u32[]{:S(2)}, u32[]{:S(2)}) collective-permute-start(bf16[576,256]{1,0:T(8,128)(2,1)S(1)} %pad_maximum_fusion.2), channel_id=1, source_target_pairs={{0,1},{1,0},{2,3},{3,2},{4,5},{5,4},{6,7},{7,6},{8,9},{9,8},{10,11... | collective-permute-start | bytes 884744 | tf_op jit(solution)/shard_map/ppermute | solution.py:425
  60.9 9.8 %collective-permute-start.3 = (bf16[192,256]{1,0:T(8,128)(2,1)S(1)}, bf16[192,256]{1,0:T(8,128)(2,1)S(1)}, u32[]{:S(2)}, u32[]{:S(2)}) collective-permute-start(bf16[192,256]{1,0:T(8,128)(2,1)S(1)} %get-tuple-element.41.own_ref), channel_id=1, source_target_pairs={{0,1},{1,0},{2,3},{3,2},{4,5},{5,4},{6,7},{7,6},{8,9},{9,8},{10,11... | collective-permute-start | bytes 294920 | tf_op jit(solution)/shard_map/ppermute | solution.py:425
  72.2 14.5 %collective-permute-start.14 = (bf16[256,1024]{1,0:T(8,128)(2,1)S(1)}, bf16[256,1024]{1,0:T(8,128)(2,1)S(1)}, u32[]{:S(2)}, u32[]{:S(2)}) collective-permute-start(bf16[256,1024]{1,0:T(8,128)(2,1)S(1)} %get-tuple-element.33), channel_id=1, source_target_pairs={{0,8},{8,0},{16,24},{24,16},{1,9},{9,1},{17,25},{25,17},{2,10},{10... | collective-permute-start | bytes 1572872 | tf_op jit(solution)/shard_map/ppermute | solution.py:465
  87.0 24.9 %copy-start.1 = (f32[2048]{0:T(1024)S(1)}, f32[2048]{0:T(1024)}, u32[]{:S(2)}) copy-start(f32[2048]{0:T(1024)} %param.17) | copy-start | bytes 24580
  101.3 3.6 %collective-permute-start.17 = (f32[1,1536]{1,0:T(1,128)S(1)}, f32[1,1536]{1,0:T(1,128)S(1)}, u32[]{:S(2)}, u32[]{:S(2)}) collective-permute-start(f32[1,1536]{1,0:T(1,128)S(1)} %get-tuple-element.32), channel_id=1, source_target_pairs={{0,6},{1,7},{2,0},{3,1},{4,2},{5,3},{6,4},{7,5},{8,14},{9,15},{10,... | collective-permute-start | bytes 18440 | tf_op jit(solution)/shard_map/ppermute | solution.py:420
  101.5 4.5 %collective-permute-start.16 = (f32[1,1536]{1,0:T(1,128)S(1)}, f32[1,1536]{1,0:T(1,128)S(1)}, u32[]{:S(2)}, u32[]{:S(2)}) collective-permute-start(f32[1,1536]{1,0:T(1,128)S(1)} %get-tuple-element.32), channel_id=1, source_target_pairs={{0,4},{1,5},{2,6},{3,7},{4,0},{5,1},{6,2},{7,3},{8,12},{9,13},{10,... | collective-permute-start | bytes 18440 | tf_op jit(solution)/shard_map/ppermute | solution.py:420
  102.7 5.4 %collective-permute-start.15 = (f32[1,1536]{1,0:T(1,128)S(1)}, f32[1,1536]{1,0:T(1,128)S(1)}, u32[]{:S(2)}, u32[]{:S(2)}) collective-permute-start(f32[1,1536]{1,0:T(1,128)S(1)} %get-tuple-element.32), channel_id=1, source_target_pairs={{0,2},{1,3},{2,4},{3,5},{4,6},{5,7},{6,0},{7,1},{8,10},{9,11},{10,... | collective-permute-start | bytes 18440 | tf_op jit(solution)/shard_map/ppermute | solution.py:420
  108.2 3.7 %collective-permute-start.18 = (f32[1,1536]{1,0:T(1,128)S(1)}, f32[1,1536]{1,0:T(1,128)S(1)}, u32[]{:S(2)}, u32[]{:S(2)}) collective-permute-start(f32[1,1536]{1,0:T(1,128)S(1)} %add_add_fusion.one_ref), channel_id=1, source_target_pairs={{0,1},{1,0},{2,3},{3,2},{4,5},{5,4},{6,7},{7,6},{8,9},{9,8},{10,11... | collective-permute-start | bytes 18440 | tf_op jit(solution)/shard_map/ppermute | solution.py:425

commit v2 on v0

v2 whole, which is shorter than its diff:
```python
import functools
import math

import jax
import jax.numpy as jnp
from jax import lax
from jax.experimental import pallas as pl
from jax.experimental.pallas import tpu as pltpu
from jax.sharding import PartitionSpec as P

HEAD_DIM = 128
STATE = 256
BLOCK = 256
INNER = 16384
RIM = 16
SLOT = 16
LOG2E = math.log2(math.e)
F32 = jnp.float32
BF16 = jnp.bfloat16
HIGHEST = lax.Precision.HIGHEST
VMEM_LIMIT = 14 * 1024 * 1024


def params():
    return pltpu.CompilerParams(vmem_limit_bytes=VMEM_LIMIT)


def whole(memory_space=pltpu.VMEM):
    return pl.BlockSpec(memory_space=memory_space)


def kept_in_vmem(shape, dtype):
    return pltpu.VMEM(shape, dtype)


def stream_in(hbm_ref, held, sems, columns=None):
    copies = []
    for c in range(held.shape[0]):
        rows = pl.ds(c * BLOCK, BLOCK)
        source = hbm_ref.at[rows, :] if columns is None else hbm_ref.at[rows, columns]
        copy = pltpu.make_async_copy(source, held.at[c], sems.at[c])
        copy.start()
        copies.append(copy)
    return copies


def in_hbm(a):
    return pltpu.with_memory_space_constraint(a, pltpu.HBM)


def cost(flops, nbytes, trans=0):
    return pl.CostEstimate(flops=int(flops), bytes_accessed=int(nbytes), transcendentals=int(trans))


def silu(v):
    half = 0.5 * v
    return half + half * jnp.tanh(half)


def split(v):
    high = v.astype(BF16).astype(F32)
    return high, v - high


def conv_slab(slab, weight, bias):
    taps = weight.shape[0]
    total = jnp.broadcast_to(bias, slab.shape)
    for k in range(taps):
        shift = taps - 1 - k
        moved = pltpu.roll(slab, shift, 0) if shift else slab
        total = total + weight[k : k + 1, :] * moved
    total = total[RIM:]
    return (total * jax.nn.sigmoid(total)).astype(BF16)


def rates_kernel(dt_ref, a_ref, skip_ref, q_ref, b_ref, dec_ref, own_ref):
    block_count = dt_ref.shape[1] // BLOCK
    diagonal = lax.broadcasted_iota(jnp.int32, (SLOT, SLOT), 0) == lax.broadcasted_iota(
        jnp.int32, (SLOT, SLOT), 1
    )

    def upright(row):
        return jnp.sum(jnp.where(diagonal, row, 0.0), axis=1, keepdims=True)

    rate = -jnp.exp(upright(a_ref[...]))
    upper = (
        lax.broadcasted_iota(jnp.int32, (BLOCK, BLOCK), 0)
        <= lax.broadcasted_iota(jnp.int32, (BLOCK, BLOCK), 1)
    ).astype(F32)
    prior = jnp.zeros((SLOT, 1), F32)
    later = jnp.zeros((SLOT, 1), F32)
    lane = lax.broadcasted_iota(jnp.int32, (SLOT, SLOT), 1)
    logs = jnp.zeros((SLOT, SLOT), F32)
    for c in range(block_count):
        columns = slice(c * BLOCK, (c + 1) * BLOCK)
        dt = dt_ref[:, columns]
        step = jnp.maximum(dt, 0.0) + jnp.log1p(jnp.exp(-jnp.abs(dt)))
        cum = jnp.dot(rate * step, upper, precision=HIGHEST, preferred_element_type=F32)
        last = cum[:, BLOCK - 1 : BLOCK]
        scaled = cum * LOG2E
        b_ref[:, columns] = scaled - jnp.log(step) * LOG2E
        parts = [scaled]
        parts.extend(split(jnp.exp(last - cum) * step))
        parts.extend(split(jnp.exp(cum)))
        parts.extend(split(jnp.exp(cum + prior)))
        parts.append(jnp.zeros_like(cum))
        q_ref[columns, :] = jnp.concatenate(parts, axis=0).T
        logs = jnp.where(lane == c, last, logs)
        logs = jnp.where(lane == block_count + c, later, logs)
        prior = prior + last
        if c > 0:
            later = later + last
    logs = jnp.where(lane == 2 * block_count, later, logs)
    logs = jnp.where(lane == SLOT - 1, prior, logs)
    factors = jnp.where(lane == 2 * block_count + 1, upright(skip_ref[...]), jnp.exp(logs))
    width = dec_ref.shape[1]
    head = lax.broadcasted_iota(jnp.int32, (SLOT, width), 1) // HEAD_DIM
    spread = (lax.broadcasted_iota(jnp.int32, (SLOT, width), 0) == head).astype(F32)
    rows = lax.dot_general(
        factors, spread, (((0,), (0,)), ((), ())), precision=HIGHEST, preferred_element_type=F32
    )
    dec_ref[...] = rows
    own_ref[...] = rows[SLOT - 1 : SLOT]


def rates(dt, a_log, d_skip, width):
    length = dt.shape[1]
    return pl.pallas_call(
        rates_kernel,
        out_shape=[
            kept_in_vmem((length, 128), F32),
            kept_in_vmem((SLOT, length), F32),
            kept_in_vmem((SLOT, width), F32),
            kept_in_vmem((1, width), F32),
        ],
        in_specs=[whole()] * 3,
        out_specs=[whole()] * 4,
        compiler_params=params(),
        cost_estimate=cost(0, 0),
    )(dt, a_log, d_skip)


def expander(ref, slot, base):
    row = lax.broadcasted_iota(jnp.int32, ref.shape, 0)
    head = (lax.broadcasted_iota(jnp.int32, ref.shape, 1) + base) // HEAD_DIM
    ref[...] = ((row == slot * SLOT + head) | (row == (slot + 1) * SLOT + head)).astype(BF16)


def prepare_kernel(place_ref, bc_ref, b_ref, c_ref, place_out):
    rows = bc_ref.shape[0]
    for i in range(place_ref.shape[0]):
        place_out[i] = place_ref[i]
    b_ref[0:rows, :] = bc_ref[:, :STATE]
    b_ref[rows : rows + RIM, :] = bc_ref[rows - RIM :, STATE:]
    c_ref[...] = bc_ref[:, STATE:]


def prepare(place, bc_raw):
    rows = bc_raw.shape[0]
    return pl.pallas_call(
        prepare_kernel,
        out_shape=[
            jax.ShapeDtypeStruct((rows + RIM, STATE), BF16),
            jax.ShapeDtypeStruct((rows, STATE), BF16),
            pltpu.SMEM(place.shape, jnp.int32),
        ],
        in_specs=[whole(pltpu.SMEM), whole()],
        out_specs=[whole(), whole(), whole(pltpu.SMEM)],
        compiler_params=params(),
        cost_estimate=cost(0, 0),
    )(place, bc_raw)


def pack_kernel(*refs):
    own_ref, side_ref, _, cat_ref, pair_ref = refs[-5:]
    per = refs[0].shape[0]
    for i, ref in enumerate(refs[:-5]):
        cat_ref[i * per : (i + 1) * per, :] = ref[...]
    rows = own_ref.shape[0]
    pair_ref[0:rows, :] = own_ref[...]
    pair_ref[rows : 2 * rows, :] = side_ref[...]


def pack(zones, own, side, after):
    rows, columns = zones[0].shape
    return pl.pallas_call(
        pack_kernel,
        out_shape=[
            jax.ShapeDtypeStruct((len(zones) * rows, columns), BF16),
            jax.ShapeDtypeStruct((2 * own.shape[0], columns), BF16),
        ],
        in_specs=[whole()] * (len(zones) + 2) + [whole(pl.ANY)],
        out_specs=[whole()] * 2,
        compiler_params=params(),
        cost_estimate=cost(0, 0),
    )(*zones, own, side, after)


def act_kernel(own_rows, plan, is_b, me_ref, weight_ref, bias_ref, *refs):
    sources = refs[: 1 + max(index for index, *_ in plan) + (not is_b)]
    act_ref, first_ref, last_ref, raw = refs[-4:]
    me = me_ref[0]
    size = act_ref.shape[0] // own_rows
    partner = me + 1 - 2 * lax.rem(me, 2)
    if is_b:
        raw[0:RIM, :] = jnp.zeros((RIM, STATE), BF16)
    else:
        raw[0:RIM, :] = sources[-1][RIM : 2 * RIM, :]
    for index, start, side, shift in plan:
        ref = sources[index]
        owner = lax.rem((partner if side else me) - 2 * shift + size, size)
        at = pl.multiple_of(RIM + owner * own_rows, 16)
        raw[pl.ds(at, own_rows), :] = ref[start : start + own_rows, :]
        if is_b:

            @pl.when(owner == size - 1)
            def _(ref=ref, start=start):
                end = start + own_rows
                last_ref[0:RIM, :] = ref[end - RIM : end, :]
                last_ref[RIM : 2 * RIM, :] = ref[end : end + RIM, :]

    first_ref[...] = raw[RIM : 2 * RIM, :]
    part = slice(0, STATE) if is_b else slice(STATE, 2 * STATE)
    weight = weight_ref[:, part]
    bias = bias_ref[:, part]
    for c in range(act_ref.shape[0] // BLOCK):
        slab = raw[c * BLOCK : c * BLOCK + RIM + BLOCK, :].astype(F32)
        act_ref[c * BLOCK : (c + 1) * BLOCK, :] = conv_slab(slab, weight, bias)


def activate(me, sources, plan, is_b, weight, bias, own_rows, after=()):
    length = len(plan) * own_rows
    return pl.pallas_call(
        functools.partial(act_kernel, own_rows, plan, is_b),
        out_shape=[
            kept_in_vmem((length, STATE), BF16),
            kept_in_vmem((RIM, STATE), BF16),
            kept_in_vmem((2 * RIM, STATE), BF16),
        ],
        in_specs=[whole(pltpu.SMEM)]
        + [whole()] * (len(sources) + 2)
        + [whole(pl.ANY)] * len(after),
        out_specs=[whole()] * 3,
        scratch_shapes=[pltpu.VMEM((RIM + length, STATE), BF16)],
        compiler_params=params(),
        cost_estimate=cost(0, 0),
    )(me, weight, bias, *sources, *after)


def tiles(width):
    step = min(512, width)
    return [slice(i, i + step) for i in range(0, width, step)]


def scale_kernel(x_ref, q_ref, first_ref, later_ref, expand_ref, held, sems):
    copies = stream_in(x_ref, held, sems)
    expander(expand_ref, 1, 0)
    for c, copy in enumerate(copies):
        rows = slice(c * BLOCK, (c + 1) * BLOCK)
        q_block = q_ref[rows, :].astype(BF16)
        copy.wait()
        for columns in tiles(x_ref.shape[1]):
            weight = jnp.dot(q_block, expand_ref[:, columns], preferred_element_type=F32)
            scaled = (held[c, :, columns].astype(F32) * weight).astype(BF16)
            if c == 0:
                first_ref[:, columns] = scaled
            else:
                later_ref[(c - 1) * BLOCK : c * BLOCK, columns] = scaled


def scale(x, q):
    length, width = x.shape
    count = length // BLOCK
    return pl.pallas_call(
        scale_kernel,
        out_shape=[
            kept_in_vmem((BLOCK, width), BF16),
            kept_in_vmem((length - BLOCK, width), BF16),
        ],
        in_specs=[whole(pltpu.HBM), whole()],
        out_specs=[whole()] * 2,
        scratch_shapes=[
            pltpu.VMEM((128, width), BF16),
            pltpu.VMEM((count, BLOCK, width), BF16),
            pltpu.SemaphoreType.DMA((count,)),
        ],
        compiler_params=params(),
        cost_estimate=cost(0, 0),
    )(x, q)


def block_state(b_block, scaled):
    return lax.dot_general(
        b_block, scaled, (((0,), (0,)), ((), ())), preferred_element_type=F32
    )


def later_states_kernel(b_ref, xs_ref, dec_ref, *refs):
    starts_ref, total_ref = refs[-2:]
    for c in range(1, b_ref.shape[0] // BLOCK):
        rows = slice(c * BLOCK, (c + 1) * BLOCK)
        b_block = b_ref[rows, :]
        for columns in tiles(xs_ref.shape[1]):
            state = block_state(b_block, xs_ref[(c - 1) * BLOCK : c * BLOCK, columns])
            if c == 1:
                starts_ref[0, :, columns] = jnp.zeros_like(state).astype(BF16)
                total_ref[:, columns] = state
            else:
                before = total_ref[:, columns]
                starts_ref[c - 1, :, columns] = before.astype(BF16)
                total_ref[:, columns] = dec_ref[c : c + 1, columns] * before + state


def later_states(b_act, xs, dec, after=()):
    length, width = xs.shape
    return pl.pallas_call(
        later_states_kernel,
        out_shape=[
            kept_in_vmem((length // BLOCK, STATE, width), BF16),
            kept_in_vmem((STATE, width), F32),
        ],
        in_specs=[whole()] * 3 + [whole(pl.ANY)] * len(after),
        out_specs=[whole()] * 2,
        compiler_params=params(),
        cost_estimate=cost(0, 0),
    )(b_act, xs, dec, *after)


def first_state_kernel(
    at_ref, b_ref, first_ref, rim_ref, weight_ref, bias_ref, xs_ref, dec_ref, later_ref, *refs
):
    b_out, state_ref, kept_ref, sent_ref, total_ref = refs[-5:]
    slab = jnp.concatenate([rim_ref[0:RIM, :], first_ref[...]], axis=0).astype(F32)
    fixed = conv_slab(slab, weight_ref[:, :STATE], bias_ref[:, :STATE])
    b_block = jnp.concatenate([fixed, b_ref[RIM:BLOCK, :]], axis=0)
    b_out[0:RIM, :] = fixed
    row = 2 * (b_out.shape[0] // BLOCK)
    for columns in tiles(xs_ref.shape[1]):
        state = block_state(b_block, xs_ref[0:BLOCK, columns])
        state_ref[:, columns] = state
        total = later_ref[:, columns] + dec_ref[row : row + 1, columns] * state
        total_ref[:, columns] = total.astype(BF16)
    half = kept_ref.shape[1]
    at = pl.multiple_of(at_ref[1], 128)
    kept_ref[...] = total_ref[:, pl.ds(at, half)]
    sent_ref[...] = total_ref[:, pl.ds(pl.multiple_of(half - at, 128), half)]


def first_state(at, b_act, first, rim, weight, bias, xs, dec, later, after=()):
    width = xs.shape[1]
    return pl.pallas_call(
        first_state_kernel,
        out_shape=[
            kept_in_vmem(b_act.shape, BF16),
            kept_in_vmem((STATE, width), F32),
            kept_in_vmem((STATE, width // 2), BF16),
            kept_in_vmem((STATE, width // 2), BF16),
        ],
        in_specs=[whole(pltpu.SMEM)] + [whole()] * 8 + [whole(pl.ANY)] * len(after),
        out_specs=[whole()] * 4,
        scratch_shapes=[pltpu.VMEM((STATE, width), BF16)],
        input_output_aliases={1: 0},
        compiler_params=params(),
        cost_estimate=cost(0, 0),
    )(at, b_act, first, rim, weight, bias, xs, dec, later, *after)


def meet_kernel(at_ref, kept_ref, got_ref, own_ref, partner_ref, out_ref):
    half = kept_ref.shape[1]
    columns = pl.ds(pl.multiple_of(at_ref[1], 128), half)
    odd = at_ref[1] == 0
    kept_decay = jnp.where(odd, 1.0, partner_ref[:, columns])
    got_decay = jnp.where(odd, own_ref[:, columns], 1.0)
    both = kept_decay * kept_ref[...].astype(F32) + got_decay * got_ref[...].astype(F32)
    out_ref[...] = both.astype(BF16)


def meet(at, kept, got, own, partner):
    return pl.pallas_call(
        meet_kernel,
        out_shape=kept_in_vmem(kept.shape, BF16),
        in_specs=[whole(pltpu.SMEM)] + [whole()] * 4,
        out_specs=whole(),
        compiler_params=params(),
        cost_estimate=cost(0, 0),
    )(at, kept, got, own, partner)


def arrive_kernel(at_ref, crossed_ref, kept_ref, got_ref, own_ref, partner_ref, *refs):
    in_ref, sent_ref = refs[-2:]
    half = kept_ref.shape[1]
    columns = pl.ds(pl.multiple_of(at_ref[1], 128), half)
    odd = at_ref[1] == 0
    decay = jnp.where(odd, partner_ref[:, columns], own_ref[:, columns])
    crossed = crossed_ref[...]
    mine = jnp.where(odd, got_ref[...].astype(F32), kept_ref[...].astype(F32))
    after_even = (decay * crossed.astype(F32) + mine).astype(BF16)
    in_ref[...] = jnp.where(odd, after_even, crossed)
    sent_ref[...] = jnp.where(odd, crossed, after_even)


def arrive(at, crossed, kept, got, own, partner, after):
    return pl.pallas_call(
        arrive_kernel,
        out_shape=[kept_in_vmem(kept.shape, BF16)] * 2,
        in_specs=[whole(pltpu.SMEM)] + [whole()] * 5 + [whole(pl.ANY)],
        out_specs=[whole()] * 2,
        compiler_params=params(),
        cost_estimate=cost(0, 0),
    )(at, crossed, kept, got, own, partner, after)


def inner_kernel(
    c_ref, b_ref, x_ref, q_ref, brow_ref, starts_ref, state_ref, dec_ref,
    out_ref, expand_ref, held, sems,
):
    stream_in(x_ref, held, sems)
    half = BLOCK // 2
    block_count = x_ref.shape[0] // BLOCK
    head_count = x_ref.shape[1] // HEAD_DIM
    expander(expand_ref, 3, 0)
    lower = lax.broadcasted_iota(jnp.int32, (half, half), 0) >= lax.broadcasted_iota(
        jnp.int32, (half, half), 1
    )

    @pl.loop(0, block_count)
    def _(c):
        at = pl.multiple_of(c * BLOCK, BLOCK)
        rows = pl.ds(at, BLOCK)
        pltpu.make_async_copy(x_ref.at[rows, :], held.at[c], sems.at[c]).wait()
        c_block = c_ref[rows, :]
        gram = lax.dot_general(
            c_block, b_ref[rows, :], (((1,), (1,)), ((), ())), preferred_element_type=F32
        )
        gram_00 = jnp.where(lower, gram[:half, :half], 0.0)
        gram_10 = gram[half:, :half]
        gram_11 = jnp.where(lower, gram[half:, half:], 0.0)
        q_block = q_ref[rows, :]
        q_short = q_block.astype(BF16)
        for h in range(head_count):
            columns = slice(h * HEAD_DIM, (h + 1) * HEAD_DIM)
            rise = jnp.broadcast_to(q_block[:, h : h + 1], (BLOCK, half))
            fall = brow_ref[h : h + 1, rows]
            w_00 = gram_00 * jnp.exp2(jnp.minimum(rise[:half] - fall[:, :half], 120.0))
            w_10 = gram_10 * jnp.exp2(rise[half:] - fall[:, :half])
            w_11 = gram_11 * jnp.exp2(jnp.minimum(rise[half:] - fall[:, half:], 120.0))
            x_head = held[c, :, columns]
            top = jnp.dot(w_00.astype(BF16), x_head[:half], preferred_element_type=F32)
            low = jnp.concatenate([w_10.astype(BF16), w_11.astype(BF16)], axis=1)
            bottom = jnp.dot(low, x_head, preferred_element_type=F32)
            out_ref[rows, columns] = jnp.concatenate([top, bottom], axis=0) + dec_ref[
                2 * block_count + 1 : 2 * block_count + 2, columns
            ] * x_head.astype(F32)

        @pl.when(c > 0)
        def _():
            for columns in tiles(x_ref.shape[1]):
                decay = dec_ref[pl.ds(block_count + c, 1), columns]
                start = starts_ref[c - 1, :, columns].astype(F32) + decay * state_ref[:, columns]
                grown = jnp.dot(q_short, expand_ref[:, columns], preferred_element_type=F32)
                carried = jnp.dot(c_block, start.astype(BF16), preferred_element_type=F32)
                out_ref[rows, columns] += grown * carried


def inner(c_act, b_act, x, q, brow, starts, state, dec):
    length, width = x.shape
    return pl.pallas_call(
        inner_kernel,
        out_shape=kept_in_vmem((length, width), F32),
        in_specs=[whole()] * 2 + [whole(pltpu.HBM)] + [whole()] * 5,
        out_specs=whole(),
        scratch_shapes=[
            pltpu.VMEM((128, width), BF16),
            pltpu.VMEM((length // BLOCK, BLOCK, width), BF16),
            pltpu.SemaphoreType.DMA((length // BLOCK,)),
        ],
        compiler_params=params(),
        cost_estimate=cost(0, 13 * length * width),
    )(c_act, b_act, x, q, brow, starts, state, dec)


def gate_kernel(second, at_ref, c_ref, y_ref, z_ref, q_ref, in_ref, *refs):
    out_ref, sum_ref, expand_ref, held, sems = refs[-5:]
    width = in_ref.shape[1]
    base = pl.multiple_of(width - at_ref[1] if second else at_ref[1], 128)
    stream_in(z_ref, held, sems, pl.ds(base, width))
    expander(expand_ref, 5, base)

    @pl.loop(0, y_ref.shape[0] // BLOCK)
    def _(c):
        rows = pl.ds(pl.multiple_of(c * BLOCK, BLOCK), BLOCK)
        pltpu.make_async_copy(z_ref.at[rows, pl.ds(base, width)], held.at[c], sems.at[c]).wait()
        c_block = c_ref[rows, :]
        q_short = q_ref[rows, :].astype(BF16)
        squares = jnp.zeros((BLOCK, 128), F32)
        for part in tiles(width):
            size = part.stop - part.start
            columns = pl.ds(pl.multiple_of(base + part.start, 128), size)
            grown = jnp.dot(q_short, expand_ref[:, part], preferred_element_type=F32)
            carried = jnp.dot(c_block, in_ref[:, part], preferred_element_type=F32)
            gated = (y_ref[rows, columns] + grown * carried) * silu(held[c, :, part].astype(F32))
            out_ref[rows, columns] = gated
            square = gated * gated
            for i in range(0, size, 128):
                squares = squares + square[:, i : i + 128]
        total = lax.dot_general(
            jnp.ones((8, 128), F32), squares, (((1,), (1,)), ((), ())),
            precision=HIGHEST, preferred_element_type=F32,
        )[0:1]
        sum_ref[:, rows] = refs[0][:, rows] + total if second else total


def gate(at, c_act, y, z, q, incoming, *before):
    length, width = y.shape
    return pl.pallas_call(
        functools.partial(gate_kernel, len(before) > 0),
        out_shape=[
            kept_in_vmem((length, width), F32),
            kept_in_vmem((1, length), F32),
        ],
        in_specs=[whole(pltpu.SMEM)]
        + [whole()] * 2
        + [whole(pltpu.HBM)]
        + [whole()] * (2 + len(before)),
        out_specs=[whole()] * 2,
        scratch_shapes=[
            pltpu.VMEM((128, incoming.shape[1]), BF16),
            pltpu.VMEM((length // BLOCK, BLOCK, incoming.shape[1]), BF16),
            pltpu.SemaphoreType.DMA((length // BLOCK,)),
        ],
        input_output_aliases={2: 0},
        compiler_params=params(),
        cost_estimate=cost(0, 8 * length * width),
    )(at, c_act, y, z, q, incoming, *before)


def norm_kernel(g_ref, one_ref, two_ref, gain_ref, out_ref, held, sems):
    copies = []
    for c in range(g_ref.shape[0] // BLOCK):
        rows = slice(c * BLOCK, (c + 1) * BLOCK)
        square_sum = one_ref[:, rows] + two_ref[:, rows]
        inverse = lax.rsqrt(square_sum / INNER + 1e-05)
        scale = jnp.broadcast_to(inverse, (128, BLOCK)).T
        for i in range(0, g_ref.shape[1], 128):
            columns = slice(i, i + 128)
            held[c, :, columns] = (g_ref[rows, columns] * scale * gain_ref[:, columns]).astype(BF16)
        copy = pltpu.make_async_copy(held.at[c], out_ref.at[rows, :], sems.at[c])
        copy.start()
        copies.append(copy)
    for copy in copies:
        copy.wait()


def norm(gated, one, two, gain):
    length, width = gated.shape
    count = length // BLOCK
    return pl.pallas_call(
        norm_kernel,
        out_shape=jax.ShapeDtypeStruct((length, width), BF16),
        in_specs=[whole()] * 4,
        out_specs=whole(pltpu.HBM),
        scratch_shapes=[
            pltpu.VMEM((count, BLOCK, width), BF16),
            pltpu.SemaphoreType.DMA((count,)),
        ],
        compiler_params=params(),
        cost_estimate=cost(0, 0),
    )(gated, one, two, gain)


SWAP = [(0, 1), (1, 0), (2, 3), (3, 2)]


def zone_shift(a, k):
    size = lax.axis_size("head")
    return lax.ppermute(a, "head", [(i, (i + 2 * k) % size) for i in range(size)])


def side_swap(a):
    size = lax.axis_size("head")
    return lax.ppermute(a, "head", [(i, i ^ 1) for i in range(size)])


def chained_state(at, kept, sent, own, partner, after):
    size = lax.axis_size("seq")
    if size == 4:
        got = lax.ppermute(sent, "seq", SWAP)
        both = meet(at, kept, got, own, partner)
        crossed = lax.ppermute(both, "seq", [(0, 2), (1, 3)])
        mine, passed = arrive(at, crossed, kept, got, own, partner, after)
        return mine, lax.ppermute(passed, "seq", SWAP)
    totals = lax.all_gather(jnp.concatenate([kept, sent], axis=1), "seq")
    decays = lax.all_gather(own, "seq")

    def one(hop, state):
        decay = lax.dynamic_index_in_dim(decays, hop, 0, False)
        return decay * state + lax.dynamic_index_in_dim(totals, hop, 0, False).astype(F32)

    place = lax.axis_index("seq")
    state = lax.fori_loop(0, place, one, jnp.zeros(totals.shape[1:], F32)).astype(BF16)
    half = kept.shape[1]
    return state[:, :half], state[:, half:]


def on_device(x_inner, z_gate, bc_raw, conv_weight, conv_bias, dt_raw, a_log, d_skip, norm_gain):
    x_inner, z_gate = in_hbm(x_inner), in_hbm(z_gate)
    head_count = a_log.shape[0]
    own_rows = bc_raw.shape[0]
    seq_size = lax.axis_size("seq")
    shifts = range(1, lax.axis_size("head") // 2)
    width = x_inner.shape[1]
    first_channel = 0
    if seq_size == 4:
        first_channel = (1 - lax.rem(lax.axis_index("seq"), 2)) * (width // 2)
    place = jnp.stack([lax.axis_index("head"), first_channel]).astype(jnp.int32)
    own_b, own_c, place = prepare(place, bc_raw)
    zones_b = [zone_shift(own_b, k) for k in shifts]
    side_b = side_swap(own_b)
    side_c = side_swap(own_c)
    pad = SLOT - head_count
    q, brow, dec, own_decay = rates(
        jnp.pad(dt_raw.T, ((0, pad), (0, 0))),
        jnp.pad(a_log, (0, pad))[None, :],
        jnp.pad(d_skip, (0, pad))[None, :],
        width,
    )
    cat_b, pair_c = pack(zones_b, own_c, side_c, own_decay)
    others_b = side_swap(cat_b)
    pairs_c = [zone_shift(pair_c, k) for k in shifts]
    sources_b = [own_b, side_b, *zones_b, others_b]
    plan_b = [(0, 0, False, 0), (1, 0, True, 0)]
    plan_b += [(k + 1, 0, False, k) for k in shifts]
    plan_b += [(len(zones_b) + 2, (k - 1) * own_b.shape[0], True, k) for k in shifts]
    sources_c = [pair_c, *pairs_c]
    plan_c = [(k, 0, False, k) for k in range(len(sources_c))]
    plan_c += [(k, own_rows, True, k) for k in range(len(sources_c))]

    bias = conv_bias[None, :]
    xs_first, xs_later = scale(x_inner, q)
    partner_decay = own_decay
    if seq_size == 4:
        partner_decay = lax.ppermute(own_decay, "seq", SWAP)
    b_act, first_b, last_rows = activate(
        place, sources_b, plan_b, True, conv_weight, bias, own_rows, [xs_first, pairs_c[0]]
    )
    rims = lax.ppermute(last_rows, "seq", [(i, i + 1) for i in range(seq_size - 1)])
    starts, later = later_states(b_act, xs_later, dec, [pairs_c[1]])
    b_act, state_0, kept, sent = first_state(
        place, b_act, first_b, rims, conv_weight, bias, xs_first, dec, later, [pairs_c[2]]
    )
    c_act, _, _ = activate(place, [*sources_c, rims], plan_c, False, conv_weight, bias, own_rows)
    local = inner(c_act, b_act, x_inner, q, brow, starts, state_0, dec)
    state_one, state_two = chained_state(place, kept, sent, own_decay, partner_decay, local)
    gated, square_one = gate(place, c_act, local, z_gate, q, state_one)
    gated, square_sum = gate(place, c_act, gated, z_gate, q, state_two, square_one)
    column = sum([zone_shift(square_sum, k) for k in shifts], square_sum)
    return norm(gated, column, side_swap(column), norm_gain[None, :])


def solution(mesh):
    placed = (
        P("seq", "head"),
        P("seq", "head"),
        P(("seq", "head"), None),
        P(),
        P(),
        P("seq", "head"),
        P("head"),
        P("head"),
        P("head"),
    )
    return jax.shard_map(
        on_device, mesh=mesh, in_specs=placed, out_specs=P("seq", "head"), check_vma=False
    )
```

time: 243 us -> 88.1 us (0.36)
  matrix products: 64 us -> 0 us
  waiting for transfers between devices: 58.4 us -> 15.8 us
  Pallas kernels: 0 us -> 39.6 us
  other arithmetic: 36.2 us -> 0.09 us
  local copies, waits for them, and re-layouts: 35 us -> 3.14 us
  blocking collectives: 27.7 us -> 0 us
  starting transfers between devices: 4.9 us -> 28.9 us
  between operations: 14.4 us -> 0.35 us
    dot_general x5 -> x0, matrix products: 64 us -> none  [the longest x1 21.9 us: on_device(): jnp.einsum('chij,cjhp->cihp', weights, x_float, precision=highest)]
    all_gather x2 -> x0, waiting for transfers between devices: 57.9 us -> none  [the longest x1 30.9 us: on_device(): bc_act = lax.all_gather(own_act, 'head', axis=0, tiled=True)]
    pallas_call x0 -> x14, Pallas kernels: none -> 39.6 us  [the longest x2 13.4 us: gate(): pl.pallas_call(functools.partial(gate_kernel, len(before) > 0), out_shape...]
    ppermute x1 -> x18, starting transfers between devices: 4.86 us -> 28.9 us  [the longest x9 19.2 us: zone_shift(): lax.ppermute(a, 'head', [(i, (i + 2 * k) % size) for i in range(size)])]
    psum x1 -> x0, blocking collectives: 21.6 us -> none  [on_device(): square_sum = lax.psum(jnp.sum(gated_out * gated_out, axis=1), 'head')]
    add x1 -> x0, local copies, waits for them, and re-layouts: 16.3 us -> none  [on_device(): ssm_out = inner_part + carried_part + d_skip[None, None, :, None] * x_float]
    convert_element_type x3 -> x0, other arithmetic: 16 us -> none  [the longest x1 13.4 us: on_device(): (gated_out * inverse_rms[:, None] * norm_gain[None, :]).astype(jnp.bfloat16)]
    ppermute x1 -> x18, waiting for transfers between devices: 0.45 us -> 15.8 us  [the longest x9 10.9 us: zone_shift(): lax.ppermute(a, 'head', [(i, (i + 2 * k) % size) for i in range(size)])]
  transfers between devices with their start and end apart: 3 -> 18, of which waited for: 3 -> 7; matrix products, arithmetic and copies ran while one was open for 16% -> 0% of each run, Pallas kernels for 0% -> 32%
where the time goes in v2:
time: 88.1 us; the launch traced here: 87.9 us
  Pallas kernels  39.6 us (45%)
  starting transfers between devices  28.9 us (33%)
  waiting for transfers between devices  15.8 us (18%)
  local copies, waits for them, and re-layouts  3.14 us (4%)
    ppermute x9, starting transfers between devices, zone_shift(): lax.ppermute(a, 'head', [(i, (i + 2 * k) % size) for i in range(size)])  19.2 us
    pallas_call x2, Pallas kernels, gate(): pl.pallas_call(functools.partial(gate_kernel, len(before) > 0), out_shape...  13.4 us
    pallas_call x1, Pallas kernels, inner(): pl.pallas_call(inner_kernel, out_shape=kept_in_vmem((length, width), F32)...  11.7 us
    ppermute x9, waiting for transfers between devices, zone_shift(): lax.ppermute(a, 'head', [(i, (i + 2 * k) % size) for i in range(size)])  10.9 us
    ppermute x4, starting transfers between devices, side_swap(): return lax.ppermute(a, 'head', [(i, i ^ 1) for i in range(size)])  4.18 us
    pallas_call x1, Pallas kernels, scale(): pl.pallas_call(scale_kernel, out_shape=[kept_in_vmem((BLOCK, width), BF16...  3.77 us
    ppermute x1, starting transfers between devices, chained_state(): crossed = lax.ppermute(both, 'seq', [(0, 2), (1, 3)])  3.61 us
    ppermute x4, waiting for transfers between devices, side_swap(): return lax.ppermute(a, 'head', [(i, i ^ 1) for i in range(size)])  3.55 us
  transfers between devices with their start and end apart: 18, of which 7 were waited for; matrix products, arithmetic and copies ran while one was open for 0% of the time, Pallas kernels for 32%

profile of v2, /device:TPU:0, one launch (start us, length us, event | category | flops | bytes accessed | tf_op | source)
XLA Modules:
  0.0 87.9 jit_solution(17496050484805476567)
XLA Ops:
  1.6 5.1 %collective-permute-start.2 = (bf16[208,256]{1,0:T(8,128)(2,1)S(1)}, bf16[208,256]{1,0:T(8,128)(2,1)S(1)}, u32[]{:S(2)}, u32[]{:S(2)}) collective-permute-start(bf16[208,256]{1,0:T(8,128)(2,1)S(1)} %get-tuple-element.33.refs_0_), channel_id=1, source_target_pairs={{0,6},{1,7},{2,0},{3,1},{4,2},{5,3},{6,4},{7,5},{8,14},{9,15},{10,... | collective-permute-start | bytes 319496 | tf_op jit(solution)/shard_map/ppermute | solution.py:576
  7.7 1.5 %collective-permute-start.3 = (bf16[192,256]{1,0:T(8,128)(2,1)S(1)}, bf16[192,256]{1,0:T(8,128)(2,1)S(1)}, u32[]{:S(2)}, u32[]{:S(2)}) collective-permute-start(bf16[192,256]{1,0:T(8,128)(2,1)S(1)} %get-tuple-element.34.refs_3_), channel_id=1, source_target_pairs={{0,1},{1,0},{2,3},{3,2},{4,5},{5,4},{6,7},{7,6},{8,9},{9,8},{10,11... | collective-permute-start | bytes 294920 | tf_op jit(solution)/shard_map/ppermute | solution.py:581
  11.4 1.2 %shard_map.92 = (f32[1536,128]{1,0:T(8,128)S(1)}, f32[16,1536]{1,0:T(8,128)S(1)}, f32[16,2048]{1,0:T(8,128)S(1)}, f32[1,2048]{1,0:T(1,128)S(1)}) custom-call(f32[16,1536]{1,0:T(8,128)S(1)} %bitcast.7, f32[1,16]{1,0:T(1,128)S(1)} %bitcast.12, f32[1,16]{1,0:T(1,128)S(1)} %bitcast.13), custom_call_target="tpu_custom_call" | custom-call | tf_op jit(solution)/shard_map/pallas_call | solution.py:128
  12.7 3.4 %collective-permute-done.1.refs_1_.refs_3_ = bf16[208,256]{1,0:T(8,128)(2,1)S(1)} collective-permute-done((bf16[208,256]{1,0:T(8,128)(2,1)S(1)}, bf16[208,256]{1,0:T(8,128)(2,1)S(1)}, u32[]{:S(2)}, u32[]{:S(2)}) %collective-permute-start.1) | collective-permute-done | bytes 106528 | tf_op jit(solution)/shard_map/ppermute | solution.py:576
  16.1 1.6 %collective-permute-start.8 = (bf16[624,256]{1,0:T(8,128)(2,1)S(1)}, bf16[624,256]{1,0:T(8,128)(2,1)S(1)}, u32[]{:S(2)}, u32[]{:S(2)}) collective-permute-start(bf16[624,256]{1,0:T(8,128)(2,1)S(1)} %get-tuple-element.37), channel_id=1, source_target_pairs={{0,1},{1,0},{2,3},{3,2},{4,5},{5,4},{6,7},{7,6},{8,9},{9,8},{10,11... | collective-permute-start | bytes 958472 | tf_op jit(solution)/shard_map/ppermute | solution.py:581
  18.1 2.0 %collective-permute-start.5 = (bf16[384,256]{1,0:T(8,128)(2,1)S(1)}, bf16[384,256]{1,0:T(8,128)(2,1)S(1)}, u32[]{:S(2)}, u32[]{:S(2)}) collective-permute-start(bf16[384,256]{1,0:T(8,128)(2,1)S(1)} %get-tuple-element.36.refs_0_), channel_id=1, source_target_pairs={{0,4},{1,5},{2,6},{3,7},{4,0},{5,1},{6,2},{7,3},{8,12},{9,13},{10,... | collective-permute-start | bytes 589832 | tf_op jit(solution)/shard_map/ppermute | solution.py:576
  20.1 2.9 %collective-permute-start.6 = (bf16[384,256]{1,0:T(8,128)(2,1)S(1)}, bf16[384,256]{1,0:T(8,128)(2,1)S(1)}, u32[]{:S(2)}, u32[]{:S(2)}) collective-permute-start(bf16[384,256]{1,0:T(8,128)(2,1)S(1)} %get-tuple-element.36.refs_0_), channel_id=1, source_target_pairs={{0,6},{1,7},{2,0},{3,1},{4,2},{5,3},{6,4},{7,5},{8,14},{9,15},{10,... | collective-permute-start | bytes 589832 | tf_op jit(solution)/shard_map/ppermute | solution.py:576
  23.5 3.8 %shard_map.94 = (bf16[256,2048]{1,0:T(8,128)(2,1)S(1)}, bf16[1280,2048]{1,0:T(8,128)(2,1)S(1)}) custom-call(bf16[1536,2048]{1,0:T(8,128)(2,1)} %x_ref.3, f32[1536,128]{1,0:T(8,128)S(1)} %get-tuple-element.38.q_ref), custom_call_target="tpu_custom_call" | custom-call | tf_op jit(solution)/shard_map/pallas_call | solution.py:274
  27.7 1.1 %shard_map.95 = (bf16[1536,256]{1,0:T(8,128)(2,1)S(1)}, bf16[16,256]{1,0:T(8,128)(2,1)S(1)}, bf16[32,256]{1,0:T(8,128)(2,1)S(1)}) custom-call(s32[2]{0:T(128)S(4)} %get-tuple-element.32.me_ref.at_ref, f32[4,512]{1,0:T(4,128)S(1)} %copy-done.2, f32[1,512]{1,0:T(1,128)S(1)} %bitcast.8, bf16[208,256]{1,0:T(8,128)(2,1)S(1)} %get-tuple-element.33.refs_0_, ...), custom_call_target="tpu_custom_call" | custom-call | tf_op jit(solution)/shard_map/pallas_call | solution.py:233
  28.7 1.3 %collective-permute-start.9 = (bf16[32,256]{1,0:T(8,128)(2,1)S(1)}, bf16[32,256]{1,0:T(8,128)(2,1)S(1)}, u32[]{:S(2)}, u32[]{:S(2)}) collective-permute-start(bf16[32,256]{1,0:T(8,128)(2,1)S(1)} %get-tuple-element.40), channel_id=1, source_target_pairs={{0,8},{8,16},{16,24},{1,9},{9,17},{17,25},{2,10},{10,18},{18,26},{... | collective-permute-start | bytes 49160 | tf_op jit(solution)/shard_map/ppermute | solution.py:646
  30.0 4.0 %collective-permute-done.5.refs_2_.refs_0_ = bf16[384,256]{1,0:T(8,128)(2,1)S(1)} collective-permute-done((bf16[384,256]{1,0:T(8,128)(2,1)S(1)}, bf16[384,256]{1,0:T(8,128)(2,1)S(1)}, u32[]{:S(2)}, u32[]{:S(2)}) %collective-permute-start.5) | collective-permute-done | bytes 196640 | tf_op jit(solution)/shard_map/ppermute | solution.py:576
  34.1 2.2 %shard_map.97 = (bf16[5,256,2048]{2,1,0:T(8,128)(2,1)S(1)}, f32[256,2048]{1,0:T(8,128)S(1)}) custom-call(bf16[1536,256]{1,0:T(8,128)(2,1)S(1)} %get-tuple-element.42.b_ref, bf16[1280,2048]{1,0:T(8,128)(2,1)S(1)} %get-tuple-element.45.xs_ref, f32[16,2048]{1,0:T(8,128)S(1)} %get-tuple-element.44.dec_ref, ...), custom_call_target="tpu_custom_call" | custom-call | tf_op jit(solution)/shard_map/pallas_call | solution.py:316
  37.4 1.4 %collective-permute-done.11.partner_ref = f32[1,2048]{1,0:T(1,128)S(1)} collective-permute-done((f32[1,2048]{1,0:T(1,128)S(1)}, f32[1,2048]{1,0:T(1,128)S(1)}, u32[]{:S(2)}, u32[]{:S(2)}) %collective-permute-start.11) | collective-permute-done | bytes 8224 | tf_op jit(solution)/shard_map/ppermute | solution.py:642
  39.0 3.6 %collective-permute-start.12 = (bf16[256,1024]{1,0:T(8,128)(2,1)S(1)}, bf16[256,1024]{1,0:T(8,128)(2,1)S(1)}, u32[]{:S(2)}, u32[]{:S(2)}) collective-permute-start(bf16[256,1024]{1,0:T(8,128)(2,1)S(1)} %shard_map.100), channel_id=1, source_target_pairs={{0,16},{8,24},{1,17},{9,25},{2,18},{10,26},{3,19},{11,27},{4,20},{... | collective-permute-start | bytes 1572872 | tf_op jit(solution)/shard_map/ppermute | solution.py:589
  42.7 1.4 %shard_map.96 = (bf16[1536,256]{1,0:T(8,128)(2,1)S(1)}, bf16[16,256]{1,0:T(8,128)(2,1)}, bf16[32,256]{1,0:T(8,128)(2,1)}) custom-call(s32[2]{0:T(128)S(4)} %get-tuple-element.32.me_ref.at_ref, f32[4,512]{1,0:T(4,128)S(1)} %copy-done.2, f32[1,512]{1,0:T(1,128)S(1)} %bitcast.10, bf16[384,256]{1,0:T(8,128)(2,1)S(1)} %get-tuple-element.36.refs_0_, ...), custom_call_target="tpu_custom_call" | custom-call | tf_op jit(solution)/shard_map/pallas_call | solution.py:233
  44.1 11.7 %shard_map.99.refs_0_.y_ref = f32[1536,2048]{1,0:T(8,128)S(1)} custom-call(bf16[1536,256]{1,0:T(8,128)(2,1)S(1)} %get-tuple-element.41.c_ref, bf16[1536,256]{1,0:T(8,128)(2,1)S(1)} %get-tuple-element.47.b_ref, bf16[1536,2048]{1,0:T(8,128)(2,1)} %x_ref.3, f32[1536,128]{1,0:T(8,128)S(1)} %get-tuple-element.38.q_ref, ...), custom_call_target="tpu_custom_call" | custom-call | bytes 40894464 | tf_op jit(solution)/shard_map/pallas_call | solution.py:467
  56.3 6.7 %shard_map.102 = (f32[1536,2048]{1,0:T(8,128)S(1)}, f32[1,1536]{1,0:T(1,128)S(1)}) custom-call(s32[2]{0:T(128)S(4)} %get-tuple-element.32.me_ref.at_ref, bf16[1536,256]{1,0:T(8,128)(2,1)S(1)} %get-tuple-element.41.c_ref, f32[1536,2048]{1,0:T(8,128)S(1)} %shard_map.99.refs_0_.y_ref, bf16[1536,2048]{1,0:T(8,128)(2,1)} %z_ref.3, ...), custom_call_target="tpu_custom_call", output_to_operand_aliasing={{0}: (2, {})} | custom-call | bytes 25165824 | tf_op jit(solution)/shard_map/pallas_call | solution.py:515
  63.0 6.7 %shard_map.103 = (f32[1536,2048]{1,0:T(8,128)S(1)}, f32[1,1536]{1,0:T(1,128)S(1)}) custom-call(s32[2]{0:T(128)S(4)} %get-tuple-element.32.me_ref.at_ref, bf16[1536,256]{1,0:T(8,128)(2,1)S(1)} %get-tuple-element.41.c_ref, f32[1536,2048]{1,0:T(8,128)S(1)} %get-tuple-element.54.y_ref, bf16[1536,2048]{1,0:T(8,128)(2,1)} %z_ref.3, ...), custom_call_target="tpu_custom_call", output_to_operand_aliasing={{0}: (2, {})} | custom-call | bytes 25165824 | tf_op jit(solution)/shard_map/pallas_call | solution.py:515
  69.7 5.3 %collective-permute-start.16 = (f32[1,1536]{1,0:T(1,128)S(1)}, f32[1,1536]{1,0:T(1,128)S(1)}, u32[]{:S(2)}, u32[]{:S(2)}) collective-permute-start(f32[1,1536]{1,0:T(1,128)S(1)} %get-tuple-element.58), channel_id=1, source_target_pairs={{0,6},{1,7},{2,0},{3,1},{4,2},{5,3},{6,4},{7,5},{8,14},{9,15},{10,... | collective-permute-start | bytes 18440 | tf_op jit(solution)/shard_map/ppermute | solution.py:576
  75.6 1.9 %collective-permute-start.14 = (f32[1,1536]{1,0:T(1,128)S(1)}, f32[1,1536]{1,0:T(1,128)S(1)}, u32[]{:S(2)}, u32[]{:S(2)}) collective-permute-start(f32[1,1536]{1,0:T(1,128)S(1)} %get-tuple-element.58), channel_id=1, source_target_pairs={{0,2},{1,3},{2,4},{3,5},{4,6},{5,7},{6,0},{7,1},{8,10},{9,11},{10,... | collective-permute-start | bytes 18440 | tf_op jit(solution)/shard_map/ppermute | solution.py:576
  77.5 2.1 %collective-permute-done.15 = f32[1,1536]{1,0:T(1,128)S(1)} collective-permute-done((f32[1,1536]{1,0:T(1,128)S(1)}, f32[1,1536]{1,0:T(1,128)S(1)}, u32[]{:S(2)}, u32[]{:S(2)}) %collective-permute-start.15) | collective-permute-done | bytes 6176 | tf_op jit(solution)/shard_map/ppermute | solution.py:576
  79.6 1.4 %collective-permute-done.14 = f32[1,1536]{1,0:T(1,128)S(1)} collective-permute-done((f32[1,1536]{1,0:T(1,128)S(1)}, f32[1,1536]{1,0:T(1,128)S(1)}, u32[]{:S(2)}, u32[]{:S(2)}) %collective-permute-start.14) | collective-permute-done | bytes 6176 | tf_op jit(solution)/shard_map/ppermute | solution.py:576
  81.6 3.1 %collective-permute-done.17.two_ref = f32[1,1536]{1,0:T(1,128)S(1)} collective-permute-done((f32[1,1536]{1,0:T(1,128)S(1)}, f32[1,1536]{1,0:T(1,128)S(1)}, u32[]{:S(2)}, u32[]{:S(2)}) %collective-permute-start.17) | collective-permute-done | bytes 6176 | tf_op jit(solution)/shard_map/ppermute | solution.py:581
  84.7 3.0 %shard_map.104 = bf16[1536,2048]{1,0:T(8,128)(2,1)} custom-call(f32[1536,2048]{1,0:T(8,128)S(1)} %get-tuple-element.57.g_ref, f32[1,1536]{1,0:T(1,128)S(1)} %add_add_fusion.one_ref, f32[1,1536]{1,0:T(1,128)S(1)} %collective-permute-done.17.two_ref, f32[1,2048]{1,0:T(1,128)S(1)} %bitcast.11), custom_call_target="tpu_custom_call" | custom-call | tf_op jit(solution)/shard_map/pallas_call | solution.py:557
  (42 shorter events, 9.1 us)
Async XLA Ops:
  0.0 27.7 %copy-start.2 = (f32[4,512]{1,0:T(4,128)S(1)}, f32[4,512]{1,0:T(4,128)}, u32[]{:S(2)}) copy-start(f32[4,512]{1,0:T(4,128)} %weight_ref.5) | copy-start | bytes 24580
  0.0 27.7 %copy-start.3 = (f32[512]{0:T(512)S(1)}, f32[512]{0:T(512)}, u32[]{:S(2)}) copy-start(f32[512]{0:T(512)} %param.13) | copy-start | bytes 6148
  0.1 0.9 %copy-start = (bf16[192,512]{1,0:T(8,128)(2,1)S(1)}, bf16[192,512]{1,0:T(8,128)(2,1)}, u32[]{:S(2)}) copy-start(bf16[192,512]{1,0:T(8,128)(2,1)} %bc_ref.1) | copy-start | bytes 589828
  1.6 11.1 %collective-permute-start.2 = (bf16[208,256]{1,0:T(8,128)(2,1)S(1)}, bf16[208,256]{1,0:T(8,128)(2,1)S(1)}, u32[]{:S(2)}, u32[]{:S(2)}) collective-permute-start(bf16[208,256]{1,0:T(8,128)(2,1)S(1)} %get-tuple-element.33.refs_0_), channel_id=1, source_target_pairs={{0,6},{1,7},{2,0},{3,1},{4,2},{5,3},{6,4},{7,5},{8,14},{9,15},{10,... | collective-permute-start | bytes 319496 | tf_op jit(solution)/shard_map/ppermute | solution.py:576
  6.7 9.4 %collective-permute-start.1 = (bf16[208,256]{1,0:T(8,128)(2,1)S(1)}, bf16[208,256]{1,0:T(8,128)(2,1)S(1)}, u32[]{:S(2)}, u32[]{:S(2)}) collective-permute-start(bf16[208,256]{1,0:T(8,128)(2,1)S(1)} %get-tuple-element.33.refs_0_), channel_id=1, source_target_pairs={{0,4},{1,5},{2,6},{3,7},{4,0},{5,1},{6,2},{7,3},{8,12},{9,13},{10,... | collective-permute-start | bytes 319496 | tf_op jit(solution)/shard_map/ppermute | solution.py:576
  6.7 9.4 %collective-permute-start = (bf16[208,256]{1,0:T(8,128)(2,1)S(1)}, bf16[208,256]{1,0:T(8,128)(2,1)S(1)}, u32[]{:S(2)}, u32[]{:S(2)}) collective-permute-start(bf16[208,256]{1,0:T(8,128)(2,1)S(1)} %get-tuple-element.33.refs_0_), channel_id=1, source_target_pairs={{0,2},{1,3},{2,4},{3,5},{4,6},{5,7},{6,0},{7,1},{8,10},{9,11},{10,... | collective-permute-start | bytes 319496 | tf_op jit(solution)/shard_map/ppermute | solution.py:576
  7.7 5.0 %collective-permute-start.3 = (bf16[192,256]{1,0:T(8,128)(2,1)S(1)}, bf16[192,256]{1,0:T(8,128)(2,1)S(1)}, u32[]{:S(2)}, u32[]{:S(2)}) collective-permute-start(bf16[192,256]{1,0:T(8,128)(2,1)S(1)} %get-tuple-element.34.refs_3_), channel_id=1, source_target_pairs={{0,1},{1,0},{2,3},{3,2},{4,5},{5,4},{6,7},{7,6},{8,9},{9,8},{10,11... | collective-permute-start | bytes 294920 | tf_op jit(solution)/shard_map/ppermute | solution.py:581
  9.2 0.9 %copy-start.1 = (f32[1536,16]{0,1:T(8,128)S(1)}, f32[1536,16]{0,1:T(8,128)}, u32[]{:S(2)}) copy-start(f32[1536,16]{0,1:T(8,128)} %param.14) | copy-start | bytes 294916
  10.1 0.7 copy-start.5
  16.1 11.6 %collective-permute-start.8 = (bf16[624,256]{1,0:T(8,128)(2,1)S(1)}, bf16[624,256]{1,0:T(8,128)(2,1)S(1)}, u32[]{:S(2)}, u32[]{:S(2)}) collective-permute-start(bf16[624,256]{1,0:T(8,128)(2,1)S(1)} %get-tuple-element.37), channel_id=1, source_target_pairs={{0,1},{1,0},{2,3},{3,2},{4,5},{5,4},{6,7},{7,6},{8,9},{9,8},{10,11... | collective-permute-start | bytes 958472 | tf_op jit(solution)/shard_map/ppermute | solution.py:581
  17.7 10.0 %collective-permute-start.4 = (bf16[384,256]{1,0:T(8,128)(2,1)S(1)}, bf16[384,256]{1,0:T(8,128)(2,1)S(1)}, u32[]{:S(2)}, u32[]{:S(2)}) collective-permute-start(bf16[384,256]{1,0:T(8,128)(2,1)S(1)} %get-tuple-element.36.refs_0_), channel_id=1, source_target_pairs={{0,2},{1,3},{2,4},{3,5},{4,6},{5,7},{6,0},{7,1},{8,10},{9,11},{10,... | collective-permute-start | bytes 589832 | tf_op jit(solution)/shard_map/ppermute | solution.py:576
  18.1 16.0 %collective-permute-start.5 = (bf16[384,256]{1,0:T(8,128)(2,1)S(1)}, bf16[384,256]{1,0:T(8,128)(2,1)S(1)}, u32[]{:S(2)}, u32[]{:S(2)}) collective-permute-start(bf16[384,256]{1,0:T(8,128)(2,1)S(1)} %get-tuple-element.36.refs_0_), channel_id=1, source_target_pairs={{0,4},{1,5},{2,6},{3,7},{4,0},{5,1},{6,2},{7,3},{8,12},{9,13},{10,... | collective-permute-start | bytes 589832 | tf_op jit(solution)/shard_map/ppermute | solution.py:576
  20.1 16.2 %collective-permute-start.6 = (bf16[384,256]{1,0:T(8,128)(2,1)S(1)}, bf16[384,256]{1,0:T(8,128)(2,1)S(1)}, u32[]{:S(2)}, u32[]{:S(2)}) collective-permute-start(bf16[384,256]{1,0:T(8,128)(2,1)S(1)} %get-tuple-element.36.refs_0_), channel_id=1, source_target_pairs={{0,6},{1,7},{2,0},{3,1},{4,2},{5,3},{6,4},{7,5},{8,14},{9,15},{10,... | collective-permute-start | bytes 589832 | tf_op jit(solution)/shard_map/ppermute | solution.py:576
  22.9 4.7 %collective-permute-start.7 = (bf16[208,256]{1,0:T(8,128)(2,1)S(1)}, bf16[208,256]{1,0:T(8,128)(2,1)S(1)}, u32[]{:S(2)}, u32[]{:S(2)}) collective-permute-start(bf16[208,256]{1,0:T(8,128)(2,1)S(1)} %get-tuple-element.33.refs_0_), channel_id=1, source_target_pairs={{0,1},{1,0},{2,3},{3,2},{4,5},{5,4},{6,7},{7,6},{8,9},{9,8},{10,11... | collective-permute-start | bytes 319496 | tf_op jit(solution)/shard_map/ppermute | solution.py:581
  28.7 7.5 %collective-permute-start.9 = (bf16[32,256]{1,0:T(8,128)(2,1)S(1)}, bf16[32,256]{1,0:T(8,128)(2,1)S(1)}, u32[]{:S(2)}, u32[]{:S(2)}) collective-permute-start(bf16[32,256]{1,0:T(8,128)(2,1)S(1)} %get-tuple-element.40), channel_id=1, source_target_pairs={{0,8},{8,16},{16,24},{1,9},{9,17},{17,25},{2,10},{10,18},{18,26},{... | collective-permute-start | bytes 49160 | tf_op jit(solution)/shard_map/ppermute | solution.py:646
  36.8 2.0 %collective-permute-start.10 = (bf16[256,1024]{1,0:T(8,128)(2,1)S(1)}, bf16[256,1024]{1,0:T(8,128)(2,1)S(1)}, u32[]{:S(2)}, u32[]{:S(2)}) collective-permute-start(bf16[256,1024]{1,0:T(8,128)(2,1)S(1)} %get-tuple-element.52), channel_id=1, source_target_pairs={{0,8},{8,0},{16,24},{24,16},{1,9},{9,1},{17,25},{25,17},{2,10},{10... | collective-permute-start | bytes 1572872 | tf_op jit(solution)/shard_map/ppermute | solution.py:587
  36.9 1.9 %collective-permute-start.11 = (f32[1,2048]{1,0:T(1,128)S(1)}, f32[1,2048]{1,0:T(1,128)S(1)}, u32[]{:S(2)}, u32[]{:S(2)}) collective-permute-start(f32[1,2048]{1,0:T(1,128)S(1)} %get-tuple-element.35.refs_5_.own_ref), channel_id=1, source_target_pairs={{0,8},{8,0},{16,24},{24,16},{1,9},{9,1},{17,25},{25,17},{2,10},{10... | collective-permute-start | bytes 24584 | tf_op jit(solution)/shard_map/ppermute | solution.py:642
  39.0 16.8 %collective-permute-start.12 = (bf16[256,1024]{1,0:T(8,128)(2,1)S(1)}, bf16[256,1024]{1,0:T(8,128)(2,1)S(1)}, u32[]{:S(2)}, u32[]{:S(2)}) collective-permute-start(bf16[256,1024]{1,0:T(8,128)(2,1)S(1)} %shard_map.100), channel_id=1, source_target_pairs={{0,16},{8,24},{1,17},{9,25},{2,18},{10,26},{3,19},{11,27},{4,20},{... | collective-permute-start | bytes 1572872 | tf_op jit(solution)/shard_map/ppermute | solution.py:589
  56.2 6.8 %collective-permute-start.13 = (bf16[256,1024]{1,0:T(8,128)(2,1)S(1)}, bf16[256,1024]{1,0:T(8,128)(2,1)S(1)}, u32[]{:S(2)}, u32[]{:S(2)}) collective-permute-start(bf16[256,1024]{1,0:T(8,128)(2,1)S(1)} %get-tuple-element.55), channel_id=1, source_target_pairs={{0,8},{8,0},{16,24},{24,16},{1,9},{9,1},{17,25},{25,17},{2,10},{10... | collective-permute-start | bytes 1572872 | tf_op jit(solution)/shard_map/ppermute | solution.py:591
  63.0 21.7 %copy-start.4 = (f32[2048]{0:T(1024)S(1)}, f32[2048]{0:T(1024)}, u32[]{:S(2)}) copy-start(f32[2048]{0:T(1024)} %param.17) | copy-start | bytes 24580
  69.7 7.8 %collective-permute-start.16 = (f32[1,1536]{1,0:T(1,128)S(1)}, f32[1,1536]{1,0:T(1,128)S(1)}, u32[]{:S(2)}, u32[]{:S(2)}) collective-permute-start(f32[1,1536]{1,0:T(1,128)S(1)} %get-tuple-element.58), channel_id=1, source_target_pairs={{0,6},{1,7},{2,0},{3,1},{4,2},{5,3},{6,4},{7,5},{8,14},{9,15},{10,... | collective-permute-start | bytes 18440 | tf_op jit(solution)/shard_map/ppermute | solution.py:576
  75.1 4.5 %collective-permute-start.15 = (f32[1,1536]{1,0:T(1,128)S(1)}, f32[1,1536]{1,0:T(1,128)S(1)}, u32[]{:S(2)}, u32[]{:S(2)}) collective-permute-start(f32[1,1536]{1,0:T(1,128)S(1)} %get-tuple-element.58), channel_id=1, source_target_pairs={{0,4},{1,5},{2,6},{3,7},{4,0},{5,1},{6,2},{7,3},{8,12},{9,13},{10,... | collective-permute-start | bytes 18440 | tf_op jit(solution)/shard_map/ppermute | solution.py:576
  75.6 5.4 %collective-permute-start.14 = (f32[1,1536]{1,0:T(1,128)S(1)}, f32[1,1536]{1,0:T(1,128)S(1)}, u32[]{:S(2)}, u32[]{:S(2)}) collective-permute-start(f32[1,1536]{1,0:T(1,128)S(1)} %get-tuple-element.58), channel_id=1, source_target_pairs={{0,2},{1,3},{2,4},{3,5},{4,6},{5,7},{6,0},{7,1},{8,10},{9,11},{10,... | collective-permute-start | bytes 18440 | tf_op jit(solution)/shard_map/ppermute | solution.py:576
  81.0 3.7 %collective-permute-start.17 = (f32[1,1536]{1,0:T(1,128)S(1)}, f32[1,1536]{1,0:T(1,128)S(1)}, u32[]{:S(2)}, u32[]{:S(2)}) collective-permute-start(f32[1,1536]{1,0:T(1,128)S(1)} %add_add_fusion.one_ref), channel_id=1, source_target_pairs={{0,1},{1,0},{2,3},{3,2},{4,5},{5,4},{6,7},{7,6},{8,9},{9,8},{10,11... | collective-permute-start | bytes 18440 | tf_op jit(solution)/shard_map/ppermute | solution.py:581
  (1 other events, 0.7 us)

commit v3 on v2

--- a/solution.py
+++ b/solution.py
@@ -73,7 +73,8 @@
     return (total * jax.nn.sigmoid(total)).astype(BF16)
 
 
-def rates_kernel(dt_ref, a_ref, skip_ref, q_ref, b_ref, dec_ref, own_ref):
+def rates_kernel(dt_ref, a_ref, skip_ref, rows_ref, q_ref, b_ref, dec_ref, own_ref, rows_out):
+    rows_out[...] = rows_ref[...]
     block_count = dt_ref.shape[1] // BLOCK
     diagonal = lax.broadcasted_iota(jnp.int32, (SLOT, SLOT), 0) == lax.broadcasted_iota(
         jnp.int32, (SLOT, SLOT), 1
@@ -123,7 +124,7 @@
     own_ref[...] = rows[SLOT - 1 : SLOT]
 
 
-def rates(dt, a_log, d_skip, width):
+def rates(dt, a_log, d_skip, rows, width):
     length = dt.shape[1]
     return pl.pallas_call(
         rates_kernel,
@@ -132,12 +133,13 @@
             kept_in_vmem((SLOT, length), F32),
             kept_in_vmem((SLOT, width), F32),
             kept_in_vmem((1, width), F32),
-        ],
-        in_specs=[whole()] * 3,
-        out_specs=[whole()] * 4,
-        compiler_params=params(),
-        cost_estimate=cost(0, 0),
-    )(dt, a_log, d_skip)
+            jax.ShapeDtypeStruct(rows.shape, BF16),
+        ],
+        in_specs=[whole()] * 4,
+        out_specs=[whole()] * 5,
+        compiler_params=params(),
+        cost_estimate=cost(0, 0),
+    )(dt, a_log, d_skip, rows)
 
 
 def expander(ref, slot, base):
@@ -171,29 +173,23 @@
     )(place, bc_raw)
 
 
-def pack_kernel(*refs):
-    own_ref, side_ref, _, cat_ref, pair_ref = refs[-5:]
+def pack_kernel(count, *refs):
+    out_ref = refs[-1]
     per = refs[0].shape[0]
-    for i, ref in enumerate(refs[:-5]):
-        cat_ref[i * per : (i + 1) * per, :] = ref[...]
-    rows = own_ref.shape[0]
-    pair_ref[0:rows, :] = own_ref[...]
-    pair_ref[rows : 2 * rows, :] = side_ref[...]
-
-
-def pack(zones, own, side, after):
+    for i in range(count):
+        out_ref[i * per : (i + 1) * per, :] = refs[i][...]
+
+
+def pack(zones, *after):
     rows, columns = zones[0].shape
     return pl.pallas_call(
-        pack_kernel,
-        out_shape=[
-            jax.ShapeDtypeStruct((len(zones) * rows, columns), BF16),
-            jax.ShapeDtypeStruct((2 * own.shape[0], columns), BF16),
-        ],
-        in_specs=[whole()] * (len(zones) + 2) + [whole(pl.ANY)],
-        out_specs=[whole()] * 2,
-        compiler_params=params(),
-        cost_estimate=cost(0, 0),
-    )(*zones, own, side, after)
+        functools.partial(pack_kernel, len(zones)),
+        out_shape=jax.ShapeDtypeStruct((len(zones) * rows, columns), BF16),
+        in_specs=[whole()] * len(zones) + [whole(pl.ANY)] * len(after),
+        out_specs=whole(),
+        compiler_params=params(),
+        cost_estimate=cost(0, 0),
+    )(*zones, *after)
 
 
 def act_kernel(own_rows, plan, is_b, me_ref, weight_ref, bias_ref, *refs):
@@ -247,8 +243,8 @@
     )(me, weight, bias, *sources, *after)
 
 
-def tiles(width):
-    step = min(512, width)
+def tiles(width, step=512):
+    step = min(step, width)
     return [slice(i, i + step) for i in range(0, width, step)]
 
 
@@ -411,10 +407,12 @@
 
 
 def inner_kernel(
-    c_ref, b_ref, x_ref, q_ref, brow_ref, starts_ref, state_ref, dec_ref,
-    out_ref, expand_ref, held, sems,
+    c_ref, b_ref, x_ref, z_ref, q_ref, brow_ref, starts_ref, state_ref, dec_ref,
+    out_ref, z_out, expand_ref, held, sems, z_sem,
 ):
     stream_in(x_ref, held, sems)
+    z_copy = pltpu.make_async_copy(z_ref, z_out, z_sem)
+    z_copy.start()
     half = BLOCK // 2
     block_count = x_ref.shape[0] // BLOCK
     head_count = x_ref.shape[1] // HEAD_DIM
@@ -461,52 +459,51 @@
                 carried = jnp.dot(c_block, start.astype(BF16), preferred_element_type=F32)
                 out_ref[rows, columns] += grown * carried
 
-
-def inner(c_act, b_act, x, q, brow, starts, state, dec):
+    z_copy.wait()
+
+
+def inner(c_act, b_act, x, z, q, brow, starts, state, dec):
     length, width = x.shape
     return pl.pallas_call(
         inner_kernel,
-        out_shape=kept_in_vmem((length, width), F32),
-        in_specs=[whole()] * 2 + [whole(pltpu.HBM)] + [whole()] * 5,
-        out_specs=whole(),
+        out_shape=[kept_in_vmem((length, width), F32), kept_in_vmem(z.shape, z.dtype)],
+        in_specs=[whole()] * 2 + [whole(pltpu.HBM)] * 2 + [whole()] * 5,
+        out_specs=[whole()] * 2,
         scratch_shapes=[
             pltpu.VMEM((128, width), BF16),
             pltpu.VMEM((length // BLOCK, BLOCK, width), BF16),
             pltpu.SemaphoreType.DMA((length // BLOCK,)),
+            pltpu.SemaphoreType.DMA,
         ],
         compiler_params=params(),
         cost_estimate=cost(0, 13 * length * width),
-    )(c_act, b_act, x, q, brow, starts, state, dec)
+    )(c_act, b_act, x, z, q, brow, starts, state, dec)
 
 
 def gate_kernel(second, at_ref, c_ref, y_ref, z_ref, q_ref, in_ref, *refs):
-    out_ref, sum_ref, expand_ref, held, sems = refs[-5:]
+    out_ref, sum_ref, expand_ref, squares_ref = refs[-4:]
     width = in_ref.shape[1]
     base = pl.multiple_of(width - at_ref[1] if second else at_ref[1], 128)
-    stream_in(z_ref, held, sems, pl.ds(base, width))
     expander(expand_ref, 5, base)
-
-    @pl.loop(0, y_ref.shape[0] // BLOCK)
-    def _(c):
-        rows = pl.ds(pl.multiple_of(c * BLOCK, BLOCK), BLOCK)
-        pltpu.make_async_copy(z_ref.at[rows, pl.ds(base, width)], held.at[c], sems.at[c]).wait()
+    blocks = [slice(c, c + BLOCK) for c in range(0, y_ref.shape[0], BLOCK)]
+    for rows in blocks:
         c_block = c_ref[rows, :]
         q_short = q_ref[rows, :].astype(BF16)
-        squares = jnp.zeros((BLOCK, 128), F32)
-        for part in tiles(width):
+        squares = None
+        for part in tiles(width, 256):
             size = part.stop - part.start
             columns = pl.ds(pl.multiple_of(base + part.start, 128), size)
             grown = jnp.dot(q_short, expand_ref[:, part], preferred_element_type=F32)
             carried = jnp.dot(c_block, in_ref[:, part], preferred_element_type=F32)
-            gated = (y_ref[rows, columns] + grown * carried) * silu(held[c, :, part].astype(F32))
+            gated = (y_ref[rows, columns] + grown * carried) * silu(z_ref[rows, columns].astype(F32))
             out_ref[rows, columns] = gated
             square = gated * gated
             for i in range(0, size, 128):
-                squares = squares + square[:, i : i + 128]
-        total = lax.dot_general(
-            jnp.ones((8, 128), F32), squares, (((1,), (1,)), ((), ())),
-            precision=HIGHEST, preferred_element_type=F32,
-        )[0:1]
+                one = square[:, i : i + 128]
+                squares = one if squares is None else squares + one
+        squares_ref[rows, :] = squares
+    for rows in blocks:
+        total = jnp.sum(squares_ref[rows, :].T, axis=0, keepdims=True)
         sum_ref[:, rows] = refs[0][:, rows] + total if second else total
 
 
@@ -518,15 +515,11 @@
             kept_in_vmem((length, width), F32),
             kept_in_vmem((1, length), F32),
         ],
-        in_specs=[whole(pltpu.SMEM)]
-        + [whole()] * 2
-        + [whole(pltpu.HBM)]
-        + [whole()] * (2 + len(before)),
+        in_specs=[whole(pltpu.SMEM)] + [whole()] * (5 + len(before)),
         out_specs=[whole()] * 2,
         scratch_shapes=[
             pltpu.VMEM((128, incoming.shape[1]), BF16),
-            pltpu.VMEM((length // BLOCK, BLOCK, incoming.shape[1]), BF16),
-            pltpu.SemaphoreType.DMA((length // BLOCK,)),
+            pltpu.VMEM((length, 128), F32),
         ],
         input_output_aliases={2: 0},
         compiler_params=params(),
@@ -616,43 +609,45 @@
     own_b, own_c, place = prepare(place, bc_raw)
     zones_b = [zone_shift(own_b, k) for k in shifts]
     side_b = side_swap(own_b)
-    side_c = side_swap(own_c)
     pad = SLOT - head_count
-    q, brow, dec, own_decay = rates(
+    q, brow, dec, own_decay, own_c = rates(
         jnp.pad(dt_raw.T, ((0, pad), (0, 0))),
         jnp.pad(a_log, (0, pad))[None, :],
         jnp.pad(d_skip, (0, pad))[None, :],
+        own_c,
         width,
     )
-    cat_b, pair_c = pack(zones_b, own_c, side_c, own_decay)
-    others_b = side_swap(cat_b)
-    pairs_c = [zone_shift(pair_c, k) for k in shifts]
+    zones_c = [zone_shift(own_c, k) for k in shifts]
+    side_c = side_swap(own_c)
+    others_b = side_swap(pack(zones_b, own_decay, side_b))
+    others_c = side_swap(pack(zones_c, side_c))
+
+    def plan(per):
+        first = [(0, 0, False, 0), (1, 0, True, 0)]
+        near = [(k + 1, 0, False, k) for k in shifts]
+        return first + near + [(len(near) + 2, (k - 1) * per, True, k) for k in shifts]
+
+    plan_b, plan_c = plan(own_b.shape[0]), plan(own_rows)
     sources_b = [own_b, side_b, *zones_b, others_b]
-    plan_b = [(0, 0, False, 0), (1, 0, True, 0)]
-    plan_b += [(k + 1, 0, False, k) for k in shifts]
-    plan_b += [(len(zones_b) + 2, (k - 1) * own_b.shape[0], True, k) for k in shifts]
-    sources_c = [pair_c, *pairs_c]
-    plan_c = [(k, 0, False, k) for k in range(len(sources_c))]
-    plan_c += [(k, own_rows, True, k) for k in range(len(sources_c))]
-
+    sources_c = [own_c, side_c, *zones_c, others_c]
     bias = conv_bias[None, :]
     xs_first, xs_later = scale(x_inner, q)
     partner_decay = own_decay
     if seq_size == 4:
         partner_decay = lax.ppermute(own_decay, "seq", SWAP)
     b_act, first_b, last_rows = activate(
-        place, sources_b, plan_b, True, conv_weight, bias, own_rows, [xs_first, pairs_c[0]]
+        place, sources_b, plan_b, True, conv_weight, bias, own_rows, [xs_first]
     )
     rims = lax.ppermute(last_rows, "seq", [(i, i + 1) for i in range(seq_size - 1)])
-    starts, later = later_states(b_act, xs_later, dec, [pairs_c[1]])
+    starts, later = later_states(b_act, xs_later, dec)
     b_act, state_0, kept, sent = first_state(
-        place, b_act, first_b, rims, conv_weight, bias, xs_first, dec, later, [pairs_c[2]]
+        place, b_act, first_b, rims, conv_weight, bias, xs_first, dec, later, [others_c]
     )
     c_act, _, _ = activate(place, [*sources_c, rims], plan_c, False, conv_weight, bias, own_rows)
-    local = inner(c_act, b_act, x_inner, q, brow, starts, state_0, dec)
+    local, z_held = inner(c_act, b_act, x_inner, z_gate, q, brow, starts, state_0, dec)
     state_one, state_two = chained_state(place, kept, sent, own_decay, partner_decay, local)
-    gated, square_one = gate(place, c_act, local, z_gate, q, state_one)
-    gated, square_sum = gate(place, c_act, gated, z_gate, q, state_two, square_one)
+    gated, square_one = gate(place, c_act, local, z_held, q, state_one)
+    gated, square_sum = gate(place, c_act, gated, z_held, q, state_two, square_one)
     column = sum([zone_shift(square_sum, k) for k in shifts], square_sum)
     return norm(gated, column, side_swap(column), norm_gain[None, :])
 

time: 88.1 us -> 80.5 us (0.914)
  Pallas kernels: 39.6 us -> 32.5 us
  waiting for transfers between devices: 15.8 us -> 12.5 us
  starting transfers between devices: 28.9 us -> 31.7 us
    pallas_call x2, Pallas kernels: 13.4 us -> 6.45 us  [gate(): pl.pallas_call(functools.partial(gate_kernel, len(before) > 0), out_shape...]
    ppermute x4 -> x5, starting transfers between devices: 4.18 us -> 7.09 us  [side_swap(): return lax.ppermute(a, 'head', [(i, i ^ 1) for i in range(size)])]
    ppermute x9, waiting for transfers between devices: 10.9 us -> 8.53 us  [zone_shift(): lax.ppermute(a, 'head', [(i, (i + 2 * k) % size) for i in range(size)])]
    ppermute x1, starting transfers between devices: 0.07 us -> 2.28 us  [chained_state(): got = lax.ppermute(sent, 'seq', SWAP)]
    ppermute x9, starting transfers between devices: 19.2 us -> 17.6 us  [zone_shift(): lax.ppermute(a, 'head', [(i, (i + 2 * k) % size) for i in range(size)])]
    ppermute x4 -> x5, waiting for transfers between devices: 3.55 us -> 2.47 us  [side_swap(): return lax.ppermute(a, 'head', [(i, i ^ 1) for i in range(size)])]
    pallas_call x2 -> x3, Pallas kernels: 11.7 us -> 11.7 us  [the longest x1 11.6 us: inner(): pl.pallas_call(inner_kernel, out_shape=[kept_in_vmem((length, width), F32...]
  transfers between devices with their start and end apart: 18 -> 19, of which waited for: 7 -> 5; matrix products, arithmetic and copies ran while one was open for 0% -> 0% of each run, Pallas kernels for 32% -> 31%
where the time goes in v3:
time: 80.5 us; the launch traced here: 80.3 us
  Pallas kernels  32.5 us (40%)
  starting transfers between devices  31.7 us (39%)
  waiting for transfers between devices  12.5 us (16%)
  local copies, waits for them, and re-layouts  3.14 us (4%)
    ppermute x9, starting transfers between devices, zone_shift(): lax.ppermute(a, 'head', [(i, (i + 2 * k) % size) for i in range(size)])  17.6 us
    pallas_call x1, Pallas kernels, inner(): pl.pallas_call(inner_kernel, out_shape=[kept_in_vmem((length, width), F32...  11.6 us
    ppermute x9, waiting for transfers between devices, zone_shift(): lax.ppermute(a, 'head', [(i, (i + 2 * k) % size) for i in range(size)])  8.53 us
    ppermute x5, starting transfers between devices, side_swap(): return lax.ppermute(a, 'head', [(i, i ^ 1) for i in range(size)])  7.09 us
    pallas_call x2, Pallas kernels, gate(): pl.pallas_call(functools.partial(gate_kernel, len(before) > 0), out_shape...  6.45 us
    pallas_call x1, Pallas kernels, scale(): pl.pallas_call(scale_kernel, out_shape=[kept_in_vmem((BLOCK, width), BF16...  3.77 us
    ppermute x1, starting transfers between devices, chained_state(): crossed = lax.ppermute(both, 'seq', [(0, 2), (1, 3)])  3.28 us
    unnamed x14, local copies, waits for them, and re-layouts  3.14 us
  transfers between devices with their start and end apart: 19, of which 5 were waited for; matrix products, arithmetic and copies ran while one was open for 0% of the time, Pallas kernels for 31%

profile of v3, /device:TPU:0, one launch (start us, length us, event | category | flops | bytes accessed | tf_op | source)
XLA Modules:
  0.0 80.3 jit_solution(1282760647605688739)
XLA Ops:
  1.6 5.1 %collective-permute-start.8 = (bf16[208,256]{1,0:T(8,128)(2,1)S(1)}, bf16[208,256]{1,0:T(8,128)(2,1)S(1)}, u32[]{:S(2)}, u32[]{:S(2)}) collective-permute-start(bf16[208,256]{1,0:T(8,128)(2,1)S(1)} %get-tuple-element.36.refs_0_), channel_id=1, source_target_pairs={{0,6},{1,7},{2,0},{3,1},{4,2},{5,3},{6,4},{7,5},{8,14},{9,15},{10,... | collective-permute-start | bytes 319496 | tf_op jit(solution)/shard_map/ppermute | solution.py:569
  7.7 1.5 %collective-permute-start.5 = (bf16[208,256]{1,0:T(8,128)(2,1)S(1)}, bf16[208,256]{1,0:T(8,128)(2,1)S(1)}, u32[]{:S(2)}, u32[]{:S(2)}) collective-permute-start(bf16[208,256]{1,0:T(8,128)(2,1)S(1)} %get-tuple-element.36.refs_0_), channel_id=1, source_target_pairs={{0,1},{1,0},{2,3},{3,2},{4,5},{5,4},{6,7},{7,6},{8,9},{9,8},{10,11... | collective-permute-start | bytes 319496 | tf_op jit(solution)/shard_map/ppermute | solution.py:574
  11.4 1.3 %shard_map.92 = (f32[1536,128]{1,0:T(8,128)S(1)}, f32[16,1536]{1,0:T(8,128)S(1)}, f32[16,2048]{1,0:T(8,128)S(1)}, f32[1,2048]{1,0:T(1,128)S(1)}, bf16[192,256]{1,0:T(8,128)(2,1)S(1)}) custom-call(f32[16,1536]{1,0:T(8,128)S(1)} %bitcast.7, f32[1,16]{1,0:T(1,128)S(1)} %bitcast.12, f32[1,16]{1,0:T(1,128)S(1)} %bitcast.13, ...), custom_call_target="tpu_custom_call" | custom-call | tf_op jit(solution)/shard_map/pallas_call | solution.py:129
  12.7 2.8 %collective-permute-start.3 = (bf16[192,256]{1,0:T(8,128)(2,1)S(1)}, bf16[192,256]{1,0:T(8,128)(2,1)S(1)}, u32[]{:S(2)}, u32[]{:S(2)}) collective-permute-start(bf16[192,256]{1,0:T(8,128)(2,1)S(1)} %get-tuple-element.35.refs_0_), channel_id=1, source_target_pairs={{0,6},{1,7},{2,0},{3,1},{4,2},{5,3},{6,4},{7,5},{8,14},{9,15},{10,... | collective-permute-start | bytes 294920 | tf_op jit(solution)/shard_map/ppermute | solution.py:569
  16.6 2.7 %collective-permute-start = (bf16[192,256]{1,0:T(8,128)(2,1)S(1)}, bf16[192,256]{1,0:T(8,128)(2,1)S(1)}, u32[]{:S(2)}, u32[]{:S(2)}) collective-permute-start(bf16[192,256]{1,0:T(8,128)(2,1)S(1)} %get-tuple-element.35.refs_0_), channel_id=1, source_target_pairs={{0,1},{1,0},{2,3},{3,2},{4,5},{5,4},{6,7},{7,6},{8,9},{9,8},{10,11... | collective-permute-start | bytes 294920 | tf_op jit(solution)/shard_map/ppermute | solution.py:574
  19.4 5.0 %collective-permute-done.2.refs_1_.refs_3_ = bf16[192,256]{1,0:T(8,128)(2,1)S(1)} collective-permute-done((bf16[192,256]{1,0:T(8,128)(2,1)S(1)}, bf16[192,256]{1,0:T(8,128)(2,1)S(1)}, u32[]{:S(2)}, u32[]{:S(2)}) %collective-permute-start.2) | collective-permute-done | bytes 98336 | tf_op jit(solution)/shard_map/ppermute | solution.py:569
  24.5 1.6 %collective-permute-start.4 = (bf16[576,256]{1,0:T(8,128)(2,1)S(1)}, bf16[576,256]{1,0:T(8,128)(2,1)S(1)}, u32[]{:S(2)}, u32[]{:S(2)}) collective-permute-start(bf16[576,256]{1,0:T(8,128)(2,1)S(1)} %shard_map.93), channel_id=1, source_target_pairs={{0,1},{1,0},{2,3},{3,2},{4,5},{5,4},{6,7},{7,6},{8,9},{9,8},{10,11... | collective-permute-start | bytes 884744 | tf_op jit(solution)/shard_map/ppermute | solution.py:574
  26.1 3.8 %shard_map.95 = (bf16[256,2048]{1,0:T(8,128)(2,1)S(1)}, bf16[1280,2048]{1,0:T(8,128)(2,1)S(1)}) custom-call(bf16[1536,2048]{1,0:T(8,128)(2,1)} %x_ref.3, f32[1536,128]{1,0:T(8,128)S(1)} %get-tuple-element.38.q_ref), custom_call_target="tpu_custom_call" | custom-call | tf_op jit(solution)/shard_map/pallas_call | solution.py:270
  31.0 1.3 %collective-permute-start.10 = (bf16[32,256]{1,0:T(8,128)(2,1)S(1)}, bf16[32,256]{1,0:T(8,128)(2,1)S(1)}, u32[]{:S(2)}, u32[]{:S(2)}) collective-permute-start(bf16[32,256]{1,0:T(8,128)(2,1)S(1)} %get-tuple-element.40), channel_id=1, source_target_pairs={{0,8},{8,16},{16,24},{1,9},{9,17},{17,25},{2,10},{10,18},{18,26},{... | collective-permute-start | bytes 49160 | tf_op jit(solution)/shard_map/ppermute | solution.py:641
  32.3 2.2 %shard_map.98 = (bf16[5,256,2048]{2,1,0:T(8,128)(2,1)S(1)}, f32[256,2048]{1,0:T(8,128)S(1)}) custom-call(bf16[1536,256]{1,0:T(8,128)(2,1)S(1)} %get-tuple-element.42.b_ref, bf16[1280,2048]{1,0:T(8,128)(2,1)S(1)} %get-tuple-element.45.xs_ref, f32[16,2048]{1,0:T(8,128)S(1)} %get-tuple-element.44.dec_ref), custom_call_target="tpu_custom_call" | custom-call | tf_op jit(solution)/shard_map/pallas_call | solution.py:312
  35.1 2.3 %collective-permute-start.11 = (bf16[256,1024]{1,0:T(8,128)(2,1)S(1)}, bf16[256,1024]{1,0:T(8,128)(2,1)S(1)}, u32[]{:S(2)}, u32[]{:S(2)}) collective-permute-start(bf16[256,1024]{1,0:T(8,128)(2,1)S(1)} %get-tuple-element.54), channel_id=1, source_target_pairs={{0,8},{8,0},{16,24},{24,16},{1,9},{9,1},{17,25},{25,17},{2,10},{10... | collective-permute-start | bytes 1572872 | tf_op jit(solution)/shard_map/ppermute | solution.py:580
  37.4 1.5 %collective-permute-done.12.partner_ref = f32[1,2048]{1,0:T(1,128)S(1)} collective-permute-done((f32[1,2048]{1,0:T(1,128)S(1)}, f32[1,2048]{1,0:T(1,128)S(1)}, u32[]{:S(2)}, u32[]{:S(2)}) %collective-permute-start.12) | collective-permute-done | bytes 8224 | tf_op jit(solution)/shard_map/ppermute | solution.py:637
  39.1 3.3 %collective-permute-start.13 = (bf16[256,1024]{1,0:T(8,128)(2,1)S(1)}, bf16[256,1024]{1,0:T(8,128)(2,1)S(1)}, u32[]{:S(2)}, u32[]{:S(2)}) collective-permute-start(bf16[256,1024]{1,0:T(8,128)(2,1)S(1)} %shard_map.101), channel_id=1, source_target_pairs={{0,16},{8,24},{1,17},{9,25},{2,18},{10,26},{3,19},{11,27},{4,20},{... | collective-permute-start | bytes 1572872 | tf_op jit(solution)/shard_map/ppermute | solution.py:582
  42.4 1.4 %shard_map.97 = (bf16[1536,256]{1,0:T(8,128)(2,1)S(1)}, bf16[16,256]{1,0:T(8,128)(2,1)}, bf16[32,256]{1,0:T(8,128)(2,1)}) custom-call(s32[2]{0:T(128)S(4)} %get-tuple-element.33.me_ref.at_ref, f32[4,512]{1,0:T(4,128)S(1)} %copy-done.2, f32[1,512]{1,0:T(1,128)S(1)} %bitcast.10, bf16[192,256]{1,0:T(8,128)(2,1)S(1)} %get-tuple-element.35.refs_0_, ...), custom_call_target="tpu_custom_call" | custom-call | tf_op jit(solution)/shard_map/pallas_call | solution.py:229
  43.8 11.6 %shard_map.100 = (f32[1536,2048]{1,0:T(8,128)S(1)}, bf16[1536,2048]{1,0:T(8,128)(2,1)S(1)}) custom-call(bf16[1536,256]{1,0:T(8,128)(2,1)S(1)} %get-tuple-element.41.c_ref, bf16[1536,256]{1,0:T(8,128)(2,1)S(1)} %get-tuple-element.47.b_ref, bf16[1536,2048]{1,0:T(8,128)(2,1)} %x_ref.3, bf16[1536,2048]{1,0:T(8,128)(2,1)} %z_ref.1, ...), custom_call_target="tpu_custom_call" | custom-call | bytes 40894464 | tf_op jit(solution)/shard_map/pallas_call | solution.py:467
  55.9 3.3 %shard_map.103 = (f32[1536,2048]{1,0:T(8,128)S(1)}, f32[1,1536]{1,0:T(1,128)S(1)}) custom-call(s32[2]{0:T(128)S(4)} %get-tuple-element.33.me_ref.at_ref, bf16[1536,256]{1,0:T(8,128)(2,1)S(1)} %get-tuple-element.41.c_ref, f32[1536,2048]{1,0:T(8,128)S(1)} %get-tuple-element.51.refs_0_.y_ref, ...), custom_call_target="tpu_custom_call", output_to_operand_aliasing={{0}: (2, {})} | custom-call | bytes 25165824 | tf_op jit(solution)/shard_map/pallas_call | solution.py:512
  59.2 3.2 %shard_map.104 = (f32[1536,2048]{1,0:T(8,128)S(1)}, f32[1,1536]{1,0:T(1,128)S(1)}) custom-call(s32[2]{0:T(128)S(4)} %get-tuple-element.33.me_ref.at_ref, bf16[1536,256]{1,0:T(8,128)(2,1)S(1)} %get-tuple-element.41.c_ref, f32[1536,2048]{1,0:T(8,128)S(1)} %get-tuple-element.56.y_ref, ...), custom_call_target="tpu_custom_call", output_to_operand_aliasing={{0}: (2, {})} | custom-call | bytes 25165824 | tf_op jit(solution)/shard_map/pallas_call | solution.py:512
  62.4 3.9 %collective-permute-start.17 = (f32[1,1536]{1,0:T(1,128)S(1)}, f32[1,1536]{1,0:T(1,128)S(1)}, u32[]{:S(2)}, u32[]{:S(2)}) collective-permute-start(f32[1,1536]{1,0:T(1,128)S(1)} %get-tuple-element.60), channel_id=1, source_target_pairs={{0,6},{1,7},{2,0},{3,1},{4,2},{5,3},{6,4},{7,5},{8,14},{9,15},{10,... | collective-permute-start | bytes 18440 | tf_op jit(solution)/shard_map/ppermute | solution.py:569
  66.2 1.7 %collective-permute-start.16 = (f32[1,1536]{1,0:T(1,128)S(1)}, f32[1,1536]{1,0:T(1,128)S(1)}, u32[]{:S(2)}, u32[]{:S(2)}) collective-permute-start(f32[1,1536]{1,0:T(1,128)S(1)} %get-tuple-element.60), channel_id=1, source_target_pairs={{0,4},{1,5},{2,6},{3,7},{4,0},{5,1},{6,2},{7,3},{8,12},{9,13},{10,... | collective-permute-start | bytes 18440 | tf_op jit(solution)/shard_map/ppermute | solution.py:569
  68.0 1.9 %collective-permute-start.15 = (f32[1,1536]{1,0:T(1,128)S(1)}, f32[1,1536]{1,0:T(1,128)S(1)}, u32[]{:S(2)}, u32[]{:S(2)}) collective-permute-start(f32[1,1536]{1,0:T(1,128)S(1)} %get-tuple-element.60), channel_id=1, source_target_pairs={{0,2},{1,3},{2,4},{3,5},{4,6},{5,7},{6,0},{7,1},{8,10},{9,11},{10,... | collective-permute-start | bytes 18440 | tf_op jit(solution)/shard_map/ppermute | solution.py:569
  70.8 2.6 %collective-permute-done.15 = f32[1,1536]{1,0:T(1,128)S(1)} collective-permute-done((f32[1,1536]{1,0:T(1,128)S(1)}, f32[1,1536]{1,0:T(1,128)S(1)}, u32[]{:S(2)}, u32[]{:S(2)}) %collective-permute-start.15) | collective-permute-done | bytes 6176 | tf_op jit(solution)/shard_map/ppermute | solution.py:569
  73.4 1.2 %collective-permute-start.18 = (f32[1,1536]{1,0:T(1,128)S(1)}, f32[1,1536]{1,0:T(1,128)S(1)}, u32[]{:S(2)}, u32[]{:S(2)}) collective-permute-start(f32[1,1536]{1,0:T(1,128)S(1)} %add_add_fusion.one_ref), channel_id=1, source_target_pairs={{0,1},{1,0},{2,3},{3,2},{4,5},{5,4},{6,7},{7,6},{8,9},{9,8},{10,11... | collective-permute-start | bytes 18440 | tf_op jit(solution)/shard_map/ppermute | solution.py:574
  74.7 2.5 %collective-permute-done.18.two_ref = f32[1,1536]{1,0:T(1,128)S(1)} collective-permute-done((f32[1,1536]{1,0:T(1,128)S(1)}, f32[1,1536]{1,0:T(1,128)S(1)}, u32[]{:S(2)}, u32[]{:S(2)}) %collective-permute-start.18) | collective-permute-done | bytes 6176 | tf_op jit(solution)/shard_map/ppermute | solution.py:574
  77.1 3.0 %shard_map.105 = bf16[1536,2048]{1,0:T(8,128)(2,1)} custom-call(f32[1536,2048]{1,0:T(8,128)S(1)} %get-tuple-element.59.g_ref, f32[1,1536]{1,0:T(1,128)S(1)} %add_add_fusion.one_ref, f32[1,1536]{1,0:T(1,128)S(1)} %collective-permute-done.18.two_ref, f32[1,2048]{1,0:T(1,128)S(1)} %bitcast.11), custom_call_target="tpu_custom_call" | custom-call | tf_op jit(solution)/shard_map/pallas_call | solution.py:550
  (45 shorter events, 9.2 us)
Async XLA Ops:
  0.0 29.9 %copy-start.2 = (f32[4,512]{1,0:T(4,128)S(1)}, f32[4,512]{1,0:T(4,128)}, u32[]{:S(2)}) copy-start(f32[4,512]{1,0:T(4,128)} %weight_ref.5) | copy-start | bytes 24580
  0.0 29.9 %copy-start.3 = (f32[512]{0:T(512)S(1)}, f32[512]{0:T(512)}, u32[]{:S(2)}) copy-start(f32[512]{0:T(512)} %param.13) | copy-start | bytes 6148
  0.1 0.9 %copy-start = (bf16[192,512]{1,0:T(8,128)(2,1)S(1)}, bf16[192,512]{1,0:T(8,128)(2,1)}, u32[]{:S(2)}) copy-start(bf16[192,512]{1,0:T(8,128)(2,1)} %bc_ref.1) | copy-start | bytes 589828
  1.6 13.9 %collective-permute-start.8 = (bf16[208,256]{1,0:T(8,128)(2,1)S(1)}, bf16[208,256]{1,0:T(8,128)(2,1)S(1)}, u32[]{:S(2)}, u32[]{:S(2)}) collective-permute-start(bf16[208,256]{1,0:T(8,128)(2,1)S(1)} %get-tuple-element.36.refs_0_), channel_id=1, source_target_pairs={{0,6},{1,7},{2,0},{3,1},{4,2},{5,3},{6,4},{7,5},{8,14},{9,15},{10,... | collective-permute-start | bytes 319496 | tf_op jit(solution)/shard_map/ppermute | solution.py:569
  6.7 10.0 %collective-permute-start.7 = (bf16[208,256]{1,0:T(8,128)(2,1)S(1)}, bf16[208,256]{1,0:T(8,128)(2,1)S(1)}, u32[]{:S(2)}, u32[]{:S(2)}) collective-permute-start(bf16[208,256]{1,0:T(8,128)(2,1)S(1)} %get-tuple-element.36.refs_0_), channel_id=1, source_target_pairs={{0,4},{1,5},{2,6},{3,7},{4,0},{5,1},{6,2},{7,3},{8,12},{9,13},{10,... | collective-permute-start | bytes 319496 | tf_op jit(solution)/shard_map/ppermute | solution.py:569
  6.7 10.0 %collective-permute-start.6 = (bf16[208,256]{1,0:T(8,128)(2,1)S(1)}, bf16[208,256]{1,0:T(8,128)(2,1)S(1)}, u32[]{:S(2)}, u32[]{:S(2)}) collective-permute-start(bf16[208,256]{1,0:T(8,128)(2,1)S(1)} %get-tuple-element.36.refs_0_), channel_id=1, source_target_pairs={{0,2},{1,3},{2,4},{3,5},{4,6},{5,7},{6,0},{7,1},{8,10},{9,11},{10,... | collective-permute-start | bytes 319496 | tf_op jit(solution)/shard_map/ppermute | solution.py:569
  7.7 11.6 %collective-permute-start.5 = (bf16[208,256]{1,0:T(8,128)(2,1)S(1)}, bf16[208,256]{1,0:T(8,128)(2,1)S(1)}, u32[]{:S(2)}, u32[]{:S(2)}) collective-permute-start(bf16[208,256]{1,0:T(8,128)(2,1)S(1)} %get-tuple-element.36.refs_0_), channel_id=1, source_target_pairs={{0,1},{1,0},{2,3},{3,2},{4,5},{5,4},{6,7},{7,6},{8,9},{9,8},{10,11... | collective-permute-start | bytes 319496 | tf_op jit(solution)/shard_map/ppermute | solution.py:574
  9.2 0.9 %copy-start.1 = (f32[1536,16]{0,1:T(8,128)S(1)}, f32[1536,16]{0,1:T(8,128)}, u32[]{:S(2)}) copy-start(f32[1536,16]{0,1:T(8,128)} %param.14) | copy-start | bytes 294916
  12.7 6.7 %collective-permute-start.3 = (bf16[192,256]{1,0:T(8,128)(2,1)S(1)}, bf16[192,256]{1,0:T(8,128)(2,1)S(1)}, u32[]{:S(2)}, u32[]{:S(2)}) collective-permute-start(bf16[192,256]{1,0:T(8,128)(2,1)S(1)} %get-tuple-element.35.refs_0_), channel_id=1, source_target_pairs={{0,6},{1,7},{2,0},{3,1},{4,2},{5,3},{6,4},{7,5},{8,14},{9,15},{10,... | collective-permute-start | bytes 294920 | tf_op jit(solution)/shard_map/ppermute | solution.py:569
  15.5 8.9 %collective-permute-start.2 = (bf16[192,256]{1,0:T(8,128)(2,1)S(1)}, bf16[192,256]{1,0:T(8,128)(2,1)S(1)}, u32[]{:S(2)}, u32[]{:S(2)}) collective-permute-start(bf16[192,256]{1,0:T(8,128)(2,1)S(1)} %get-tuple-element.35.refs_0_), channel_id=1, source_target_pairs={{0,4},{1,5},{2,6},{3,7},{4,0},{5,1},{6,2},{7,3},{8,12},{9,13},{10,... | collective-permute-start | bytes 294920 | tf_op jit(solution)/shard_map/ppermute | solution.py:569
  16.6 7.8 %collective-permute-start.1 = (bf16[192,256]{1,0:T(8,128)(2,1)S(1)}, bf16[192,256]{1,0:T(8,128)(2,1)S(1)}, u32[]{:S(2)}, u32[]{:S(2)}) collective-permute-start(bf16[192,256]{1,0:T(8,128)(2,1)S(1)} %get-tuple-element.35.refs_0_), channel_id=1, source_target_pairs={{0,2},{1,3},{2,4},{3,5},{4,6},{5,7},{6,0},{7,1},{8,10},{9,11},{10,... | collective-permute-start | bytes 294920 | tf_op jit(solution)/shard_map/ppermute | solution.py:569
  16.6 7.8 %collective-permute-start = (bf16[192,256]{1,0:T(8,128)(2,1)S(1)}, bf16[192,256]{1,0:T(8,128)(2,1)S(1)}, u32[]{:S(2)}, u32[]{:S(2)}) collective-permute-start(bf16[192,256]{1,0:T(8,128)(2,1)S(1)} %get-tuple-element.35.refs_0_), channel_id=1, source_target_pairs={{0,1},{1,0},{2,3},{3,2},{4,5},{5,4},{6,7},{7,6},{8,9},{9,8},{10,11... | collective-permute-start | bytes 294920 | tf_op jit(solution)/shard_map/ppermute | solution.py:574
  19.3 10.5 %collective-permute-start.9 = (bf16[624,256]{1,0:T(8,128)(2,1)S(1)}, bf16[624,256]{1,0:T(8,128)(2,1)S(1)}, u32[]{:S(2)}, u32[]{:S(2)}) collective-permute-start(bf16[624,256]{1,0:T(8,128)(2,1)S(1)} %shard_map.94), channel_id=1, source_target_pairs={{0,1},{1,0},{2,3},{3,2},{4,5},{5,4},{6,7},{7,6},{8,9},{9,8},{10,11... | collective-permute-start | bytes 958472 | tf_op jit(solution)/shard_map/ppermute | solution.py:574
  24.5 10.0 %collective-permute-start.4 = (bf16[576,256]{1,0:T(8,128)(2,1)S(1)}, bf16[576,256]{1,0:T(8,128)(2,1)S(1)}, u32[]{:S(2)}, u32[]{:S(2)}) collective-permute-start(bf16[576,256]{1,0:T(8,128)(2,1)S(1)} %shard_map.93), channel_id=1, source_target_pairs={{0,1},{1,0},{2,3},{3,2},{4,5},{5,4},{6,7},{7,6},{8,9},{9,8},{10,11... | collective-permute-start | bytes 884744 | tf_op jit(solution)/shard_map/ppermute | solution.py:574
  31.0 3.5 %collective-permute-start.10 = (bf16[32,256]{1,0:T(8,128)(2,1)S(1)}, bf16[32,256]{1,0:T(8,128)(2,1)S(1)}, u32[]{:S(2)}, u32[]{:S(2)}) collective-permute-start(bf16[32,256]{1,0:T(8,128)(2,1)S(1)} %get-tuple-element.40), channel_id=1, source_target_pairs={{0,8},{8,16},{16,24},{1,9},{9,17},{17,25},{2,10},{10,18},{18,26},{... | collective-permute-start | bytes 49160 | tf_op jit(solution)/shard_map/ppermute | solution.py:641
  35.1 3.8 %collective-permute-start.11 = (bf16[256,1024]{1,0:T(8,128)(2,1)S(1)}, bf16[256,1024]{1,0:T(8,128)(2,1)S(1)}, u32[]{:S(2)}, u32[]{:S(2)}) collective-permute-start(bf16[256,1024]{1,0:T(8,128)(2,1)S(1)} %get-tuple-element.54), channel_id=1, source_target_pairs={{0,8},{8,0},{16,24},{24,16},{1,9},{9,1},{17,25},{25,17},{2,10},{10... | collective-permute-start | bytes 1572872 | tf_op jit(solution)/shard_map/ppermute | solution.py:580
  37.3 1.5 %collective-permute-start.12 = (f32[1,2048]{1,0:T(1,128)S(1)}, f32[1,2048]{1,0:T(1,128)S(1)}, u32[]{:S(2)}, u32[]{:S(2)}) collective-permute-start(f32[1,2048]{1,0:T(1,128)S(1)} %get-tuple-element.37.refs_3_.own_ref), channel_id=1, source_target_pairs={{0,8},{8,0},{16,24},{24,16},{1,9},{9,1},{17,25},{25,17},{2,10},{10... | collective-permute-start | bytes 24584 | tf_op jit(solution)/shard_map/ppermute | solution.py:637
  39.1 16.4 %collective-permute-start.13 = (bf16[256,1024]{1,0:T(8,128)(2,1)S(1)}, bf16[256,1024]{1,0:T(8,128)(2,1)S(1)}, u32[]{:S(2)}, u32[]{:S(2)}) collective-permute-start(bf16[256,1024]{1,0:T(8,128)(2,1)S(1)} %shard_map.101), channel_id=1, source_target_pairs={{0,16},{8,24},{1,17},{9,25},{2,18},{10,26},{3,19},{11,27},{4,20},{... | collective-permute-start | bytes 1572872 | tf_op jit(solution)/shard_map/ppermute | solution.py:582
  55.8 3.4 %collective-permute-start.14 = (bf16[256,1024]{1,0:T(8,128)(2,1)S(1)}, bf16[256,1024]{1,0:T(8,128)(2,1)S(1)}, u32[]{:S(2)}, u32[]{:S(2)}) collective-permute-start(bf16[256,1024]{1,0:T(8,128)(2,1)S(1)} %get-tuple-element.57), channel_id=1, source_target_pairs={{0,8},{8,0},{16,24},{24,16},{1,9},{9,1},{17,25},{25,17},{2,10},{10... | collective-permute-start | bytes 1572872 | tf_op jit(solution)/shard_map/ppermute | solution.py:584
  59.2 17.9 %copy-start.4 = (f32[2048]{0:T(1024)S(1)}, f32[2048]{0:T(1024)}, u32[]{:S(2)}) copy-start(f32[2048]{0:T(1024)} %param.17) | copy-start | bytes 24580
  62.4 7.5 %collective-permute-start.17 = (f32[1,1536]{1,0:T(1,128)S(1)}, f32[1,1536]{1,0:T(1,128)S(1)}, u32[]{:S(2)}, u32[]{:S(2)}) collective-permute-start(f32[1,1536]{1,0:T(1,128)S(1)} %get-tuple-element.60), channel_id=1, source_target_pairs={{0,6},{1,7},{2,0},{3,1},{4,2},{5,3},{6,4},{7,5},{8,14},{9,15},{10,... | collective-permute-start | bytes 18440 | tf_op jit(solution)/shard_map/ppermute | solution.py:569
  66.2 4.5 %collective-permute-start.16 = (f32[1,1536]{1,0:T(1,128)S(1)}, f32[1,1536]{1,0:T(1,128)S(1)}, u32[]{:S(2)}, u32[]{:S(2)}) collective-permute-start(f32[1,1536]{1,0:T(1,128)S(1)} %get-tuple-element.60), channel_id=1, source_target_pairs={{0,4},{1,5},{2,6},{3,7},{4,0},{5,1},{6,2},{7,3},{8,12},{9,13},{10,... | collective-permute-start | bytes 18440 | tf_op jit(solution)/shard_map/ppermute | solution.py:569
  68.0 5.4 %collective-permute-start.15 = (f32[1,1536]{1,0:T(1,128)S(1)}, f32[1,1536]{1,0:T(1,128)S(1)}, u32[]{:S(2)}, u32[]{:S(2)}) collective-permute-start(f32[1,1536]{1,0:T(1,128)S(1)} %get-tuple-element.60), channel_id=1, source_target_pairs={{0,2},{1,3},{2,4},{3,5},{4,6},{5,7},{6,0},{7,1},{8,10},{9,11},{10,... | collective-permute-start | bytes 18440 | tf_op jit(solution)/shard_map/ppermute | solution.py:569
  73.4 3.7 %collective-permute-start.18 = (f32[1,1536]{1,0:T(1,128)S(1)}, f32[1,1536]{1,0:T(1,128)S(1)}, u32[]{:S(2)}, u32[]{:S(2)}) collective-permute-start(f32[1,1536]{1,0:T(1,128)S(1)} %add_add_fusion.one_ref), channel_id=1, source_target_pairs={{0,1},{1,0},{2,3},{3,2},{4,5},{5,4},{6,7},{7,6},{8,9},{9,8},{10,11... | collective-permute-start | bytes 18440 | tf_op jit(solution)/shard_map/ppermute | solution.py:574
  (2 other events, 1.3 us)

commit v4 on v3

--- a/solution.py
+++ b/solution.py
@@ -14,6 +14,7 @@
 INNER = 16384
 RIM = 16
 SLOT = 16
+PIECES = 4
 LOG2E = math.log2(math.e)
 F32 = jnp.float32
 BF16 = jnp.bfloat16
@@ -73,8 +74,14 @@
     return (total * jax.nn.sigmoid(total)).astype(BF16)
 
 
-def rates_kernel(dt_ref, a_ref, skip_ref, rows_ref, q_ref, b_ref, dec_ref, own_ref, rows_out):
-    rows_out[...] = rows_ref[...]
+def rates_kernel(
+    dt_hbm, a_ref, skip_ref, x_ref, q_ref, b_ref, dec_ref, own_ref, first_ref, later_ref,
+    dt_ref, expand_ref, held, sems, dt_sem,
+):
+    dt_copy = pltpu.make_async_copy(dt_hbm, dt_ref, dt_sem)
+    dt_copy.start()
+    copies = stream_in(x_ref, held, sems)
+    expander(expand_ref, 1, 0)
     block_count = dt_ref.shape[1] // BLOCK
     diagonal = lax.broadcasted_iota(jnp.int32, (SLOT, SLOT), 0) == lax.broadcasted_iota(
         jnp.int32, (SLOT, SLOT), 1
@@ -92,6 +99,7 @@
     later = jnp.zeros((SLOT, 1), F32)
     lane = lax.broadcasted_iota(jnp.int32, (SLOT, SLOT), 1)
     logs = jnp.zeros((SLOT, SLOT), F32)
+    dt_copy.wait()
     for c in range(block_count):
         columns = slice(c * BLOCK, (c + 1) * BLOCK)
         dt = dt_ref[:, columns]
@@ -122,10 +130,23 @@
     )
     dec_ref[...] = rows
     own_ref[...] = rows[SLOT - 1 : SLOT]
-
-
-def rates(dt, a_log, d_skip, rows, width):
-    length = dt.shape[1]
+    for copy in copies:
+        copy.wait()
+    for c in range(block_count):
+        rows = slice(c * BLOCK, (c + 1) * BLOCK)
+        q_block = q_ref[rows, :].astype(BF16)
+        for columns in tiles(width):
+            weight = jnp.dot(q_block, expand_ref[:, columns], preferred_element_type=F32)
+            scaled = (held[c, :, columns].astype(F32) * weight).astype(BF16)
+            if c == 0:
+                first_ref[:, columns] = scaled
+            else:
+                later_ref[(c - 1) * BLOCK : c * BLOCK, columns] = scaled
+
+
+def rates(dt, a_log, d_skip, x):
+    length, width = x.shape
+    count = length // BLOCK
     return pl.pallas_call(
         rates_kernel,
         out_shape=[
@@ -133,13 +154,21 @@
             kept_in_vmem((SLOT, length), F32),
             kept_in_vmem((SLOT, width), F32),
             kept_in_vmem((1, width), F32),
-            jax.ShapeDtypeStruct(rows.shape, BF16),
-        ],
-        in_specs=[whole()] * 4,
-        out_specs=[whole()] * 5,
-        compiler_params=params(),
-        cost_estimate=cost(0, 0),
-    )(dt, a_log, d_skip, rows)
+            kept_in_vmem((BLOCK, width), BF16),
+            kept_in_vmem((length - BLOCK, width), BF16),
+        ],
+        in_specs=[whole(pltpu.HBM), whole(), whole(), whole(pltpu.HBM)],
+        out_specs=[whole()] * 6,
+        scratch_shapes=[
+            pltpu.VMEM(dt.shape, F32),
+            pltpu.VMEM((128, width), BF16),
+            pltpu.VMEM((count, BLOCK, width), BF16),
+            pltpu.SemaphoreType.DMA((count,)),
+            pltpu.SemaphoreType.DMA,
+        ],
+        compiler_params=params(),
+        cost_estimate=cost(0, 0),
+    )(in_hbm(dt), a_log, d_skip, x)
 
 
 def expander(ref, slot, base):
@@ -148,13 +177,21 @@
     ref[...] = ((row == slot * SLOT + head) | (row == (slot + 1) * SLOT + head)).astype(BF16)
 
 
-def prepare_kernel(place_ref, bc_ref, b_ref, c_ref, place_out):
+def prepare_kernel(place_ref, bc_ref, b_ref, c_ref, place_out, sems):
     rows = bc_ref.shape[0]
+    copies = [
+        pltpu.make_async_copy(bc_ref.at[:, 0:STATE], b_ref.at[0:rows, :], sems.at[0]),
+        pltpu.make_async_copy(
+            bc_ref.at[rows - RIM : rows, STATE : 2 * STATE], b_ref.at[rows : rows + RIM, :], sems.at[1]
+        ),
+        pltpu.make_async_copy(bc_ref.at[:, STATE : 2 * STATE], c_ref, sems.at[2]),
+    ]
+    for copy in copies:
+        copy.start()
     for i in range(place_ref.shape[0]):
         place_out[i] = place_ref[i]
-    b_ref[0:rows, :] = bc_ref[:, :STATE]
-    b_ref[rows : rows + RIM, :] = bc_ref[rows - RIM :, STATE:]
-    c_ref[...] = bc_ref[:, STATE:]
+    for copy in copies:
+        copy.wait()
 
 
 def prepare(place, bc_raw):
@@ -166,30 +203,38 @@
             jax.ShapeDtypeStruct((rows, STATE), BF16),
             pltpu.SMEM(place.shape, jnp.int32),
         ],
-        in_specs=[whole(pltpu.SMEM), whole()],
+        in_specs=[whole(pltpu.SMEM), whole(pltpu.HBM)],
         out_specs=[whole(), whole(), whole(pltpu.SMEM)],
-        compiler_params=params(),
-        cost_estimate=cost(0, 0),
-    )(place, bc_raw)
+        scratch_shapes=[pltpu.SemaphoreType.DMA((3,))],
+        compiler_params=params(),
+        cost_estimate=cost(0, 0),
+    )(place, in_hbm(bc_raw))
 
 
 def pack_kernel(count, *refs):
-    out_ref = refs[-1]
+    own_ref, side_ref = refs[count : count + 2]
+    cat_ref, pair_ref = refs[-2:]
     per = refs[0].shape[0]
     for i in range(count):
-        out_ref[i * per : (i + 1) * per, :] = refs[i][...]
-
-
-def pack(zones, *after):
+        cat_ref[i * per : (i + 1) * per, :] = refs[i][...]
+    rows = own_ref.shape[0]
+    pair_ref[0:rows, :] = own_ref[...]
+    pair_ref[rows : 2 * rows, :] = side_ref[...]
+
+
+def pack(zones, own, side, *after):
     rows, columns = zones[0].shape
     return pl.pallas_call(
         functools.partial(pack_kernel, len(zones)),
-        out_shape=jax.ShapeDtypeStruct((len(zones) * rows, columns), BF16),
-        in_specs=[whole()] * len(zones) + [whole(pl.ANY)] * len(after),
-        out_specs=whole(),
-        compiler_params=params(),
-        cost_estimate=cost(0, 0),
-    )(*zones, *after)
+        out_shape=[
+            jax.ShapeDtypeStruct((len(zones) * rows, columns), BF16),
+            jax.ShapeDtypeStruct((2 * own.shape[0], columns), BF16),
+        ],
+        in_specs=[whole()] * (len(zones) + 2) + [whole(pl.ANY)] * len(after),
+        out_specs=[whole()] * 2,
+        compiler_params=params(),
+        cost_estimate=cost(0, 0),
+    )(*zones, own, side, *after)
 
 
 def act_kernel(own_rows, plan, is_b, me_ref, weight_ref, bias_ref, *refs):
@@ -248,43 +293,6 @@
     return [slice(i, i + step) for i in range(0, width, step)]
 
 
-def scale_kernel(x_ref, q_ref, first_ref, later_ref, expand_ref, held, sems):
-    copies = stream_in(x_ref, held, sems)
-    expander(expand_ref, 1, 0)
-    for c, copy in enumerate(copies):
-        rows = slice(c * BLOCK, (c + 1) * BLOCK)
-        q_block = q_ref[rows, :].astype(BF16)
-        copy.wait()
-        for columns in tiles(x_ref.shape[1]):
-            weight = jnp.dot(q_block, expand_ref[:, columns], preferred_element_type=F32)
-            scaled = (held[c, :, columns].astype(F32) * weight).astype(BF16)
-            if c == 0:
-                first_ref[:, columns] = scaled
-            else:
-                later_ref[(c - 1) * BLOCK : c * BLOCK, columns] = scaled
-
-
-def scale(x, q):
-    length, width = x.shape
-    count = length // BLOCK
-    return pl.pallas_call(
-        scale_kernel,
-        out_shape=[
-            kept_in_vmem((BLOCK, width), BF16),
-            kept_in_vmem((length - BLOCK, width), BF16),
-        ],
-        in_specs=[whole(pltpu.HBM), whole()],
-        out_specs=[whole()] * 2,
-        scratch_shapes=[
-            pltpu.VMEM((128, width), BF16),
-            pltpu.VMEM((count, BLOCK, width), BF16),
-            pltpu.SemaphoreType.DMA((count,)),
-        ],
-        compiler_params=params(),
-        cost_estimate=cost(0, 0),
-    )(x, q)
-
-
 def block_state(b_block, scaled):
     return lax.dot_general(
         b_block, scaled, (((0,), (0,)), ((), ())), preferred_element_type=F32
@@ -325,7 +333,7 @@
 def first_state_kernel(
     at_ref, b_ref, first_ref, rim_ref, weight_ref, bias_ref, xs_ref, dec_ref, later_ref, *refs
 ):
-    b_out, state_ref, kept_ref, sent_ref, total_ref = refs[-5:]
+    own_ref, b_out, state_ref, kept_ref, *sent_refs, total_ref = refs
     slab = jnp.concatenate([rim_ref[0:RIM, :], first_ref[...]], axis=0).astype(F32)
     fixed = conv_slab(slab, weight_ref[:, :STATE], bias_ref[:, :STATE])
     b_block = jnp.concatenate([fixed, b_ref[RIM:BLOCK, :]], axis=0)
@@ -339,47 +347,70 @@
     half = kept_ref.shape[1]
     at = pl.multiple_of(at_ref[1], 128)
     kept_ref[...] = total_ref[:, pl.ds(at, half)]
-    sent_ref[...] = total_ref[:, pl.ds(pl.multiple_of(half - at, 128), half)]
-
-
-def first_state(at, b_act, first, rim, weight, bias, xs, dec, later, after=()):
+    size = half // len(sent_refs)
+    row_index = lax.broadcasted_iota(jnp.int32, (RIM, size), 0)
+    for i, sent_ref in enumerate(sent_refs):
+        columns = pl.ds(pl.multiple_of(half - at + i * size, 128), size)
+        sent_ref[0:STATE, :] = total_ref[:, columns]
+        rest = own_ref[:, columns]
+        rows = jnp.zeros((RIM, size), F32)
+        for k in range(3):
+            term = rest.astype(BF16).astype(F32)
+            rows = jnp.where(row_index == k, term, rows)
+            rest = rest - term
+        sent_ref[STATE : STATE + RIM, :] = rows.astype(BF16)
+
+
+def first_state(at, b_act, first, rim, weight, bias, xs, dec, later, own):
     width = xs.shape[1]
+    pieces = PIECES if width >= 256 * PIECES else 1
     return pl.pallas_call(
         first_state_kernel,
         out_shape=[
             kept_in_vmem(b_act.shape, BF16),
             kept_in_vmem((STATE, width), F32),
             kept_in_vmem((STATE, width // 2), BF16),
-            kept_in_vmem((STATE, width // 2), BF16),
-        ],
-        in_specs=[whole(pltpu.SMEM)] + [whole()] * 8 + [whole(pl.ANY)] * len(after),
-        out_specs=[whole()] * 4,
+        ]
+        + [kept_in_vmem((STATE + RIM, width // 2 // pieces), BF16)] * pieces,
+        in_specs=[whole(pltpu.SMEM)] + [whole()] * 9,
+        out_specs=[whole()] * (3 + pieces),
         scratch_shapes=[pltpu.VMEM((STATE, width), BF16)],
         input_output_aliases={1: 0},
         compiler_params=params(),
         cost_estimate=cost(0, 0),
-    )(at, b_act, first, rim, weight, bias, xs, dec, later, *after)
-
-
-def meet_kernel(at_ref, kept_ref, got_ref, own_ref, partner_ref, out_ref):
+    )(at, b_act, first, rim, weight, bias, xs, dec, later, own)
+
+
+def meet_kernel(count, at_ref, kept_ref, own_ref, *refs):
+    got_refs = refs[:count]
+    out_ref, got_ref, partner_ref = refs[-3:]
+    size = got_refs[0].shape[1]
+    for i, ref in enumerate(got_refs):
+        part = slice(i * size, (i + 1) * size)
+        got_ref[:, part] = ref[0:STATE, :]
+        rows = ref[STATE : STATE + RIM, :].astype(F32)
+        partner_ref[:, part] = rows[0:1] + rows[1:2] + rows[2:3]
     half = kept_ref.shape[1]
     columns = pl.ds(pl.multiple_of(at_ref[1], 128), half)
     odd = at_ref[1] == 0
-    kept_decay = jnp.where(odd, 1.0, partner_ref[:, columns])
+    kept_decay = jnp.where(odd, 1.0, partner_ref[...])
     got_decay = jnp.where(odd, own_ref[:, columns], 1.0)
     both = kept_decay * kept_ref[...].astype(F32) + got_decay * got_ref[...].astype(F32)
     out_ref[...] = both.astype(BF16)
 
 
-def meet(at, kept, got, own, partner):
-    return pl.pallas_call(
-        meet_kernel,
-        out_shape=kept_in_vmem(kept.shape, BF16),
-        in_specs=[whole(pltpu.SMEM)] + [whole()] * 4,
-        out_specs=whole(),
-        compiler_params=params(),
-        cost_estimate=cost(0, 0),
-    )(at, kept, got, own, partner)
+def meet(at, kept, own, got, after):
+    return pl.pallas_call(
+        functools.partial(meet_kernel, len(got)),
+        out_shape=[kept_in_vmem(kept.shape, BF16)] * 2
+        + [kept_in_vmem((1, kept.shape[1]), F32)],
+        in_specs=[whole(pltpu.SMEM)]
+        + [whole()] * (2 + len(got))
+        + [whole(pl.ANY)] * len(after),
+        out_specs=[whole()] * 3,
+        compiler_params=params(),
+        cost_estimate=cost(0, 0),
+    )(at, kept, own, *got, *after)
 
 
 def arrive_kernel(at_ref, crossed_ref, kept_ref, got_ref, own_ref, partner_ref, *refs):
@@ -387,7 +418,7 @@
     half = kept_ref.shape[1]
     columns = pl.ds(pl.multiple_of(at_ref[1], 128), half)
     odd = at_ref[1] == 0
-    decay = jnp.where(odd, partner_ref[:, columns], own_ref[:, columns])
+    decay = jnp.where(odd, partner_ref[...], own_ref[:, columns])
     crossed = crossed_ref[...]
     mine = jnp.where(odd, got_ref[...].astype(F32), kept_ref[...].astype(F32))
     after_even = (decay * crossed.astype(F32) + mine).astype(BF16)
@@ -476,7 +507,7 @@
             pltpu.SemaphoreType.DMA,
         ],
         compiler_params=params(),
-        cost_estimate=cost(0, 13 * length * width),
+        cost_estimate=cost(0, 80 * length * width),
     )(c_act, b_act, x, z, q, brow, starts, state, dec)
 
 
@@ -574,15 +605,15 @@
     return lax.ppermute(a, "head", [(i, i ^ 1) for i in range(size)])
 
 
-def chained_state(at, kept, sent, own, partner, after):
+def chained_state(at, kept, sent, own, after, late):
     size = lax.axis_size("seq")
     if size == 4:
-        got = lax.ppermute(sent, "seq", SWAP)
-        both = meet(at, kept, got, own, partner)
+        got = [lax.ppermute(piece, "seq", SWAP) for piece in sent]
+        both, got, partner = meet(at, kept, own, got, late)
         crossed = lax.ppermute(both, "seq", [(0, 2), (1, 3)])
         mine, passed = arrive(at, crossed, kept, got, own, partner, after)
         return mine, lax.ppermute(passed, "seq", SWAP)
-    totals = lax.all_gather(jnp.concatenate([kept, sent], axis=1), "seq")
+    totals = lax.all_gather(jnp.concatenate([kept, *[a[:STATE] for a in sent]], axis=1), "seq")
     decays = lax.all_gather(own, "seq")
 
     def one(hop, state):
@@ -610,42 +641,36 @@
     zones_b = [zone_shift(own_b, k) for k in shifts]
     side_b = side_swap(own_b)
     pad = SLOT - head_count
-    q, brow, dec, own_decay, own_c = rates(
+    q, brow, dec, own_decay, xs_first, xs_later = rates(
         jnp.pad(dt_raw.T, ((0, pad), (0, 0))),
         jnp.pad(a_log, (0, pad))[None, :],
         jnp.pad(d_skip, (0, pad))[None, :],
-        own_c,
-        width,
-    )
-    zones_c = [zone_shift(own_c, k) for k in shifts]
+        x_inner,
+    )
     side_c = side_swap(own_c)
-    others_b = side_swap(pack(zones_b, own_decay, side_b))
-    others_c = side_swap(pack(zones_c, side_c))
-
-    def plan(per):
-        first = [(0, 0, False, 0), (1, 0, True, 0)]
-        near = [(k + 1, 0, False, k) for k in shifts]
-        return first + near + [(len(near) + 2, (k - 1) * per, True, k) for k in shifts]
-
-    plan_b, plan_c = plan(own_b.shape[0]), plan(own_rows)
+    cat_b, pair_c = pack(zones_b, own_c, side_c, xs_first, side_b)
+    others_b = side_swap(cat_b)
+    pairs_c = [zone_shift(pair_c, k) for k in shifts]
+    per = own_b.shape[0]
     sources_b = [own_b, side_b, *zones_b, others_b]
-    sources_c = [own_c, side_c, *zones_c, others_c]
+    plan_b = [(0, 0, False, 0), (1, 0, True, 0)]
+    plan_b += [(k + 1, 0, False, k) for k in shifts]
+    plan_b += [(len(zones_b) + 2, (k - 1) * per, True, k) for k in shifts]
+    sources_c = [pair_c, *pairs_c]
+    plan_c = [(k, 0, False, k) for k in range(len(sources_c))]
+    plan_c += [(k, own_rows, True, k) for k in range(len(sources_c))]
     bias = conv_bias[None, :]
-    xs_first, xs_later = scale(x_inner, q)
-    partner_decay = own_decay
-    if seq_size == 4:
-        partner_decay = lax.ppermute(own_decay, "seq", SWAP)
     b_act, first_b, last_rows = activate(
         place, sources_b, plan_b, True, conv_weight, bias, own_rows, [xs_first]
     )
     rims = lax.ppermute(last_rows, "seq", [(i, i + 1) for i in range(seq_size - 1)])
     starts, later = later_states(b_act, xs_later, dec)
-    b_act, state_0, kept, sent = first_state(
-        place, b_act, first_b, rims, conv_weight, bias, xs_first, dec, later, [others_c]
+    b_act, state_0, kept, *sent = first_state(
+        place, b_act, first_b, rims, conv_weight, bias, xs_first, dec, later, own_decay
     )
     c_act, _, _ = activate(place, [*sources_c, rims], plan_c, False, conv_weight, bias, own_rows)
     local, z_held = inner(c_act, b_act, x_inner, z_gate, q, brow, starts, state_0, dec)
-    state_one, state_two = chained_state(place, kept, sent, own_decay, partner_decay, local)
+    state_one, state_two = chained_state(place, kept, sent, own_decay, local, pairs_c)
     gated, square_one = gate(place, c_act, local, z_held, q, state_one)
     gated, square_sum = gate(place, c_act, gated, z_held, q, state_two, square_one)
     column = sum([zone_shift(square_sum, k) for k in shifts], square_sum)

time: 80.5 us -> 76.6 us (0.952)
  starting transfers between devices: 31.7 us -> 24.4 us
  waiting for transfers between devices: 12.5 us -> 16 us
  local copies, waits for them, and re-layouts: 3.14 us -> 1.32 us
  Pallas kernels: 32.5 us -> 34.2 us
    ppermute x9, starting transfers between devices: 17.6 us -> 11.5 us  [zone_shift(): lax.ppermute(a, 'head', [(i, (i + 2 * k) % size) for i in range(size)])]
    ppermute x5 -> x4, waiting for transfers between devices: 2.47 us -> 6.88 us  [side_swap(): return lax.ppermute(a, 'head', [(i, i ^ 1) for i in range(size)])]
    pallas_call x1, Pallas kernels: 1.26 us -> 5.5 us  [rates(): pl.pallas_call(rates_kernel, out_shape=[kept_in_vmem((length, 128), F32),...]
    pallas_call x4 -> x2, Pallas kernels: 4.01 us -> 0.45 us  [the longest x1 0.42 us: meet(): pl.pallas_call(functools.partial(meet_kernel, len(got)), out_shape=[kept_...]
    ppermute x5 -> x4, starting transfers between devices: 7.09 us -> 5.12 us  [side_swap(): return lax.ppermute(a, 'head', [(i, i ^ 1) for i in range(size)])]
    unnamed x14 -> x10, local copies, waits for them, and re-layouts: 3.14 us -> 1.32 us
    pallas_call x1, Pallas kernels: 0.55 us -> 1.54 us  [prepare(): pl.pallas_call(prepare_kernel, out_shape=[jax.ShapeDtypeStruct((rows + RI...]
    ppermute x2 -> x4, starting transfers between devices: 2.36 us -> 2.8 us  [chained_state(): got = [lax.ppermute(piece, 'seq', SWAP) for piece in sent]]
  transfers between devices with their start and end apart: 19 -> 20, of which waited for: 5 -> 8; matrix products, arithmetic and copies ran while one was open for 0% -> 0% of each run, Pallas kernels for 31% -> 34%
where the time goes in v4:
time: 76.6 us; the launch traced here: 76.4 us
  Pallas kernels  34.2 us (45%)
  starting transfers between devices  24.4 us (32%)
  waiting for transfers between devices  16 us (21%)
  local copies, waits for them, and re-layouts  1.32 us (2%)
    pallas_call x1, Pallas kernels, inner(): pl.pallas_call(inner_kernel, out_shape=[kept_in_vmem((length, width), F32...  11.6 us
    ppermute x9, starting transfers between devices, zone_shift(): lax.ppermute(a, 'head', [(i, (i + 2 * k) % size) for i in range(size)])  11.5 us
    ppermute x9, waiting for transfers between devices, zone_shift(): lax.ppermute(a, 'head', [(i, (i + 2 * k) % size) for i in range(size)])  7.8 us
    ppermute x4, waiting for transfers between devices, side_swap(): return lax.ppermute(a, 'head', [(i, i ^ 1) for i in range(size)])  6.88 us
    pallas_call x2, Pallas kernels, gate(): pl.pallas_call(functools.partial(gate_kernel, len(before) > 0), out_shape...  6.46 us
    pallas_call x1, Pallas kernels, rates(): pl.pallas_call(rates_kernel, out_shape=[kept_in_vmem((length, 128), F32),...  5.5 us
    ppermute x4, starting transfers between devices, side_swap(): return lax.ppermute(a, 'head', [(i, i ^ 1) for i in range(size)])  5.12 us
    ppermute x1, starting transfers between devices, chained_state(): crossed = lax.ppermute(both, 'seq', [(0, 2), (1, 3)])  3.61 us
  transfers between devices with their start and end apart: 20, of which 8 were waited for; matrix products, arithmetic and copies ran while one was open for 0% of the time, Pallas kernels for 34%

profile of v4, /device:TPU:0, one launch (start us, length us, event | category | flops | bytes accessed | tf_op | source)
XLA Modules:
  0.0 76.4 jit_solution(9567335070963904785)
XLA Ops:
  0.1 1.5 %shard_map.91 = (bf16[208,256]{1,0:T(8,128)(2,1)S(1)}, bf16[192,256]{1,0:T(8,128)(2,1)S(1)}, s32[2]{0:T(128)S(4)}) custom-call(s32[2]{0:T(128)S(1)} %pad_add_fusion.place_ref, bf16[192,512]{1,0:T(8,128)(2,1)} %bc_ref.1), custom_call_target="tpu_custom_call" | custom-call | tf_op jit(solution)/shard_map/pallas_call | solution.py:199
  1.6 3.0 %collective-permute-start.4 = (bf16[208,256]{1,0:T(8,128)(2,1)S(1)}, bf16[208,256]{1,0:T(8,128)(2,1)S(1)}, u32[]{:S(2)}, u32[]{:S(2)}) collective-permute-start(bf16[208,256]{1,0:T(8,128)(2,1)S(1)} %get-tuple-element.41.refs_0_), channel_id=1, source_target_pairs={{0,1},{1,0},{2,3},{3,2},{4,5},{5,4},{6,7},{7,6},{8,9},{9,8},{10,11... | collective-permute-start | bytes 319496 | tf_op jit(solution)/shard_map/ppermute | solution.py:605
  4.7 3.6 %collective-permute-start.2 = (bf16[208,256]{1,0:T(8,128)(2,1)S(1)}, bf16[208,256]{1,0:T(8,128)(2,1)S(1)}, u32[]{:S(2)}, u32[]{:S(2)}) collective-permute-start(bf16[208,256]{1,0:T(8,128)(2,1)S(1)} %get-tuple-element.41.refs_0_), channel_id=1, source_target_pairs={{0,6},{1,7},{2,0},{3,1},{4,2},{5,3},{6,4},{7,5},{8,14},{9,15},{10,... | collective-permute-start | bytes 319496 | tf_op jit(solution)/shard_map/ppermute | solution.py:600
  8.3 1.0 %collective-permute-start = (bf16[208,256]{1,0:T(8,128)(2,1)S(1)}, bf16[208,256]{1,0:T(8,128)(2,1)S(1)}, u32[]{:S(2)}, u32[]{:S(2)}) collective-permute-start(bf16[208,256]{1,0:T(8,128)(2,1)S(1)} %get-tuple-element.41.refs_0_), channel_id=1, source_target_pairs={{0,2},{1,3},{2,4},{3,5},{4,6},{5,7},{6,0},{7,1},{8,10},{9,11},{10,... | collective-permute-start | bytes 319496 | tf_op jit(solution)/shard_map/ppermute | solution.py:600
  11.1 5.5 %shard_map.92 = (f32[1536,128]{1,0:T(8,128)S(1)}, f32[16,1536]{1,0:T(8,128)S(1)}, f32[16,2048]{1,0:T(8,128)S(1)}, f32[1,2048]{1,0:T(1,128)S(1)}, bf16[256,2048]{...) custom-call(f32[16,1536]{1,0:T(8,128)} %bitcast.13, f32[1,16]{1,0:T(1,128)S(1)} %bitcast.11, f32[1,16]{1,0:T(1,128)S(1)} %bitcast.12, ...), custom_call_target="tpu_custom_call" | custom-call | tf_op jit(solution)/shard_map/pallas_call | solution.py:150
  17.3 1.0 %collective-permute-start.8 = (bf16[624,256]{1,0:T(8,128)(2,1)S(1)}, bf16[624,256]{1,0:T(8,128)(2,1)S(1)}, u32[]{:S(2)}, u32[]{:S(2)}) collective-permute-start(bf16[624,256]{1,0:T(8,128)(2,1)S(1)} %get-tuple-element.45), channel_id=1, source_target_pairs={{0,1},{1,0},{2,3},{3,2},{4,5},{5,4},{6,7},{7,6},{8,9},{9,8},{10,11... | collective-permute-start | bytes 958472 | tf_op jit(solution)/shard_map/ppermute | solution.py:605
  18.3 2.8 %collective-permute-start.7 = (bf16[384,256]{1,0:T(8,128)(2,1)S(1)}, bf16[384,256]{1,0:T(8,128)(2,1)S(1)}, u32[]{:S(2)}, u32[]{:S(2)}) collective-permute-start(bf16[384,256]{1,0:T(8,128)(2,1)S(1)} %get-tuple-element.44.refs_0_), channel_id=1, source_target_pairs={{0,6},{1,7},{2,0},{3,1},{4,2},{5,3},{6,4},{7,5},{8,14},{9,15},{10,... | collective-permute-start | bytes 589832 | tf_op jit(solution)/shard_map/ppermute | solution.py:600
  21.1 1.1 %collective-permute-start.6 = (bf16[384,256]{1,0:T(8,128)(2,1)S(1)}, bf16[384,256]{1,0:T(8,128)(2,1)S(1)}, u32[]{:S(2)}, u32[]{:S(2)}) collective-permute-start(bf16[384,256]{1,0:T(8,128)(2,1)S(1)} %get-tuple-element.44.refs_0_), channel_id=1, source_target_pairs={{0,4},{1,5},{2,6},{3,7},{4,0},{5,1},{6,2},{7,3},{8,12},{9,13},{10,... | collective-permute-start | bytes 589832 | tf_op jit(solution)/shard_map/ppermute | solution.py:600
  22.3 3.7 %collective-permute-done.8.refs_5_ = bf16[624,256]{1,0:T(8,128)(2,1)S(1)} collective-permute-done((bf16[624,256]{1,0:T(8,128)(2,1)S(1)}, bf16[624,256]{1,0:T(8,128)(2,1)S(1)}, u32[]{:S(2)}, u32[]{:S(2)}) %collective-permute-start.8) | collective-permute-done | bytes 319520 | tf_op jit(solution)/shard_map/ppermute | solution.py:605
  26.1 1.1 %shard_map.94 = (bf16[1536,256]{1,0:T(8,128)(2,1)S(1)}, bf16[16,256]{1,0:T(8,128)(2,1)S(1)}, bf16[32,256]{1,0:T(8,128)(2,1)S(1)}) custom-call(s32[2]{0:T(128)S(4)} %get-tuple-element.40.me_ref.at_ref, f32[4,512]{1,0:T(4,128)S(1)} %copy-done, f32[1,512]{1,0:T(1,128)S(1)} %bitcast.7, bf16[208,256]{1,0:T(8,128)(2,1)S(1)} %get-tuple-element.41.refs_0_, ...), custom_call_target="tpu_custom_call" | custom-call | tf_op jit(solution)/shard_map/pallas_call | solution.py:274
  27.1 1.3 %collective-permute-start.9 = (bf16[32,256]{1,0:T(8,128)(2,1)S(1)}, bf16[32,256]{1,0:T(8,128)(2,1)S(1)}, u32[]{:S(2)}, u32[]{:S(2)}) collective-permute-start(bf16[32,256]{1,0:T(8,128)(2,1)S(1)} %get-tuple-element.46), channel_id=1, source_target_pairs={{0,8},{8,16},{16,24},{1,9},{9,17},{17,25},{2,10},{10,18},{18,26},{... | collective-permute-start | bytes 49160 | tf_op jit(solution)/shard_map/ppermute | solution.py:666
  28.4 2.2 %shard_map.96 = (bf16[5,256,2048]{2,1,0:T(8,128)(2,1)S(1)}, f32[256,2048]{1,0:T(8,128)S(1)}) custom-call(bf16[1536,256]{1,0:T(8,128)(2,1)S(1)} %get-tuple-element.48.b_ref, bf16[1280,2048]{1,0:T(8,128)(2,1)S(1)} %get-tuple-element.51.xs_ref, f32[16,2048]{1,0:T(8,128)S(1)} %get-tuple-element.50.dec_ref), custom_call_target="tpu_custom_call" | custom-call | tf_op jit(solution)/shard_map/pallas_call | solution.py:320
  31.3 2.3 %collective-permute-start.10 = (bf16[272,256]{1,0:T(8,128)(2,1)S(1)}, bf16[272,256]{1,0:T(8,128)(2,1)S(1)}, u32[]{:S(2)}, u32[]{:S(2)}) collective-permute-start(bf16[272,256]{1,0:T(8,128)(2,1)S(1)} %get-tuple-element.62), channel_id=1, source_target_pairs={{0,8},{8,0},{16,24},{24,16},{1,9},{9,1},{17,25},{25,17},{2,10},{10... | collective-permute-start | bytes 417800 | tf_op jit(solution)/shard_map/ppermute | solution.py:611
  34.1 3.7 %collective-permute-done.6.refs_2_.refs_5_ = bf16[384,256]{1,0:T(8,128)(2,1)S(1)} collective-permute-done((bf16[384,256]{1,0:T(8,128)(2,1)S(1)}, bf16[384,256]{1,0:T(8,128)(2,1)S(1)}, u32[]{:S(2)}, u32[]{:S(2)}) %collective-permute-start.6) | collective-permute-done | bytes 196640 | tf_op jit(solution)/shard_map/ppermute | solution.py:600
  37.8 1.3 %collective-permute-done.13.refs_3_ = bf16[272,256]{1,0:T(8,128)(2,1)S(1)} collective-permute-done((bf16[272,256]{1,0:T(8,128)(2,1)S(1)}, bf16[272,256]{1,0:T(8,128)(2,1)S(1)}, u32[]{:S(2)}, u32[]{:S(2)}) %collective-permute-start.13) | collective-permute-done | bytes 139296 | tf_op jit(solution)/shard_map/ppermute | solution.py:611
  39.6 3.6 %collective-permute-start.14 = (bf16[256,1024]{1,0:T(8,128)(2,1)S(1)}, bf16[256,1024]{1,0:T(8,128)(2,1)S(1)}, u32[]{:S(2)}, u32[]{:S(2)}) collective-permute-start(bf16[256,1024]{1,0:T(8,128)(2,1)S(1)} %get-tuple-element.66), channel_id=1, source_target_pairs={{0,16},{8,24},{1,17},{9,25},{2,18},{10,26},{3,19},{11,27},{4,20},{... | collective-permute-start | bytes 1572872 | tf_op jit(solution)/shard_map/ppermute | solution.py:613
  43.2 1.4 %shard_map.95 = (bf16[1536,256]{1,0:T(8,128)(2,1)S(1)}, bf16[16,256]{1,0:T(8,128)(2,1)}, bf16[32,256]{1,0:T(8,128)(2,1)}) custom-call(s32[2]{0:T(128)S(4)} %get-tuple-element.40.me_ref.at_ref, f32[4,512]{1,0:T(4,128)S(1)} %copy-done, f32[1,512]{1,0:T(1,128)S(1)} %bitcast.9, bf16[384,256]{1,0:T(8,128)(2,1)S(1)} %get-tuple-element.44.refs_0_, ...), custom_call_target="tpu_custom_call" | custom-call | tf_op jit(solution)/shard_map/pallas_call | solution.py:274
  44.6 11.6 %shard_map.98 = (f32[1536,2048]{1,0:T(8,128)S(1)}, bf16[1536,2048]{1,0:T(8,128)(2,1)S(1)}) custom-call(bf16[1536,256]{1,0:T(8,128)(2,1)S(1)} %get-tuple-element.47.c_ref, bf16[1536,256]{1,0:T(8,128)(2,1)S(1)} %get-tuple-element.54.b_ref, bf16[1536,2048]{1,0:T(8,128)(2,1)} %x_ref.3, bf16[1536,2048]{1,0:T(8,128)(2,1)} %z_ref.1, ...), custom_call_target="tpu_custom_call" | custom-call | bytes 251658240 | tf_op jit(solution)/shard_map/pallas_call | solution.py:498
  56.7 3.3 %shard_map.101 = (f32[1536,2048]{1,0:T(8,128)S(1)}, f32[1,1536]{1,0:T(1,128)S(1)}) custom-call(s32[2]{0:T(128)S(4)} %get-tuple-element.40.me_ref.at_ref, bf16[1536,256]{1,0:T(8,128)(2,1)S(1)} %get-tuple-element.47.c_ref, f32[1536,2048]{1,0:T(8,128)S(1)} %get-tuple-element.59.refs_0_.y_ref, ...), custom_call_target="tpu_custom_call", output_to_operand_aliasing={{0}: (2, {})} | custom-call | bytes 25165824 | tf_op jit(solution)/shard_map/pallas_call | solution.py:543
  60.0 3.2 %shard_map.102 = (f32[1536,2048]{1,0:T(8,128)S(1)}, f32[1,1536]{1,0:T(1,128)S(1)}) custom-call(s32[2]{0:T(128)S(4)} %get-tuple-element.40.me_ref.at_ref, bf16[1536,256]{1,0:T(8,128)(2,1)S(1)} %get-tuple-element.47.c_ref, f32[1536,2048]{1,0:T(8,128)S(1)} %get-tuple-element.70.y_ref, ...), custom_call_target="tpu_custom_call", output_to_operand_aliasing={{0}: (2, {})} | custom-call | bytes 25165824 | tf_op jit(solution)/shard_map/pallas_call | solution.py:543
  64.1 1.9 %collective-permute-start.16 = (f32[1,1536]{1,0:T(1,128)S(1)}, f32[1,1536]{1,0:T(1,128)S(1)}, u32[]{:S(2)}, u32[]{:S(2)}) collective-permute-start(f32[1,1536]{1,0:T(1,128)S(1)} %get-tuple-element.74), channel_id=1, source_target_pairs={{0,2},{1,3},{2,4},{3,5},{4,6},{5,7},{6,0},{7,1},{8,10},{9,11},{10,... | collective-permute-start | bytes 18440 | tf_op jit(solution)/shard_map/ppermute | solution.py:600
  67.8 1.7 %collective-permute-done.16 = f32[1,1536]{1,0:T(1,128)S(1)} collective-permute-done((f32[1,1536]{1,0:T(1,128)S(1)}, f32[1,1536]{1,0:T(1,128)S(1)}, u32[]{:S(2)}, u32[]{:S(2)}) %collective-permute-start.16) | collective-permute-done | bytes 6176 | tf_op jit(solution)/shard_map/ppermute | solution.py:600
  70.1 3.1 %collective-permute-done.19.two_ref = f32[1,1536]{1,0:T(1,128)S(1)} collective-permute-done((f32[1,1536]{1,0:T(1,128)S(1)}, f32[1,1536]{1,0:T(1,128)S(1)}, u32[]{:S(2)}, u32[]{:S(2)}) %collective-permute-start.19) | collective-permute-done | bytes 6176 | tf_op jit(solution)/shard_map/ppermute | solution.py:605
  73.2 3.0 %shard_map.103 = bf16[1536,2048]{1,0:T(8,128)(2,1)} custom-call(f32[1536,2048]{1,0:T(8,128)S(1)} %get-tuple-element.73.g_ref, f32[1,1536]{1,0:T(1,128)S(1)} %add_add_fusion.one_ref, f32[1,1536]{1,0:T(1,128)S(1)} %collective-permute-done.19.two_ref, f32[1,2048]{1,0:T(1,128)S(1)} %bitcast.10), custom_call_target="tpu_custom_call" | custom-call | tf_op jit(solution)/shard_map/pallas_call | solution.py:581
  (41 shorter events, 7.9 us)
Async XLA Ops:
  0.0 26.1 %copy-start = (f32[4,512]{1,0:T(4,128)S(1)}, f32[4,512]{1,0:T(4,128)}, u32[]{:S(2)}) copy-start(f32[4,512]{1,0:T(4,128)} %weight_ref.5) | copy-start | bytes 24580
  0.0 26.1 %copy-start.1 = (f32[512]{0:T(512)S(1)}, f32[512]{0:T(512)}, u32[]{:S(2)}) copy-start(f32[512]{0:T(512)} %param.13) | copy-start | bytes 6148
  1.6 15.0 %collective-permute-start.4 = (bf16[208,256]{1,0:T(8,128)(2,1)S(1)}, bf16[208,256]{1,0:T(8,128)(2,1)S(1)}, u32[]{:S(2)}, u32[]{:S(2)}) collective-permute-start(bf16[208,256]{1,0:T(8,128)(2,1)S(1)} %get-tuple-element.41.refs_0_), channel_id=1, source_target_pairs={{0,1},{1,0},{2,3},{3,2},{4,5},{5,4},{6,7},{7,6},{8,9},{9,8},{10,11... | collective-permute-start | bytes 319496 | tf_op jit(solution)/shard_map/ppermute | solution.py:605
  4.7 12.0 %collective-permute-start.2 = (bf16[208,256]{1,0:T(8,128)(2,1)S(1)}, bf16[208,256]{1,0:T(8,128)(2,1)S(1)}, u32[]{:S(2)}, u32[]{:S(2)}) collective-permute-start(bf16[208,256]{1,0:T(8,128)(2,1)S(1)} %get-tuple-element.41.refs_0_), channel_id=1, source_target_pairs={{0,6},{1,7},{2,0},{3,1},{4,2},{5,3},{6,4},{7,5},{8,14},{9,15},{10,... | collective-permute-start | bytes 319496 | tf_op jit(solution)/shard_map/ppermute | solution.py:600
  8.3 9.0 %collective-permute-start.1 = (bf16[208,256]{1,0:T(8,128)(2,1)S(1)}, bf16[208,256]{1,0:T(8,128)(2,1)S(1)}, u32[]{:S(2)}, u32[]{:S(2)}) collective-permute-start(bf16[208,256]{1,0:T(8,128)(2,1)S(1)} %get-tuple-element.41.refs_0_), channel_id=1, source_target_pairs={{0,4},{1,5},{2,6},{3,7},{4,0},{5,1},{6,2},{7,3},{8,12},{9,13},{10,... | collective-permute-start | bytes 319496 | tf_op jit(solution)/shard_map/ppermute | solution.py:600
  8.3 9.0 %collective-permute-start = (bf16[208,256]{1,0:T(8,128)(2,1)S(1)}, bf16[208,256]{1,0:T(8,128)(2,1)S(1)}, u32[]{:S(2)}, u32[]{:S(2)}) collective-permute-start(bf16[208,256]{1,0:T(8,128)(2,1)S(1)} %get-tuple-element.41.refs_0_), channel_id=1, source_target_pairs={{0,2},{1,3},{2,4},{3,5},{4,6},{5,7},{6,0},{7,1},{8,10},{9,11},{10,... | collective-permute-start | bytes 319496 | tf_op jit(solution)/shard_map/ppermute | solution.py:600
  9.3 7.3 %collective-permute-start.3 = (bf16[192,256]{1,0:T(8,128)(2,1)S(1)}, bf16[192,256]{1,0:T(8,128)(2,1)S(1)}, u32[]{:S(2)}, u32[]{:S(2)}) collective-permute-start(bf16[192,256]{1,0:T(8,128)(2,1)S(1)} %get-tuple-element.42.refs_3_), channel_id=1, source_target_pairs={{0,1},{1,0},{2,3},{3,2},{4,5},{5,4},{6,7},{7,6},{8,9},{9,8},{10,11... | collective-permute-start | bytes 294920 | tf_op jit(solution)/shard_map/ppermute | solution.py:605
  9.8 0.7 copy-start.3
  17.3 8.8 %collective-permute-start.8 = (bf16[624,256]{1,0:T(8,128)(2,1)S(1)}, bf16[624,256]{1,0:T(8,128)(2,1)S(1)}, u32[]{:S(2)}, u32[]{:S(2)}) collective-permute-start(bf16[624,256]{1,0:T(8,128)(2,1)S(1)} %get-tuple-element.45), channel_id=1, source_target_pairs={{0,1},{1,0},{2,3},{3,2},{4,5},{5,4},{6,7},{7,6},{8,9},{9,8},{10,11... | collective-permute-start | bytes 958472 | tf_op jit(solution)/shard_map/ppermute | solution.py:605
  18.3 15.4 %collective-permute-start.7 = (bf16[384,256]{1,0:T(8,128)(2,1)S(1)}, bf16[384,256]{1,0:T(8,128)(2,1)S(1)}, u32[]{:S(2)}, u32[]{:S(2)}) collective-permute-start(bf16[384,256]{1,0:T(8,128)(2,1)S(1)} %get-tuple-element.44.refs_0_), channel_id=1, source_target_pairs={{0,6},{1,7},{2,0},{3,1},{4,2},{5,3},{6,4},{7,5},{8,14},{9,15},{10,... | collective-permute-start | bytes 589832 | tf_op jit(solution)/shard_map/ppermute | solution.py:600
  21.1 16.7 %collective-permute-start.6 = (bf16[384,256]{1,0:T(8,128)(2,1)S(1)}, bf16[384,256]{1,0:T(8,128)(2,1)S(1)}, u32[]{:S(2)}, u32[]{:S(2)}) collective-permute-start(bf16[384,256]{1,0:T(8,128)(2,1)S(1)} %get-tuple-element.44.refs_0_), channel_id=1, source_target_pairs={{0,4},{1,5},{2,6},{3,7},{4,0},{5,1},{6,2},{7,3},{8,12},{9,13},{10,... | collective-permute-start | bytes 589832 | tf_op jit(solution)/shard_map/ppermute | solution.py:600
  22.2 15.6 %collective-permute-start.5 = (bf16[384,256]{1,0:T(8,128)(2,1)S(1)}, bf16[384,256]{1,0:T(8,128)(2,1)S(1)}, u32[]{:S(2)}, u32[]{:S(2)}) collective-permute-start(bf16[384,256]{1,0:T(8,128)(2,1)S(1)} %get-tuple-element.44.refs_0_), channel_id=1, source_target_pairs={{0,2},{1,3},{2,4},{3,5},{4,6},{5,7},{6,0},{7,1},{8,10},{9,11},{10,... | collective-permute-start | bytes 589832 | tf_op jit(solution)/shard_map/ppermute | solution.py:600
  27.1 3.5 %collective-permute-start.9 = (bf16[32,256]{1,0:T(8,128)(2,1)S(1)}, bf16[32,256]{1,0:T(8,128)(2,1)S(1)}, u32[]{:S(2)}, u32[]{:S(2)}) collective-permute-start(bf16[32,256]{1,0:T(8,128)(2,1)S(1)} %get-tuple-element.46), channel_id=1, source_target_pairs={{0,8},{8,16},{16,24},{1,9},{9,17},{17,25},{2,10},{10,18},{18,26},{... | collective-permute-start | bytes 49160 | tf_op jit(solution)/shard_map/ppermute | solution.py:666
  31.3 6.5 %collective-permute-start.10 = (bf16[272,256]{1,0:T(8,128)(2,1)S(1)}, bf16[272,256]{1,0:T(8,128)(2,1)S(1)}, u32[]{:S(2)}, u32[]{:S(2)}) collective-permute-start(bf16[272,256]{1,0:T(8,128)(2,1)S(1)} %get-tuple-element.62), channel_id=1, source_target_pairs={{0,8},{8,0},{16,24},{24,16},{1,9},{9,1},{17,25},{25,17},{2,10},{10... | collective-permute-start | bytes 417800 | tf_op jit(solution)/shard_map/ppermute | solution.py:611
  33.6 4.3 %collective-permute-start.11 = (bf16[272,256]{1,0:T(8,128)(2,1)S(1)}, bf16[272,256]{1,0:T(8,128)(2,1)S(1)}, u32[]{:S(2)}, u32[]{:S(2)}) collective-permute-start(bf16[272,256]{1,0:T(8,128)(2,1)S(1)} %get-tuple-element.63), channel_id=1, source_target_pairs={{0,8},{8,0},{16,24},{24,16},{1,9},{9,1},{17,25},{25,17},{2,10},{10... | collective-permute-start | bytes 417800 | tf_op jit(solution)/shard_map/ppermute | solution.py:611
  33.6 4.2 %collective-permute-start.12 = (bf16[272,256]{1,0:T(8,128)(2,1)S(1)}, bf16[272,256]{1,0:T(8,128)(2,1)S(1)}, u32[]{:S(2)}, u32[]{:S(2)}) collective-permute-start(bf16[272,256]{1,0:T(8,128)(2,1)S(1)} %get-tuple-element.64), channel_id=1, source_target_pairs={{0,8},{8,0},{16,24},{24,16},{1,9},{9,1},{17,25},{25,17},{2,10},{10... | collective-permute-start | bytes 417800 | tf_op jit(solution)/shard_map/ppermute | solution.py:611
  37.8 1.4 %collective-permute-start.13 = (bf16[272,256]{1,0:T(8,128)(2,1)S(1)}, bf16[272,256]{1,0:T(8,128)(2,1)S(1)}, u32[]{:S(2)}, u32[]{:S(2)}) collective-permute-start(bf16[272,256]{1,0:T(8,128)(2,1)S(1)} %get-tuple-element.65), channel_id=1, source_target_pairs={{0,8},{8,0},{16,24},{24,16},{1,9},{9,1},{17,25},{25,17},{2,10},{10... | collective-permute-start | bytes 417800 | tf_op jit(solution)/shard_map/ppermute | solution.py:611
  39.6 16.6 %collective-permute-start.14 = (bf16[256,1024]{1,0:T(8,128)(2,1)S(1)}, bf16[256,1024]{1,0:T(8,128)(2,1)S(1)}, u32[]{:S(2)}, u32[]{:S(2)}) collective-permute-start(bf16[256,1024]{1,0:T(8,128)(2,1)S(1)} %get-tuple-element.66), channel_id=1, source_target_pairs={{0,16},{8,24},{1,17},{9,25},{2,18},{10,26},{3,19},{11,27},{4,20},{... | collective-permute-start | bytes 1572872 | tf_op jit(solution)/shard_map/ppermute | solution.py:613
  56.6 3.4 %collective-permute-start.15 = (bf16[256,1024]{1,0:T(8,128)(2,1)S(1)}, bf16[256,1024]{1,0:T(8,128)(2,1)S(1)}, u32[]{:S(2)}, u32[]{:S(2)}) collective-permute-start(bf16[256,1024]{1,0:T(8,128)(2,1)S(1)} %get-tuple-element.71), channel_id=1, source_target_pairs={{0,8},{8,0},{16,24},{24,16},{1,9},{9,1},{17,25},{25,17},{2,10},{10... | collective-permute-start | bytes 1572872 | tf_op jit(solution)/shard_map/ppermute | solution.py:615
  60.0 13.2 %copy-start.2 = (f32[2048]{0:T(1024)S(1)}, f32[2048]{0:T(1024)}, u32[]{:S(2)}) copy-start(f32[2048]{0:T(1024)} %param.17) | copy-start | bytes 24580
  63.2 3.7 %collective-permute-start.18 = (f32[1,1536]{1,0:T(1,128)S(1)}, f32[1,1536]{1,0:T(1,128)S(1)}, u32[]{:S(2)}, u32[]{:S(2)}) collective-permute-start(f32[1,1536]{1,0:T(1,128)S(1)} %get-tuple-element.74), channel_id=1, source_target_pairs={{0,6},{1,7},{2,0},{3,1},{4,2},{5,3},{6,4},{7,5},{8,14},{9,15},{10,... | collective-permute-start | bytes 18440 | tf_op jit(solution)/shard_map/ppermute | solution.py:600
  63.2 4.6 %collective-permute-start.17 = (f32[1,1536]{1,0:T(1,128)S(1)}, f32[1,1536]{1,0:T(1,128)S(1)}, u32[]{:S(2)}, u32[]{:S(2)}) collective-permute-start(f32[1,1536]{1,0:T(1,128)S(1)} %get-tuple-element.74), channel_id=1, source_target_pairs={{0,4},{1,5},{2,6},{3,7},{4,0},{5,1},{6,2},{7,3},{8,12},{9,13},{10,... | collective-permute-start | bytes 18440 | tf_op jit(solution)/shard_map/ppermute | solution.py:600
  64.1 5.4 %collective-permute-start.16 = (f32[1,1536]{1,0:T(1,128)S(1)}, f32[1,1536]{1,0:T(1,128)S(1)}, u32[]{:S(2)}, u32[]{:S(2)}) collective-permute-start(f32[1,1536]{1,0:T(1,128)S(1)} %get-tuple-element.74), channel_id=1, source_target_pairs={{0,2},{1,3},{2,4},{3,5},{4,6},{5,7},{6,0},{7,1},{8,10},{9,11},{10,... | collective-permute-start | bytes 18440 | tf_op jit(solution)/shard_map/ppermute | solution.py:600
  69.5 3.7 %collective-permute-start.19 = (f32[1,1536]{1,0:T(1,128)S(1)}, f32[1,1536]{1,0:T(1,128)S(1)}, u32[]{:S(2)}, u32[]{:S(2)}) collective-permute-start(f32[1,1536]{1,0:T(1,128)S(1)} %add_add_fusion.one_ref), channel_id=1, source_target_pairs={{0,1},{1,0},{2,3},{3,2},{4,5},{5,4},{6,7},{7,6},{8,9},{9,8},{10,11... | collective-permute-start | bytes 18440 | tf_op jit(solution)/shard_map/ppermute | solution.py:605
  (1 other events, 0.7 us)

commit v5 on v4

--- a/solution.py
+++ b/solution.py
@@ -249,7 +249,7 @@
         raw[0:RIM, :] = sources[-1][RIM : 2 * RIM, :]
     for index, start, side, shift in plan:
         ref = sources[index]
-        owner = lax.rem((partner if side else me) - 2 * shift + size, size)
+        owner = jnp.bitwise_xor(partner if side else me, 2 * shift)
         at = pl.multiple_of(RIM + owner * own_rows, 16)
         raw[pl.ds(at, own_rows), :] = ref[start : start + own_rows, :]
         if is_b:
@@ -441,7 +441,7 @@
     c_ref, b_ref, x_ref, z_ref, q_ref, brow_ref, starts_ref, state_ref, dec_ref,
     out_ref, z_out, expand_ref, held, sems, z_sem,
 ):
-    stream_in(x_ref, held, sems)
+    copies = stream_in(x_ref, held, sems)
     z_copy = pltpu.make_async_copy(z_ref, z_out, z_sem)
     z_copy.start()
     half = BLOCK // 2
@@ -452,20 +452,25 @@
         jnp.int32, (half, half), 1
     )
 
-    @pl.loop(0, block_count)
-    def _(c):
-        at = pl.multiple_of(c * BLOCK, BLOCK)
-        rows = pl.ds(at, BLOCK)
-        pltpu.make_async_copy(x_ref.at[rows, :], held.at[c], sems.at[c]).wait()
+    for c in range(block_count):
+        rows = slice(c * BLOCK, (c + 1) * BLOCK)
         c_block = c_ref[rows, :]
+        q_block = q_ref[rows, :]
+        if c > 0:
+            q_short = q_block.astype(BF16)
+            for columns in tiles(x_ref.shape[1], 256):
+                decay = dec_ref[block_count + c : block_count + c + 1, columns]
+                start = starts_ref[c - 1, :, columns].astype(F32) + decay * state_ref[:, columns]
+                grown = jnp.dot(q_short, expand_ref[:, columns], preferred_element_type=F32)
+                carried = jnp.dot(c_block, start.astype(BF16), preferred_element_type=F32)
+                out_ref[rows, columns] = grown * carried
+        copies[c].wait()
         gram = lax.dot_general(
             c_block, b_ref[rows, :], (((1,), (1,)), ((), ())), preferred_element_type=F32
         )
         gram_00 = jnp.where(lower, gram[:half, :half], 0.0)
         gram_10 = gram[half:, :half]
         gram_11 = jnp.where(lower, gram[half:, half:], 0.0)
-        q_block = q_ref[rows, :]
-        q_short = q_block.astype(BF16)
         for h in range(head_count):
             columns = slice(h * HEAD_DIM, (h + 1) * HEAD_DIM)
             rise = jnp.broadcast_to(q_block[:, h : h + 1], (BLOCK, half))
@@ -477,18 +482,11 @@
             top = jnp.dot(w_00.astype(BF16), x_head[:half], preferred_element_type=F32)
             low = jnp.concatenate([w_10.astype(BF16), w_11.astype(BF16)], axis=1)
             bottom = jnp.dot(low, x_head, preferred_element_type=F32)
-            out_ref[rows, columns] = jnp.concatenate([top, bottom], axis=0) + dec_ref[
-                2 * block_count + 1 : 2 * block_count + 2, columns
-            ] * x_head.astype(F32)
-
-        @pl.when(c > 0)
-        def _():
-            for columns in tiles(x_ref.shape[1]):
-                decay = dec_ref[pl.ds(block_count + c, 1), columns]
-                start = starts_ref[c - 1, :, columns].astype(F32) + decay * state_ref[:, columns]
-                grown = jnp.dot(q_short, expand_ref[:, columns], preferred_element_type=F32)
-                carried = jnp.dot(c_block, start.astype(BF16), preferred_element_type=F32)
-                out_ref[rows, columns] += grown * carried
+            skip = dec_ref[2 * block_count + 1 : 2 * block_count + 2, columns] * x_head.astype(F32)
+            own = jnp.concatenate([top, bottom], axis=0) + skip
+            if c > 0:
+                own = own + out_ref[rows, columns]
+            out_ref[rows, columns] = own
 
     z_copy.wait()
 
@@ -595,9 +593,9 @@
 SWAP = [(0, 1), (1, 0), (2, 3), (3, 2)]
 
 
-def zone_shift(a, k):
+def zone_swap(a, k):
     size = lax.axis_size("head")
-    return lax.ppermute(a, "head", [(i, (i + 2 * k) % size) for i in range(size)])
+    return lax.ppermute(a, "head", [(i, i ^ (2 * k)) for i in range(size)])
 
 
 def side_swap(a):
@@ -638,7 +636,7 @@
         first_channel = (1 - lax.rem(lax.axis_index("seq"), 2)) * (width // 2)
     place = jnp.stack([lax.axis_index("head"), first_channel]).astype(jnp.int32)
     own_b, own_c, place = prepare(place, bc_raw)
-    zones_b = [zone_shift(own_b, k) for k in shifts]
+    zones_b = [zone_swap(own_b, k) for k in shifts]
     side_b = side_swap(own_b)
     pad = SLOT - head_count
     q, brow, dec, own_decay, xs_first, xs_later = rates(
@@ -650,7 +648,7 @@
     side_c = side_swap(own_c)
     cat_b, pair_c = pack(zones_b, own_c, side_c, xs_first, side_b)
     others_b = side_swap(cat_b)
-    pairs_c = [zone_shift(pair_c, k) for k in shifts]
+    pairs_c = [zone_swap(pair_c, k) for k in shifts]
     per = own_b.shape[0]
     sources_b = [own_b, side_b, *zones_b, others_b]
     plan_b = [(0, 0, False, 0), (1, 0, True, 0)]
@@ -673,7 +671,7 @@
     state_one, state_two = chained_state(place, kept, sent, own_decay, local, pairs_c)
     gated, square_one = gate(place, c_act, local, z_held, q, state_one)
     gated, square_sum = gate(place, c_act, gated, z_held, q, state_two, square_one)
-    column = sum([zone_shift(square_sum, k) for k in shifts], square_sum)
+    column = sum([zone_swap(square_sum, k) for k in shifts], square_sum)
     return norm(gated, column, side_swap(column), norm_gain[None, :])
 
 

time: 76.6 us -> 76 us (level)
  waiting for transfers between devices: 16 us -> 14 us
  starting transfers between devices: 24.4 us -> 25.9 us
    ppermute x9, starting transfers between devices: 11.5 us -> 13.2 us  [zone_swap(): return lax.ppermute(a, 'head', [(i, i ^ 2 * k) for i in range(size)])]
    ppermute x9, waiting for transfers between devices: 7.8 us -> 6.35 us  [zone_swap(): return lax.ppermute(a, 'head', [(i, i ^ 2 * k) for i in range(size)])]
  transfers between devices with their start and end apart: 20 -> 20, of which waited for: 8 -> 7; matrix products, arithmetic and copies ran while one was open for 0% -> 0% of each run, Pallas kernels for 34% -> 34%
where the time goes in v5:
time: 76 us; the launch traced here: 75.8 us
  Pallas kernels  34.1 us (45%)
  starting transfers between devices  25.9 us (34%)
  waiting for transfers between devices  14 us (18%)
  local copies, waits for them, and re-layouts  1.32 us (2%)
    ppermute x9, starting transfers between devices, zone_swap(): return lax.ppermute(a, 'head', [(i, i ^ 2 * k) for i in range(size)])  13.2 us
    pallas_call x1, Pallas kernels, inner(): pl.pallas_call(inner_kernel, out_shape=[kept_in_vmem((length, width), F32...  11.3 us
    pallas_call x2, Pallas kernels, gate(): pl.pallas_call(functools.partial(gate_kernel, len(before) > 0), out_shape...  6.68 us
    ppermute x9, waiting for transfers between devices, zone_swap(): return lax.ppermute(a, 'head', [(i, i ^ 2 * k) for i in range(size)])  6.35 us
    ppermute x4, waiting for transfers between devices, side_swap(): return lax.ppermute(a, 'head', [(i, i ^ 1) for i in range(size)])  6.31 us
    pallas_call x1, Pallas kernels, rates(): pl.pallas_call(rates_kernel, out_shape=[kept_in_vmem((length, 128), F32),...  5.51 us
    ppermute x4, starting transfers between devices, side_swap(): return lax.ppermute(a, 'head', [(i, i ^ 1) for i in range(size)])  4.93 us
    ppermute x1, starting transfers between devices, chained_state(): crossed = lax.ppermute(both, 'seq', [(0, 2), (1, 3)])  3.61 us
  transfers between devices with their start and end apart: 20, of which 7 were waited for; matrix products, arithmetic and copies ran while one was open for 0% of the time, Pallas kernels for 34%

profile of v5, /device:TPU:0, one launch (start us, length us, event | category | flops | bytes accessed | tf_op | source)
XLA Modules:
  0.0 75.8 jit_solution(18444044567536773819)
XLA Ops:
  0.1 1.5 %shard_map.91 = (bf16[208,256]{1,0:T(8,128)(2,1)S(1)}, bf16[192,256]{1,0:T(8,128)(2,1)S(1)}, s32[2]{0:T(128)S(4)}) custom-call(s32[2]{0:T(128)S(1)} %pad_add_fusion.place_ref, bf16[192,512]{1,0:T(8,128)(2,1)} %bc_ref.1), custom_call_target="tpu_custom_call" | custom-call | tf_op jit(solution)/shard_map/pallas_call | solution.py:199
  1.6 3.0 %collective-permute-start.4 = (bf16[208,256]{1,0:T(8,128)(2,1)S(1)}, bf16[208,256]{1,0:T(8,128)(2,1)S(1)}, u32[]{:S(2)}, u32[]{:S(2)}) collective-permute-start(bf16[208,256]{1,0:T(8,128)(2,1)S(1)} %get-tuple-element.41.refs_0_), channel_id=1, source_target_pairs={{0,1},{1,0},{2,3},{3,2},{4,5},{5,4},{6,7},{7,6},{8,9},{9,8},{10,11... | collective-permute-start | bytes 319496 | tf_op jit(solution)/shard_map/ppermute | solution.py:603
  4.7 3.6 %collective-permute-start.2 = (bf16[208,256]{1,0:T(8,128)(2,1)S(1)}, bf16[208,256]{1,0:T(8,128)(2,1)S(1)}, u32[]{:S(2)}, u32[]{:S(2)}) collective-permute-start(bf16[208,256]{1,0:T(8,128)(2,1)S(1)} %get-tuple-element.41.refs_0_), channel_id=1, source_target_pairs={{0,6},{1,7},{2,4},{3,5},{4,2},{5,3},{6,0},{7,1},{8,14},{9,15},{10,... | collective-permute-start | bytes 319496 | tf_op jit(solution)/shard_map/ppermute | solution.py:598
  10.6 5.5 %shard_map.92 = (f32[1536,128]{1,0:T(8,128)S(1)}, f32[16,1536]{1,0:T(8,128)S(1)}, f32[16,2048]{1,0:T(8,128)S(1)}, f32[1,2048]{1,0:T(1,128)S(1)}, bf16[256,2048]{...) custom-call(f32[16,1536]{1,0:T(8,128)} %bitcast.13, f32[1,16]{1,0:T(1,128)S(1)} %bitcast.11, f32[1,16]{1,0:T(1,128)S(1)} %bitcast.12, ...), custom_call_target="tpu_custom_call" | custom-call | tf_op jit(solution)/shard_map/pallas_call | solution.py:150
  17.0 1.1 %collective-permute-start.8 = (bf16[624,256]{1,0:T(8,128)(2,1)S(1)}, bf16[624,256]{1,0:T(8,128)(2,1)S(1)}, u32[]{:S(2)}, u32[]{:S(2)}) collective-permute-start(bf16[624,256]{1,0:T(8,128)(2,1)S(1)} %get-tuple-element.45), channel_id=1, source_target_pairs={{0,1},{1,0},{2,3},{3,2},{4,5},{5,4},{6,7},{7,6},{8,9},{9,8},{10,11... | collective-permute-start | bytes 958472 | tf_op jit(solution)/shard_map/ppermute | solution.py:603
  18.1 3.6 %collective-permute-start.7 = (bf16[384,256]{1,0:T(8,128)(2,1)S(1)}, bf16[384,256]{1,0:T(8,128)(2,1)S(1)}, u32[]{:S(2)}, u32[]{:S(2)}) collective-permute-start(bf16[384,256]{1,0:T(8,128)(2,1)S(1)} %get-tuple-element.44.refs_0_), channel_id=1, source_target_pairs={{0,6},{1,7},{2,4},{3,5},{4,2},{5,3},{6,0},{7,1},{8,14},{9,15},{10,... | collective-permute-start | bytes 589832 | tf_op jit(solution)/shard_map/ppermute | solution.py:598
  22.5 3.2 %collective-permute-done.8.refs_5_ = bf16[624,256]{1,0:T(8,128)(2,1)S(1)} collective-permute-done((bf16[624,256]{1,0:T(8,128)(2,1)S(1)}, bf16[624,256]{1,0:T(8,128)(2,1)S(1)}, u32[]{:S(2)}, u32[]{:S(2)}) %collective-permute-start.8) | collective-permute-done | bytes 319520 | tf_op jit(solution)/shard_map/ppermute | solution.py:603
  25.6 1.0 %shard_map.94 = (bf16[1536,256]{1,0:T(8,128)(2,1)S(1)}, bf16[16,256]{1,0:T(8,128)(2,1)S(1)}, bf16[32,256]{1,0:T(8,128)(2,1)S(1)}) custom-call(s32[2]{0:T(128)S(4)} %get-tuple-element.40.me_ref.at_ref, f32[4,512]{1,0:T(4,128)S(1)} %copy-done, f32[1,512]{1,0:T(1,128)S(1)} %bitcast.7, bf16[208,256]{1,0:T(8,128)(2,1)S(1)} %get-tuple-element.41.refs_0_, ...), custom_call_target="tpu_custom_call" | custom-call | tf_op jit(solution)/shard_map/pallas_call | solution.py:274
  26.6 1.3 %collective-permute-start.9 = (bf16[32,256]{1,0:T(8,128)(2,1)S(1)}, bf16[32,256]{1,0:T(8,128)(2,1)S(1)}, u32[]{:S(2)}, u32[]{:S(2)}) collective-permute-start(bf16[32,256]{1,0:T(8,128)(2,1)S(1)} %get-tuple-element.46), channel_id=1, source_target_pairs={{0,8},{8,16},{16,24},{1,9},{9,17},{17,25},{2,10},{10,18},{18,26},{... | collective-permute-start | bytes 49160 | tf_op jit(solution)/shard_map/ppermute | solution.py:664
  27.9 2.2 %shard_map.96 = (bf16[5,256,2048]{2,1,0:T(8,128)(2,1)S(1)}, f32[256,2048]{1,0:T(8,128)S(1)}) custom-call(bf16[1536,256]{1,0:T(8,128)(2,1)S(1)} %get-tuple-element.48.b_ref, bf16[1280,2048]{1,0:T(8,128)(2,1)S(1)} %get-tuple-element.51.xs_ref, f32[16,2048]{1,0:T(8,128)S(1)} %get-tuple-element.50.dec_ref), custom_call_target="tpu_custom_call" | custom-call | tf_op jit(solution)/shard_map/pallas_call | solution.py:320
  30.8 2.3 %collective-permute-start.10 = (bf16[272,256]{1,0:T(8,128)(2,1)S(1)}, bf16[272,256]{1,0:T(8,128)(2,1)S(1)}, u32[]{:S(2)}, u32[]{:S(2)}) collective-permute-start(bf16[272,256]{1,0:T(8,128)(2,1)S(1)} %get-tuple-element.62), channel_id=1, source_target_pairs={{0,8},{8,0},{16,24},{24,16},{1,9},{9,1},{17,25},{25,17},{2,10},{10... | collective-permute-start | bytes 417800 | tf_op jit(solution)/shard_map/ppermute | solution.py:609
  33.6 3.0 %collective-permute-done.6.refs_2_.refs_5_ = bf16[384,256]{1,0:T(8,128)(2,1)S(1)} collective-permute-done((bf16[384,256]{1,0:T(8,128)(2,1)S(1)}, bf16[384,256]{1,0:T(8,128)(2,1)S(1)}, u32[]{:S(2)}, u32[]{:S(2)}) %collective-permute-start.6) | collective-permute-done | bytes 196640 | tf_op jit(solution)/shard_map/ppermute | solution.py:598
  36.7 1.3 %collective-permute-done.13.refs_3_ = bf16[272,256]{1,0:T(8,128)(2,1)S(1)} collective-permute-done((bf16[272,256]{1,0:T(8,128)(2,1)S(1)}, bf16[272,256]{1,0:T(8,128)(2,1)S(1)}, u32[]{:S(2)}, u32[]{:S(2)}) %collective-permute-start.13) | collective-permute-done | bytes 139296 | tf_op jit(solution)/shard_map/ppermute | solution.py:609
  38.4 3.6 %collective-permute-start.14 = (bf16[256,1024]{1,0:T(8,128)(2,1)S(1)}, bf16[256,1024]{1,0:T(8,128)(2,1)S(1)}, u32[]{:S(2)}, u32[]{:S(2)}) collective-permute-start(bf16[256,1024]{1,0:T(8,128)(2,1)S(1)} %get-tuple-element.66), channel_id=1, source_target_pairs={{0,16},{8,24},{1,17},{9,25},{2,18},{10,26},{3,19},{11,27},{4,20},{... | collective-permute-start | bytes 1572872 | tf_op jit(solution)/shard_map/ppermute | solution.py:611
  42.0 1.4 %shard_map.95 = (bf16[1536,256]{1,0:T(8,128)(2,1)S(1)}, bf16[16,256]{1,0:T(8,128)(2,1)}, bf16[32,256]{1,0:T(8,128)(2,1)}) custom-call(s32[2]{0:T(128)S(4)} %get-tuple-element.40.me_ref.at_ref, f32[4,512]{1,0:T(4,128)S(1)} %copy-done, f32[1,512]{1,0:T(1,128)S(1)} %bitcast.9, bf16[384,256]{1,0:T(8,128)(2,1)S(1)} %get-tuple-element.44.refs_0_, ...), custom_call_target="tpu_custom_call" | custom-call | tf_op jit(solution)/shard_map/pallas_call | solution.py:274
  43.5 11.3 %shard_map.98 = (f32[1536,2048]{1,0:T(8,128)S(1)}, bf16[1536,2048]{1,0:T(8,128)(2,1)S(1)}) custom-call(bf16[1536,256]{1,0:T(8,128)(2,1)S(1)} %get-tuple-element.47.c_ref, bf16[1536,256]{1,0:T(8,128)(2,1)S(1)} %get-tuple-element.54.b_ref, bf16[1536,2048]{1,0:T(8,128)(2,1)} %x_ref.3, bf16[1536,2048]{1,0:T(8,128)(2,1)} %z_ref.1, ...), custom_call_target="tpu_custom_call" | custom-call | bytes 251658240 | tf_op jit(solution)/shard_map/pallas_call | solution.py:496
  55.2 3.5 %shard_map.101 = (f32[1536,2048]{1,0:T(8,128)S(1)}, f32[1,1536]{1,0:T(1,128)S(1)}) custom-call(s32[2]{0:T(128)S(4)} %get-tuple-element.40.me_ref.at_ref, bf16[1536,256]{1,0:T(8,128)(2,1)S(1)} %get-tuple-element.47.c_ref, f32[1536,2048]{1,0:T(8,128)S(1)} %get-tuple-element.59.refs_0_.y_ref, ...), custom_call_target="tpu_custom_call", output_to_operand_aliasing={{0}: (2, {})} | custom-call | bytes 25165824 | tf_op jit(solution)/shard_map/pallas_call | solution.py:541
  58.7 3.2 %shard_map.102 = (f32[1536,2048]{1,0:T(8,128)S(1)}, f32[1,1536]{1,0:T(1,128)S(1)}) custom-call(s32[2]{0:T(128)S(4)} %get-tuple-element.40.me_ref.at_ref, bf16[1536,256]{1,0:T(8,128)(2,1)S(1)} %get-tuple-element.47.c_ref, f32[1536,2048]{1,0:T(8,128)S(1)} %get-tuple-element.70.y_ref, ...), custom_call_target="tpu_custom_call", output_to_operand_aliasing={{0}: (2, {})} | custom-call | bytes 25165824 | tf_op jit(solution)/shard_map/pallas_call | solution.py:541
  61.9 2.5 %collective-permute-start.18 = (f32[1,1536]{1,0:T(1,128)S(1)}, f32[1,1536]{1,0:T(1,128)S(1)}, u32[]{:S(2)}, u32[]{:S(2)}) collective-permute-start(f32[1,1536]{1,0:T(1,128)S(1)} %get-tuple-element.74), channel_id=1, source_target_pairs={{0,6},{1,7},{2,4},{3,5},{4,2},{5,3},{6,0},{7,1},{8,14},{9,15},{10,... | collective-permute-start | bytes 18440 | tf_op jit(solution)/shard_map/ppermute | solution.py:598
  64.4 2.0 %collective-permute-start.16 = (f32[1,1536]{1,0:T(1,128)S(1)}, f32[1,1536]{1,0:T(1,128)S(1)}, u32[]{:S(2)}, u32[]{:S(2)}) collective-permute-start(f32[1,1536]{1,0:T(1,128)S(1)} %get-tuple-element.74), channel_id=1, source_target_pairs={{0,2},{1,3},{2,0},{3,1},{4,6},{5,7},{6,4},{7,5},{8,10},{9,11},{10,... | collective-permute-start | bytes 18440 | tf_op jit(solution)/shard_map/ppermute | solution.py:598
  66.3 1.0 %collective-permute-done.18 = f32[1,1536]{1,0:T(1,128)S(1)} collective-permute-done((f32[1,1536]{1,0:T(1,128)S(1)}, f32[1,1536]{1,0:T(1,128)S(1)}, u32[]{:S(2)}, u32[]{:S(2)}) %collective-permute-start.18) | collective-permute-done | bytes 6176 | tf_op jit(solution)/shard_map/ppermute | solution.py:598
  67.4 1.5 %collective-permute-done.17 = f32[1,1536]{1,0:T(1,128)S(1)} collective-permute-done((f32[1,1536]{1,0:T(1,128)S(1)}, f32[1,1536]{1,0:T(1,128)S(1)}, u32[]{:S(2)}, u32[]{:S(2)}) %collective-permute-start.17) | collective-permute-done | bytes 6176 | tf_op jit(solution)/shard_map/ppermute | solution.py:598
  69.4 3.2 %collective-permute-done.19.two_ref = f32[1,1536]{1,0:T(1,128)S(1)} collective-permute-done((f32[1,1536]{1,0:T(1,128)S(1)}, f32[1,1536]{1,0:T(1,128)S(1)}, u32[]{:S(2)}, u32[]{:S(2)}) %collective-permute-start.19) | collective-permute-done | bytes 6176 | tf_op jit(solution)/shard_map/ppermute | solution.py:603
  72.6 3.0 %shard_map.103 = bf16[1536,2048]{1,0:T(8,128)(2,1)} custom-call(f32[1536,2048]{1,0:T(8,128)S(1)} %get-tuple-element.73.g_ref, f32[1,1536]{1,0:T(1,128)S(1)} %add_add_fusion.one_ref, f32[1,1536]{1,0:T(1,128)S(1)} %collective-permute-done.19.two_ref, f32[1,2048]{1,0:T(1,128)S(1)} %bitcast.10), custom_call_target="tpu_custom_call" | custom-call | tf_op jit(solution)/shard_map/pallas_call | solution.py:579
  (41 shorter events, 6.6 us)
Async XLA Ops:
  0.0 25.6 %copy-start = (f32[4,512]{1,0:T(4,128)S(1)}, f32[4,512]{1,0:T(4,128)}, u32[]{:S(2)}) copy-start(f32[4,512]{1,0:T(4,128)} %weight_ref.5) | copy-start | bytes 24580
  0.0 25.6 %copy-start.1 = (f32[512]{0:T(512)S(1)}, f32[512]{0:T(512)}, u32[]{:S(2)}) copy-start(f32[512]{0:T(512)} %param.13) | copy-start | bytes 6148
  1.6 14.6 %collective-permute-start.4 = (bf16[208,256]{1,0:T(8,128)(2,1)S(1)}, bf16[208,256]{1,0:T(8,128)(2,1)S(1)}, u32[]{:S(2)}, u32[]{:S(2)}) collective-permute-start(bf16[208,256]{1,0:T(8,128)(2,1)S(1)} %get-tuple-element.41.refs_0_), channel_id=1, source_target_pairs={{0,1},{1,0},{2,3},{3,2},{4,5},{5,4},{6,7},{7,6},{8,9},{9,8},{10,11... | collective-permute-start | bytes 319496 | tf_op jit(solution)/shard_map/ppermute | solution.py:603
  4.7 11.5 %collective-permute-start.2 = (bf16[208,256]{1,0:T(8,128)(2,1)S(1)}, bf16[208,256]{1,0:T(8,128)(2,1)S(1)}, u32[]{:S(2)}, u32[]{:S(2)}) collective-permute-start(bf16[208,256]{1,0:T(8,128)(2,1)S(1)} %get-tuple-element.41.refs_0_), channel_id=1, source_target_pairs={{0,6},{1,7},{2,4},{3,5},{4,2},{5,3},{6,0},{7,1},{8,14},{9,15},{10,... | collective-permute-start | bytes 319496 | tf_op jit(solution)/shard_map/ppermute | solution.py:598
  8.3 8.7 %collective-permute-start.1 = (bf16[208,256]{1,0:T(8,128)(2,1)S(1)}, bf16[208,256]{1,0:T(8,128)(2,1)S(1)}, u32[]{:S(2)}, u32[]{:S(2)}) collective-permute-start(bf16[208,256]{1,0:T(8,128)(2,1)S(1)} %get-tuple-element.41.refs_0_), channel_id=1, source_target_pairs={{0,4},{1,5},{2,6},{3,7},{4,0},{5,1},{6,2},{7,3},{8,12},{9,13},{10,... | collective-permute-start | bytes 319496 | tf_op jit(solution)/shard_map/ppermute | solution.py:598
  8.3 8.7 %collective-permute-start = (bf16[208,256]{1,0:T(8,128)(2,1)S(1)}, bf16[208,256]{1,0:T(8,128)(2,1)S(1)}, u32[]{:S(2)}, u32[]{:S(2)}) collective-permute-start(bf16[208,256]{1,0:T(8,128)(2,1)S(1)} %get-tuple-element.41.refs_0_), channel_id=1, source_target_pairs={{0,2},{1,3},{2,0},{3,1},{4,6},{5,7},{6,4},{7,5},{8,10},{9,11},{10,... | collective-permute-start | bytes 319496 | tf_op jit(solution)/shard_map/ppermute | solution.py:598
  9.0 7.1 %collective-permute-start.3 = (bf16[192,256]{1,0:T(8,128)(2,1)S(1)}, bf16[192,256]{1,0:T(8,128)(2,1)S(1)}, u32[]{:S(2)}, u32[]{:S(2)}) collective-permute-start(bf16[192,256]{1,0:T(8,128)(2,1)S(1)} %get-tuple-element.42.refs_3_), channel_id=1, source_target_pairs={{0,1},{1,0},{2,3},{3,2},{4,5},{5,4},{6,7},{7,6},{8,9},{9,8},{10,11... | collective-permute-start | bytes 294920 | tf_op jit(solution)/shard_map/ppermute | solution.py:603
  9.3 0.7 copy-start.3
  17.0 8.6 %collective-permute-start.8 = (bf16[624,256]{1,0:T(8,128)(2,1)S(1)}, bf16[624,256]{1,0:T(8,128)(2,1)S(1)}, u32[]{:S(2)}, u32[]{:S(2)}) collective-permute-start(bf16[624,256]{1,0:T(8,128)(2,1)S(1)} %get-tuple-element.45), channel_id=1, source_target_pairs={{0,1},{1,0},{2,3},{3,2},{4,5},{5,4},{6,7},{7,6},{8,9},{9,8},{10,11... | collective-permute-start | bytes 958472 | tf_op jit(solution)/shard_map/ppermute | solution.py:603
  18.1 15.1 %collective-permute-start.7 = (bf16[384,256]{1,0:T(8,128)(2,1)S(1)}, bf16[384,256]{1,0:T(8,128)(2,1)S(1)}, u32[]{:S(2)}, u32[]{:S(2)}) collective-permute-start(bf16[384,256]{1,0:T(8,128)(2,1)S(1)} %get-tuple-element.44.refs_0_), channel_id=1, source_target_pairs={{0,6},{1,7},{2,4},{3,5},{4,2},{5,3},{6,0},{7,1},{8,14},{9,15},{10,... | collective-permute-start | bytes 589832 | tf_op jit(solution)/shard_map/ppermute | solution.py:598
  21.7 15.0 %collective-permute-start.6 = (bf16[384,256]{1,0:T(8,128)(2,1)S(1)}, bf16[384,256]{1,0:T(8,128)(2,1)S(1)}, u32[]{:S(2)}, u32[]{:S(2)}) collective-permute-start(bf16[384,256]{1,0:T(8,128)(2,1)S(1)} %get-tuple-element.44.refs_0_), channel_id=1, source_target_pairs={{0,4},{1,5},{2,6},{3,7},{4,0},{5,1},{6,2},{7,3},{8,12},{9,13},{10,... | collective-permute-start | bytes 589832 | tf_op jit(solution)/shard_map/ppermute | solution.py:598
  21.7 15.0 %collective-permute-start.5 = (bf16[384,256]{1,0:T(8,128)(2,1)S(1)}, bf16[384,256]{1,0:T(8,128)(2,1)S(1)}, u32[]{:S(2)}, u32[]{:S(2)}) collective-permute-start(bf16[384,256]{1,0:T(8,128)(2,1)S(1)} %get-tuple-element.44.refs_0_), channel_id=1, source_target_pairs={{0,2},{1,3},{2,0},{3,1},{4,6},{5,7},{6,4},{7,5},{8,10},{9,11},{10,... | collective-permute-start | bytes 589832 | tf_op jit(solution)/shard_map/ppermute | solution.py:598
  26.6 3.5 %collective-permute-start.9 = (bf16[32,256]{1,0:T(8,128)(2,1)S(1)}, bf16[32,256]{1,0:T(8,128)(2,1)S(1)}, u32[]{:S(2)}, u32[]{:S(2)}) collective-permute-start(bf16[32,256]{1,0:T(8,128)(2,1)S(1)} %get-tuple-element.46), channel_id=1, source_target_pairs={{0,8},{8,16},{16,24},{1,9},{9,17},{17,25},{2,10},{10,18},{18,26},{... | collective-permute-start | bytes 49160 | tf_op jit(solution)/shard_map/ppermute | solution.py:664
  30.8 5.9 %collective-permute-start.10 = (bf16[272,256]{1,0:T(8,128)(2,1)S(1)}, bf16[272,256]{1,0:T(8,128)(2,1)S(1)}, u32[]{:S(2)}, u32[]{:S(2)}) collective-permute-start(bf16[272,256]{1,0:T(8,128)(2,1)S(1)} %get-tuple-element.62), channel_id=1, source_target_pairs={{0,8},{8,0},{16,24},{24,16},{1,9},{9,1},{17,25},{25,17},{2,10},{10... | collective-permute-start | bytes 417800 | tf_op jit(solution)/shard_map/ppermute | solution.py:609
  33.1 3.6 %collective-permute-start.11 = (bf16[272,256]{1,0:T(8,128)(2,1)S(1)}, bf16[272,256]{1,0:T(8,128)(2,1)S(1)}, u32[]{:S(2)}, u32[]{:S(2)}) collective-permute-start(bf16[272,256]{1,0:T(8,128)(2,1)S(1)} %get-tuple-element.63), channel_id=1, source_target_pairs={{0,8},{8,0},{16,24},{24,16},{1,9},{9,1},{17,25},{25,17},{2,10},{10... | collective-permute-start | bytes 417800 | tf_op jit(solution)/shard_map/ppermute | solution.py:609
  33.1 3.5 %collective-permute-start.12 = (bf16[272,256]{1,0:T(8,128)(2,1)S(1)}, bf16[272,256]{1,0:T(8,128)(2,1)S(1)}, u32[]{:S(2)}, u32[]{:S(2)}) collective-permute-start(bf16[272,256]{1,0:T(8,128)(2,1)S(1)} %get-tuple-element.64), channel_id=1, source_target_pairs={{0,8},{8,0},{16,24},{24,16},{1,9},{9,1},{17,25},{25,17},{2,10},{10... | collective-permute-start | bytes 417800 | tf_op jit(solution)/shard_map/ppermute | solution.py:609
  36.6 1.4 %collective-permute-start.13 = (bf16[272,256]{1,0:T(8,128)(2,1)S(1)}, bf16[272,256]{1,0:T(8,128)(2,1)S(1)}, u32[]{:S(2)}, u32[]{:S(2)}) collective-permute-start(bf16[272,256]{1,0:T(8,128)(2,1)S(1)} %get-tuple-element.65), channel_id=1, source_target_pairs={{0,8},{8,0},{16,24},{24,16},{1,9},{9,1},{17,25},{25,17},{2,10},{10... | collective-permute-start | bytes 417800 | tf_op jit(solution)/shard_map/ppermute | solution.py:609
  38.4 16.3 %collective-permute-start.14 = (bf16[256,1024]{1,0:T(8,128)(2,1)S(1)}, bf16[256,1024]{1,0:T(8,128)(2,1)S(1)}, u32[]{:S(2)}, u32[]{:S(2)}) collective-permute-start(bf16[256,1024]{1,0:T(8,128)(2,1)S(1)} %get-tuple-element.66), channel_id=1, source_target_pairs={{0,16},{8,24},{1,17},{9,25},{2,18},{10,26},{3,19},{11,27},{4,20},{... | collective-permute-start | bytes 1572872 | tf_op jit(solution)/shard_map/ppermute | solution.py:611
  55.1 3.6 %collective-permute-start.15 = (bf16[256,1024]{1,0:T(8,128)(2,1)S(1)}, bf16[256,1024]{1,0:T(8,128)(2,1)S(1)}, u32[]{:S(2)}, u32[]{:S(2)}) collective-permute-start(bf16[256,1024]{1,0:T(8,128)(2,1)S(1)} %get-tuple-element.71), channel_id=1, source_target_pairs={{0,8},{8,0},{16,24},{24,16},{1,9},{9,1},{17,25},{25,17},{2,10},{10... | collective-permute-start | bytes 1572872 | tf_op jit(solution)/shard_map/ppermute | solution.py:613
  58.7 13.9 %copy-start.2 = (f32[2048]{0:T(1024)S(1)}, f32[2048]{0:T(1024)}, u32[]{:S(2)}) copy-start(f32[2048]{0:T(1024)} %param.17) | copy-start | bytes 24580
  61.9 5.5 %collective-permute-start.18 = (f32[1,1536]{1,0:T(1,128)S(1)}, f32[1,1536]{1,0:T(1,128)S(1)}, u32[]{:S(2)}, u32[]{:S(2)}) collective-permute-start(f32[1,1536]{1,0:T(1,128)S(1)} %get-tuple-element.74), channel_id=1, source_target_pairs={{0,6},{1,7},{2,4},{3,5},{4,2},{5,3},{6,0},{7,1},{8,14},{9,15},{10,... | collective-permute-start | bytes 18440 | tf_op jit(solution)/shard_map/ppermute | solution.py:598
  64.4 4.5 %collective-permute-start.17 = (f32[1,1536]{1,0:T(1,128)S(1)}, f32[1,1536]{1,0:T(1,128)S(1)}, u32[]{:S(2)}, u32[]{:S(2)}) collective-permute-start(f32[1,1536]{1,0:T(1,128)S(1)} %get-tuple-element.74), channel_id=1, source_target_pairs={{0,4},{1,5},{2,6},{3,7},{4,0},{5,1},{6,2},{7,3},{8,12},{9,13},{10,... | collective-permute-start | bytes 18440 | tf_op jit(solution)/shard_map/ppermute | solution.py:598
  64.4 4.5 %collective-permute-start.16 = (f32[1,1536]{1,0:T(1,128)S(1)}, f32[1,1536]{1,0:T(1,128)S(1)}, u32[]{:S(2)}, u32[]{:S(2)}) collective-permute-start(f32[1,1536]{1,0:T(1,128)S(1)} %get-tuple-element.74), channel_id=1, source_target_pairs={{0,2},{1,3},{2,0},{3,1},{4,6},{5,7},{6,4},{7,5},{8,10},{9,11},{10,... | collective-permute-start | bytes 18440 | tf_op jit(solution)/shard_map/ppermute | solution.py:598
  68.9 3.7 %collective-permute-start.19 = (f32[1,1536]{1,0:T(1,128)S(1)}, f32[1,1536]{1,0:T(1,128)S(1)}, u32[]{:S(2)}, u32[]{:S(2)}) collective-permute-start(f32[1,1536]{1,0:T(1,128)S(1)} %add_add_fusion.one_ref), channel_id=1, source_target_pairs={{0,1},{1,0},{2,3},{3,2},{4,5},{5,4},{6,7},{7,6},{8,9},{9,8},{10,11... | collective-permute-start | bytes 18440 | tf_op jit(solution)/shard_map/ppermute | solution.py:603
  (1 other events, 0.7 us)

commit v6 on v5

--- a/solution.py
+++ b/solution.py
@@ -107,7 +107,8 @@
         cum = jnp.dot(rate * step, upper, precision=HIGHEST, preferred_element_type=F32)
         last = cum[:, BLOCK - 1 : BLOCK]
         scaled = cum * LOG2E
-        b_ref[:, columns] = scaled - jnp.log(step) * LOG2E
+        b_ref[0:SLOT, columns] = scaled
+        b_ref[SLOT : 2 * SLOT, columns] = step
         parts = [scaled]
         parts.extend(split(jnp.exp(last - cum) * step))
         parts.extend(split(jnp.exp(cum)))
@@ -151,7 +152,7 @@
         rates_kernel,
         out_shape=[
             kept_in_vmem((length, 128), F32),
-            kept_in_vmem((SLOT, length), F32),
+            kept_in_vmem((2 * SLOT, length), F32),
             kept_in_vmem((SLOT, width), F32),
             kept_in_vmem((1, width), F32),
             kept_in_vmem((BLOCK, width), BF16),
@@ -475,9 +476,13 @@
             columns = slice(h * HEAD_DIM, (h + 1) * HEAD_DIM)
             rise = jnp.broadcast_to(q_block[:, h : h + 1], (BLOCK, half))
             fall = brow_ref[h : h + 1, rows]
+            step = brow_ref[SLOT + h : SLOT + h + 1, rows]
             w_00 = gram_00 * jnp.exp2(jnp.minimum(rise[:half] - fall[:, :half], 120.0))
             w_10 = gram_10 * jnp.exp2(rise[half:] - fall[:, :half])
             w_11 = gram_11 * jnp.exp2(jnp.minimum(rise[half:] - fall[:, half:], 120.0))
+            w_00 = w_00 * step[:, :half]
+            w_10 = w_10 * step[:, :half]
+            w_11 = w_11 * step[:, half:]
             x_head = held[c, :, columns]
             top = jnp.dot(w_00.astype(BF16), x_head[:half], preferred_element_type=F32)
             low = jnp.concatenate([w_10.astype(BF16), w_11.astype(BF16)], axis=1)

time: 76 us -> 76.5 us (level)
  no operation moved by 1% of the time
where the time goes in v6:
time: 76.5 us; the launch traced here: 76.3 us
  Pallas kernels  34.6 us (45%)
  starting transfers between devices  25.9 us (34%)
  waiting for transfers between devices  14 us (18%)
  local copies, waits for them, and re-layouts  1.32 us (2%)
    ppermute x9, starting transfers between devices, zone_swap(): return lax.ppermute(a, 'head', [(i, i ^ 2 * k) for i in range(size)])  13.2 us
    pallas_call x1, Pallas kernels, inner(): pl.pallas_call(inner_kernel, out_shape=[kept_in_vmem((length, width), F32...  11.9 us
    pallas_call x2, Pallas kernels, gate(): pl.pallas_call(functools.partial(gate_kernel, len(before) > 0), out_shape...  6.36 us
    ppermute x9, waiting for transfers between devices, zone_swap(): return lax.ppermute(a, 'head', [(i, i ^ 2 * k) for i in range(size)])  6.35 us
    ppermute x4, waiting for transfers between devices, side_swap(): return lax.ppermute(a, 'head', [(i, i ^ 1) for i in range(size)])  6.31 us
    pallas_call x1, Pallas kernels, rates(): pl.pallas_call(rates_kernel, out_shape=[kept_in_vmem((length, 128), F32),...  5.51 us
    ppermute x4, starting transfers between devices, side_swap(): return lax.ppermute(a, 'head', [(i, i ^ 1) for i in range(size)])  4.93 us
    ppermute x1, starting transfers between devices, chained_state(): crossed = lax.ppermute(both, 'seq', [(0, 2), (1, 3)])  3.61 us
  transfers between devices with their start and end apart: 20, of which 7 were waited for; matrix products, arithmetic and copies ran while one was open for 0% of the time, Pallas kernels for 34%

profile of v6, /device:TPU:0, one launch (start us, length us, event | category | flops | bytes accessed | tf_op | source)
XLA Modules:
  0.0 76.3 jit_solution(17739402256516101645)
XLA Ops:
  0.1 1.5 %shard_map.91 = (bf16[208,256]{1,0:T(8,128)(2,1)S(1)}, bf16[192,256]{1,0:T(8,128)(2,1)S(1)}, s32[2]{0:T(128)S(4)}) custom-call(s32[2]{0:T(128)S(1)} %pad_add_fusion.place_ref, bf16[192,512]{1,0:T(8,128)(2,1)} %bc_ref.1), custom_call_target="tpu_custom_call" | custom-call | tf_op jit(solution)/shard_map/pallas_call | solution.py:200
  1.6 3.0 %collective-permute-start.4 = (bf16[208,256]{1,0:T(8,128)(2,1)S(1)}, bf16[208,256]{1,0:T(8,128)(2,1)S(1)}, u32[]{:S(2)}, u32[]{:S(2)}) collective-permute-start(bf16[208,256]{1,0:T(8,128)(2,1)S(1)} %get-tuple-element.41.refs_0_), channel_id=1, source_target_pairs={{0,1},{1,0},{2,3},{3,2},{4,5},{5,4},{6,7},{7,6},{8,9},{9,8},{10,11... | collective-permute-start | bytes 319496 | tf_op jit(solution)/shard_map/ppermute | solution.py:608
  4.7 3.6 %collective-permute-start.2 = (bf16[208,256]{1,0:T(8,128)(2,1)S(1)}, bf16[208,256]{1,0:T(8,128)(2,1)S(1)}, u32[]{:S(2)}, u32[]{:S(2)}) collective-permute-start(bf16[208,256]{1,0:T(8,128)(2,1)S(1)} %get-tuple-element.41.refs_0_), channel_id=1, source_target_pairs={{0,6},{1,7},{2,4},{3,5},{4,2},{5,3},{6,0},{7,1},{8,14},{9,15},{10,... | collective-permute-start | bytes 319496 | tf_op jit(solution)/shard_map/ppermute | solution.py:603
  10.6 5.5 %shard_map.92 = (f32[1536,128]{1,0:T(8,128)S(1)}, f32[32,1536]{1,0:T(8,128)S(1)}, f32[16,2048]{1,0:T(8,128)S(1)}, f32[1,2048]{1,0:T(1,128)S(1)}, bf16[256,2048]{...) custom-call(f32[16,1536]{1,0:T(8,128)} %bitcast.13, f32[1,16]{1,0:T(1,128)S(1)} %bitcast.11, f32[1,16]{1,0:T(1,128)S(1)} %bitcast.12, ...), custom_call_target="tpu_custom_call" | custom-call | tf_op jit(solution)/shard_map/pallas_call | solution.py:151
  17.0 1.1 %collective-permute-start.8 = (bf16[624,256]{1,0:T(8,128)(2,1)S(1)}, bf16[624,256]{1,0:T(8,128)(2,1)S(1)}, u32[]{:S(2)}, u32[]{:S(2)}) collective-permute-start(bf16[624,256]{1,0:T(8,128)(2,1)S(1)} %get-tuple-element.45), channel_id=1, source_target_pairs={{0,1},{1,0},{2,3},{3,2},{4,5},{5,4},{6,7},{7,6},{8,9},{9,8},{10,11... | collective-permute-start | bytes 958472 | tf_op jit(solution)/shard_map/ppermute | solution.py:608
  18.1 3.6 %collective-permute-start.7 = (bf16[384,256]{1,0:T(8,128)(2,1)S(1)}, bf16[384,256]{1,0:T(8,128)(2,1)S(1)}, u32[]{:S(2)}, u32[]{:S(2)}) collective-permute-start(bf16[384,256]{1,0:T(8,128)(2,1)S(1)} %get-tuple-element.44.refs_0_), channel_id=1, source_target_pairs={{0,6},{1,7},{2,4},{3,5},{4,2},{5,3},{6,0},{7,1},{8,14},{9,15},{10,... | collective-permute-start | bytes 589832 | tf_op jit(solution)/shard_map/ppermute | solution.py:603
  22.5 3.2 %collective-permute-done.8.refs_5_ = bf16[624,256]{1,0:T(8,128)(2,1)S(1)} collective-permute-done((bf16[624,256]{1,0:T(8,128)(2,1)S(1)}, bf16[624,256]{1,0:T(8,128)(2,1)S(1)}, u32[]{:S(2)}, u32[]{:S(2)}) %collective-permute-start.8) | collective-permute-done | bytes 319520 | tf_op jit(solution)/shard_map/ppermute | solution.py:608
  25.6 1.0 %shard_map.94 = (bf16[1536,256]{1,0:T(8,128)(2,1)S(1)}, bf16[16,256]{1,0:T(8,128)(2,1)S(1)}, bf16[32,256]{1,0:T(8,128)(2,1)S(1)}) custom-call(s32[2]{0:T(128)S(4)} %get-tuple-element.40.me_ref.at_ref, f32[4,512]{1,0:T(4,128)S(1)} %copy-done, f32[1,512]{1,0:T(1,128)S(1)} %bitcast.7, bf16[208,256]{1,0:T(8,128)(2,1)S(1)} %get-tuple-element.41.refs_0_, ...), custom_call_target="tpu_custom_call" | custom-call | tf_op jit(solution)/shard_map/pallas_call | solution.py:275
  26.6 1.3 %collective-permute-start.9 = (bf16[32,256]{1,0:T(8,128)(2,1)S(1)}, bf16[32,256]{1,0:T(8,128)(2,1)S(1)}, u32[]{:S(2)}, u32[]{:S(2)}) collective-permute-start(bf16[32,256]{1,0:T(8,128)(2,1)S(1)} %get-tuple-element.46), channel_id=1, source_target_pairs={{0,8},{8,16},{16,24},{1,9},{9,17},{17,25},{2,10},{10,18},{18,26},{... | collective-permute-start | bytes 49160 | tf_op jit(solution)/shard_map/ppermute | solution.py:669
  27.9 2.2 %shard_map.96 = (bf16[5,256,2048]{2,1,0:T(8,128)(2,1)S(1)}, f32[256,2048]{1,0:T(8,128)S(1)}) custom-call(bf16[1536,256]{1,0:T(8,128)(2,1)S(1)} %get-tuple-element.48.b_ref, bf16[1280,2048]{1,0:T(8,128)(2,1)S(1)} %get-tuple-element.51.xs_ref, f32[16,2048]{1,0:T(8,128)S(1)} %get-tuple-element.50.dec_ref), custom_call_target="tpu_custom_call" | custom-call | tf_op jit(solution)/shard_map/pallas_call | solution.py:321
  30.8 2.3 %collective-permute-start.10 = (bf16[272,256]{1,0:T(8,128)(2,1)S(1)}, bf16[272,256]{1,0:T(8,128)(2,1)S(1)}, u32[]{:S(2)}, u32[]{:S(2)}) collective-permute-start(bf16[272,256]{1,0:T(8,128)(2,1)S(1)} %get-tuple-element.62), channel_id=1, source_target_pairs={{0,8},{8,0},{16,24},{24,16},{1,9},{9,1},{17,25},{25,17},{2,10},{10... | collective-permute-start | bytes 417800 | tf_op jit(solution)/shard_map/ppermute | solution.py:614
  33.6 3.0 %collective-permute-done.6.refs_2_.refs_5_ = bf16[384,256]{1,0:T(8,128)(2,1)S(1)} collective-permute-done((bf16[384,256]{1,0:T(8,128)(2,1)S(1)}, bf16[384,256]{1,0:T(8,128)(2,1)S(1)}, u32[]{:S(2)}, u32[]{:S(2)}) %collective-permute-start.6) | collective-permute-done | bytes 196640 | tf_op jit(solution)/shard_map/ppermute | solution.py:603
  36.7 1.3 %collective-permute-done.13.refs_3_ = bf16[272,256]{1,0:T(8,128)(2,1)S(1)} collective-permute-done((bf16[272,256]{1,0:T(8,128)(2,1)S(1)}, bf16[272,256]{1,0:T(8,128)(2,1)S(1)}, u32[]{:S(2)}, u32[]{:S(2)}) %collective-permute-start.13) | collective-permute-done | bytes 139296 | tf_op jit(solution)/shard_map/ppermute | solution.py:614
  38.4 3.6 %collective-permute-start.14 = (bf16[256,1024]{1,0:T(8,128)(2,1)S(1)}, bf16[256,1024]{1,0:T(8,128)(2,1)S(1)}, u32[]{:S(2)}, u32[]{:S(2)}) collective-permute-start(bf16[256,1024]{1,0:T(8,128)(2,1)S(1)} %get-tuple-element.66), channel_id=1, source_target_pairs={{0,16},{8,24},{1,17},{9,25},{2,18},{10,26},{3,19},{11,27},{4,20},{... | collective-permute-start | bytes 1572872 | tf_op jit(solution)/shard_map/ppermute | solution.py:616
  42.0 1.4 %shard_map.95 = (bf16[1536,256]{1,0:T(8,128)(2,1)S(1)}, bf16[16,256]{1,0:T(8,128)(2,1)}, bf16[32,256]{1,0:T(8,128)(2,1)}) custom-call(s32[2]{0:T(128)S(4)} %get-tuple-element.40.me_ref.at_ref, f32[4,512]{1,0:T(4,128)S(1)} %copy-done, f32[1,512]{1,0:T(1,128)S(1)} %bitcast.9, bf16[384,256]{1,0:T(8,128)(2,1)S(1)} %get-tuple-element.44.refs_0_, ...), custom_call_target="tpu_custom_call" | custom-call | tf_op jit(solution)/shard_map/pallas_call | solution.py:275
  43.5 11.9 %shard_map.98 = (f32[1536,2048]{1,0:T(8,128)S(1)}, bf16[1536,2048]{1,0:T(8,128)(2,1)S(1)}) custom-call(bf16[1536,256]{1,0:T(8,128)(2,1)S(1)} %get-tuple-element.47.c_ref, bf16[1536,256]{1,0:T(8,128)(2,1)S(1)} %get-tuple-element.54.b_ref, bf16[1536,2048]{1,0:T(8,128)(2,1)} %x_ref.3, bf16[1536,2048]{1,0:T(8,128)(2,1)} %z_ref.1, ...), custom_call_target="tpu_custom_call" | custom-call | bytes 251658240 | tf_op jit(solution)/shard_map/pallas_call | solution.py:501
  56.0 3.2 %shard_map.101 = (f32[1536,2048]{1,0:T(8,128)S(1)}, f32[1,1536]{1,0:T(1,128)S(1)}) custom-call(s32[2]{0:T(128)S(4)} %get-tuple-element.40.me_ref.at_ref, bf16[1536,256]{1,0:T(8,128)(2,1)S(1)} %get-tuple-element.47.c_ref, f32[1536,2048]{1,0:T(8,128)S(1)} %get-tuple-element.59.refs_0_.y_ref, ...), custom_call_target="tpu_custom_call", output_to_operand_aliasing={{0}: (2, {})} | custom-call | bytes 25165824 | tf_op jit(solution)/shard_map/pallas_call | solution.py:546
  59.2 3.2 %shard_map.102 = (f32[1536,2048]{1,0:T(8,128)S(1)}, f32[1,1536]{1,0:T(1,128)S(1)}) custom-call(s32[2]{0:T(128)S(4)} %get-tuple-element.40.me_ref.at_ref, bf16[1536,256]{1,0:T(8,128)(2,1)S(1)} %get-tuple-element.47.c_ref, f32[1536,2048]{1,0:T(8,128)S(1)} %get-tuple-element.70.y_ref, ...), custom_call_target="tpu_custom_call", output_to_operand_aliasing={{0}: (2, {})} | custom-call | bytes 25165824 | tf_op jit(solution)/shard_map/pallas_call | solution.py:546
  62.4 2.5 %collective-permute-start.18 = (f32[1,1536]{1,0:T(1,128)S(1)}, f32[1,1536]{1,0:T(1,128)S(1)}, u32[]{:S(2)}, u32[]{:S(2)}) collective-permute-start(f32[1,1536]{1,0:T(1,128)S(1)} %get-tuple-element.74), channel_id=1, source_target_pairs={{0,6},{1,7},{2,4},{3,5},{4,2},{5,3},{6,0},{7,1},{8,14},{9,15},{10,... | collective-permute-start | bytes 18440 | tf_op jit(solution)/shard_map/ppermute | solution.py:603
  64.9 2.0 %collective-permute-start.16 = (f32[1,1536]{1,0:T(1,128)S(1)}, f32[1,1536]{1,0:T(1,128)S(1)}, u32[]{:S(2)}, u32[]{:S(2)}) collective-permute-start(f32[1,1536]{1,0:T(1,128)S(1)} %get-tuple-element.74), channel_id=1, source_target_pairs={{0,2},{1,3},{2,0},{3,1},{4,6},{5,7},{6,4},{7,5},{8,10},{9,11},{10,... | collective-permute-start | bytes 18440 | tf_op jit(solution)/shard_map/ppermute | solution.py:603
  66.8 1.0 %collective-permute-done.18 = f32[1,1536]{1,0:T(1,128)S(1)} collective-permute-done((f32[1,1536]{1,0:T(1,128)S(1)}, f32[1,1536]{1,0:T(1,128)S(1)}, u32[]{:S(2)}, u32[]{:S(2)}) %collective-permute-start.18) | collective-permute-done | bytes 6176 | tf_op jit(solution)/shard_map/ppermute | solution.py:603
  67.9 1.5 %collective-permute-done.17 = f32[1,1536]{1,0:T(1,128)S(1)} collective-permute-done((f32[1,1536]{1,0:T(1,128)S(1)}, f32[1,1536]{1,0:T(1,128)S(1)}, u32[]{:S(2)}, u32[]{:S(2)}) %collective-permute-start.17) | collective-permute-done | bytes 6176 | tf_op jit(solution)/shard_map/ppermute | solution.py:603
  69.9 3.2 %collective-permute-done.19.two_ref = f32[1,1536]{1,0:T(1,128)S(1)} collective-permute-done((f32[1,1536]{1,0:T(1,128)S(1)}, f32[1,1536]{1,0:T(1,128)S(1)}, u32[]{:S(2)}, u32[]{:S(2)}) %collective-permute-start.19) | collective-permute-done | bytes 6176 | tf_op jit(solution)/shard_map/ppermute | solution.py:608
  73.1 3.0 %shard_map.103 = bf16[1536,2048]{1,0:T(8,128)(2,1)} custom-call(f32[1536,2048]{1,0:T(8,128)S(1)} %get-tuple-element.73.g_ref, f32[1,1536]{1,0:T(1,128)S(1)} %add_add_fusion.one_ref, f32[1,1536]{1,0:T(1,128)S(1)} %collective-permute-done.19.two_ref, f32[1,2048]{1,0:T(1,128)S(1)} %bitcast.10), custom_call_target="tpu_custom_call" | custom-call | tf_op jit(solution)/shard_map/pallas_call | solution.py:584
  (41 shorter events, 6.8 us)
Async XLA Ops:
  0.0 25.6 %copy-start = (f32[4,512]{1,0:T(4,128)S(1)}, f32[4,512]{1,0:T(4,128)}, u32[]{:S(2)}) copy-start(f32[4,512]{1,0:T(4,128)} %weight_ref.5) | copy-start | bytes 24580
  0.0 25.6 %copy-start.1 = (f32[512]{0:T(512)S(1)}, f32[512]{0:T(512)}, u32[]{:S(2)}) copy-start(f32[512]{0:T(512)} %param.13) | copy-start | bytes 6148
  1.6 14.6 %collective-permute-start.4 = (bf16[208,256]{1,0:T(8,128)(2,1)S(1)}, bf16[208,256]{1,0:T(8,128)(2,1)S(1)}, u32[]{:S(2)}, u32[]{:S(2)}) collective-permute-start(bf16[208,256]{1,0:T(8,128)(2,1)S(1)} %get-tuple-element.41.refs_0_), channel_id=1, source_target_pairs={{0,1},{1,0},{2,3},{3,2},{4,5},{5,4},{6,7},{7,6},{8,9},{9,8},{10,11... | collective-permute-start | bytes 319496 | tf_op jit(solution)/shard_map/ppermute | solution.py:608
  4.7 11.5 %collective-permute-start.2 = (bf16[208,256]{1,0:T(8,128)(2,1)S(1)}, bf16[208,256]{1,0:T(8,128)(2,1)S(1)}, u32[]{:S(2)}, u32[]{:S(2)}) collective-permute-start(bf16[208,256]{1,0:T(8,128)(2,1)S(1)} %get-tuple-element.41.refs_0_), channel_id=1, source_target_pairs={{0,6},{1,7},{2,4},{3,5},{4,2},{5,3},{6,0},{7,1},{8,14},{9,15},{10,... | collective-permute-start | bytes 319496 | tf_op jit(solution)/shard_map/ppermute | solution.py:603
  8.3 8.7 %collective-permute-start.1 = (bf16[208,256]{1,0:T(8,128)(2,1)S(1)}, bf16[208,256]{1,0:T(8,128)(2,1)S(1)}, u32[]{:S(2)}, u32[]{:S(2)}) collective-permute-start(bf16[208,256]{1,0:T(8,128)(2,1)S(1)} %get-tuple-element.41.refs_0_), channel_id=1, source_target_pairs={{0,4},{1,5},{2,6},{3,7},{4,0},{5,1},{6,2},{7,3},{8,12},{9,13},{10,... | collective-permute-start | bytes 319496 | tf_op jit(solution)/shard_map/ppermute | solution.py:603
  8.3 8.7 %collective-permute-start = (bf16[208,256]{1,0:T(8,128)(2,1)S(1)}, bf16[208,256]{1,0:T(8,128)(2,1)S(1)}, u32[]{:S(2)}, u32[]{:S(2)}) collective-permute-start(bf16[208,256]{1,0:T(8,128)(2,1)S(1)} %get-tuple-element.41.refs_0_), channel_id=1, source_target_pairs={{0,2},{1,3},{2,0},{3,1},{4,6},{5,7},{6,4},{7,5},{8,10},{9,11},{10,... | collective-permute-start | bytes 319496 | tf_op jit(solution)/shard_map/ppermute | solution.py:603
  9.0 7.1 %collective-permute-start.3 = (bf16[192,256]{1,0:T(8,128)(2,1)S(1)}, bf16[192,256]{1,0:T(8,128)(2,1)S(1)}, u32[]{:S(2)}, u32[]{:S(2)}) collective-permute-start(bf16[192,256]{1,0:T(8,128)(2,1)S(1)} %get-tuple-element.42.refs_3_), channel_id=1, source_target_pairs={{0,1},{1,0},{2,3},{3,2},{4,5},{5,4},{6,7},{7,6},{8,9},{9,8},{10,11... | collective-permute-start | bytes 294920 | tf_op jit(solution)/shard_map/ppermute | solution.py:608
  9.3 0.7 copy-start.3
  17.0 8.6 %collective-permute-start.8 = (bf16[624,256]{1,0:T(8,128)(2,1)S(1)}, bf16[624,256]{1,0:T(8,128)(2,1)S(1)}, u32[]{:S(2)}, u32[]{:S(2)}) collective-permute-start(bf16[624,256]{1,0:T(8,128)(2,1)S(1)} %get-tuple-element.45), channel_id=1, source_target_pairs={{0,1},{1,0},{2,3},{3,2},{4,5},{5,4},{6,7},{7,6},{8,9},{9,8},{10,11... | collective-permute-start | bytes 958472 | tf_op jit(solution)/shard_map/ppermute | solution.py:608
  18.1 15.1 %collective-permute-start.7 = (bf16[384,256]{1,0:T(8,128)(2,1)S(1)}, bf16[384,256]{1,0:T(8,128)(2,1)S(1)}, u32[]{:S(2)}, u32[]{:S(2)}) collective-permute-start(bf16[384,256]{1,0:T(8,128)(2,1)S(1)} %get-tuple-element.44.refs_0_), channel_id=1, source_target_pairs={{0,6},{1,7},{2,4},{3,5},{4,2},{5,3},{6,0},{7,1},{8,14},{9,15},{10,... | collective-permute-start | bytes 589832 | tf_op jit(solution)/shard_map/ppermute | solution.py:603
  21.7 15.0 %collective-permute-start.6 = (bf16[384,256]{1,0:T(8,128)(2,1)S(1)}, bf16[384,256]{1,0:T(8,128)(2,1)S(1)}, u32[]{:S(2)}, u32[]{:S(2)}) collective-permute-start(bf16[384,256]{1,0:T(8,128)(2,1)S(1)} %get-tuple-element.44.refs_0_), channel_id=1, source_target_pairs={{0,4},{1,5},{2,6},{3,7},{4,0},{5,1},{6,2},{7,3},{8,12},{9,13},{10,... | collective-permute-start | bytes 589832 | tf_op jit(solution)/shard_map/ppermute | solution.py:603
  21.7 15.0 %collective-permute-start.5 = (bf16[384,256]{1,0:T(8,128)(2,1)S(1)}, bf16[384,256]{1,0:T(8,128)(2,1)S(1)}, u32[]{:S(2)}, u32[]{:S(2)}) collective-permute-start(bf16[384,256]{1,0:T(8,128)(2,1)S(1)} %get-tuple-element.44.refs_0_), channel_id=1, source_target_pairs={{0,2},{1,3},{2,0},{3,1},{4,6},{5,7},{6,4},{7,5},{8,10},{9,11},{10,... | collective-permute-start | bytes 589832 | tf_op jit(solution)/shard_map/ppermute | solution.py:603
  26.6 3.5 %collective-permute-start.9 = (bf16[32,256]{1,0:T(8,128)(2,1)S(1)}, bf16[32,256]{1,0:T(8,128)(2,1)S(1)}, u32[]{:S(2)}, u32[]{:S(2)}) collective-permute-start(bf16[32,256]{1,0:T(8,128)(2,1)S(1)} %get-tuple-element.46), channel_id=1, source_target_pairs={{0,8},{8,16},{16,24},{1,9},{9,17},{17,25},{2,10},{10,18},{18,26},{... | collective-permute-start | bytes 49160 | tf_op jit(solution)/shard_map/ppermute | solution.py:669
  30.8 5.9 %collective-permute-start.10 = (bf16[272,256]{1,0:T(8,128)(2,1)S(1)}, bf16[272,256]{1,0:T(8,128)(2,1)S(1)}, u32[]{:S(2)}, u32[]{:S(2)}) collective-permute-start(bf16[272,256]{1,0:T(8,128)(2,1)S(1)} %get-tuple-element.62), channel_id=1, source_target_pairs={{0,8},{8,0},{16,24},{24,16},{1,9},{9,1},{17,25},{25,17},{2,10},{10... | collective-permute-start | bytes 417800 | tf_op jit(solution)/shard_map/ppermute | solution.py:614
  33.1 3.6 %collective-permute-start.11 = (bf16[272,256]{1,0:T(8,128)(2,1)S(1)}, bf16[272,256]{1,0:T(8,128)(2,1)S(1)}, u32[]{:S(2)}, u32[]{:S(2)}) collective-permute-start(bf16[272,256]{1,0:T(8,128)(2,1)S(1)} %get-tuple-element.63), channel_id=1, source_target_pairs={{0,8},{8,0},{16,24},{24,16},{1,9},{9,1},{17,25},{25,17},{2,10},{10... | collective-permute-start | bytes 417800 | tf_op jit(solution)/shard_map/ppermute | solution.py:614
  33.1 3.5 %collective-permute-start.12 = (bf16[272,256]{1,0:T(8,128)(2,1)S(1)}, bf16[272,256]{1,0:T(8,128)(2,1)S(1)}, u32[]{:S(2)}, u32[]{:S(2)}) collective-permute-start(bf16[272,256]{1,0:T(8,128)(2,1)S(1)} %get-tuple-element.64), channel_id=1, source_target_pairs={{0,8},{8,0},{16,24},{24,16},{1,9},{9,1},{17,25},{25,17},{2,10},{10... | collective-permute-start | bytes 417800 | tf_op jit(solution)/shard_map/ppermute | solution.py:614
  36.6 1.4 %collective-permute-start.13 = (bf16[272,256]{1,0:T(8,128)(2,1)S(1)}, bf16[272,256]{1,0:T(8,128)(2,1)S(1)}, u32[]{:S(2)}, u32[]{:S(2)}) collective-permute-start(bf16[272,256]{1,0:T(8,128)(2,1)S(1)} %get-tuple-element.65), channel_id=1, source_target_pairs={{0,8},{8,0},{16,24},{24,16},{1,9},{9,1},{17,25},{25,17},{2,10},{10... | collective-permute-start | bytes 417800 | tf_op jit(solution)/shard_map/ppermute | solution.py:614
  38.4 16.9 %collective-permute-start.14 = (bf16[256,1024]{1,0:T(8,128)(2,1)S(1)}, bf16[256,1024]{1,0:T(8,128)(2,1)S(1)}, u32[]{:S(2)}, u32[]{:S(2)}) collective-permute-start(bf16[256,1024]{1,0:T(8,128)(2,1)S(1)} %get-tuple-element.66), channel_id=1, source_target_pairs={{0,16},{8,24},{1,17},{9,25},{2,18},{10,26},{3,19},{11,27},{4,20},{... | collective-permute-start | bytes 1572872 | tf_op jit(solution)/shard_map/ppermute | solution.py:616
  55.9 3.3 %collective-permute-start.15 = (bf16[256,1024]{1,0:T(8,128)(2,1)S(1)}, bf16[256,1024]{1,0:T(8,128)(2,1)S(1)}, u32[]{:S(2)}, u32[]{:S(2)}) collective-permute-start(bf16[256,1024]{1,0:T(8,128)(2,1)S(1)} %get-tuple-element.71), channel_id=1, source_target_pairs={{0,8},{8,0},{16,24},{24,16},{1,9},{9,1},{17,25},{25,17},{2,10},{10... | collective-permute-start | bytes 1572872 | tf_op jit(solution)/shard_map/ppermute | solution.py:618
  59.2 13.9 %copy-start.2 = (f32[2048]{0:T(1024)S(1)}, f32[2048]{0:T(1024)}, u32[]{:S(2)}) copy-start(f32[2048]{0:T(1024)} %param.17) | copy-start | bytes 24580
  62.4 5.5 %collective-permute-start.18 = (f32[1,1536]{1,0:T(1,128)S(1)}, f32[1,1536]{1,0:T(1,128)S(1)}, u32[]{:S(2)}, u32[]{:S(2)}) collective-permute-start(f32[1,1536]{1,0:T(1,128)S(1)} %get-tuple-element.74), channel_id=1, source_target_pairs={{0,6},{1,7},{2,4},{3,5},{4,2},{5,3},{6,0},{7,1},{8,14},{9,15},{10,... | collective-permute-start | bytes 18440 | tf_op jit(solution)/shard_map/ppermute | solution.py:603
  64.8 4.5 %collective-permute-start.17 = (f32[1,1536]{1,0:T(1,128)S(1)}, f32[1,1536]{1,0:T(1,128)S(1)}, u32[]{:S(2)}, u32[]{:S(2)}) collective-permute-start(f32[1,1536]{1,0:T(1,128)S(1)} %get-tuple-element.74), channel_id=1, source_target_pairs={{0,4},{1,5},{2,6},{3,7},{4,0},{5,1},{6,2},{7,3},{8,12},{9,13},{10,... | collective-permute-start | bytes 18440 | tf_op jit(solution)/shard_map/ppermute | solution.py:603
  64.9 4.5 %collective-permute-start.16 = (f32[1,1536]{1,0:T(1,128)S(1)}, f32[1,1536]{1,0:T(1,128)S(1)}, u32[]{:S(2)}, u32[]{:S(2)}) collective-permute-start(f32[1,1536]{1,0:T(1,128)S(1)} %get-tuple-element.74), channel_id=1, source_target_pairs={{0,2},{1,3},{2,0},{3,1},{4,6},{5,7},{6,4},{7,5},{8,10},{9,11},{10,... | collective-permute-start | bytes 18440 | tf_op jit(solution)/shard_map/ppermute | solution.py:603
  69.4 3.7 %collective-permute-start.19 = (f32[1,1536]{1,0:T(1,128)S(1)}, f32[1,1536]{1,0:T(1,128)S(1)}, u32[]{:S(2)}, u32[]{:S(2)}) collective-permute-start(f32[1,1536]{1,0:T(1,128)S(1)} %add_add_fusion.one_ref), channel_id=1, source_target_pairs={{0,1},{1,0},{2,3},{3,2},{4,5},{5,4},{6,7},{7,6},{8,9},{9,8},{10,11... | collective-permute-start | bytes 18440 | tf_op jit(solution)/shard_map/ppermute | solution.py:608
  (1 other events, 0.7 us)
